TPU v7x, 32 devices: a whole 2x2x4 slice. The times are simulated.
32 devices in a mesh: groups: 2 (over x), expert: 16 (over z, y, core).
Axes of the slice: x: 2, y: 2, z: 4, core: 2. Of those that a mesh axis runs over, the one named last changes fastest.
Arguments:
- token_codes: bfloat16 [2048, 1024], P(('groups', 'expert')), parts along dimension 0, may hold values from -6 to 6
- route_devices: int32 [2048, 8], P(('groups', 'expert')), parts along dimension 0, may hold values from 0 to 15, all different within a row; in each aligned block of 64 rows (0 to 63, 64 to 127, ...) at most 64 rows name the same one
- route_members: int32 [2048, 8], P(('groups', 'expert')), parts along dimension 0, may hold values from 0 to 1
- gate_scores: bfloat16 [2048, 8], P(('groups', 'expert')), parts along dimension 0, may hold values from 0.049804688 to 1
- gate_core: bfloat16 [32, 1024, 1024], P('expert'), may hold values from -0.1875 to 0.1875
- up_core: bfloat16 [32, 1024, 1024], P('expert'), may hold values from -0.1875 to 0.1875
- down_core: bfloat16 [32, 1024, 512], P('expert'), may hold values from -0.1875 to 0.1875
Outputs:
- mixed_codes: bfloat16 [2048, 512], P(('groups', 'expert')), parts along dimension 0
There are 2 independent parts, one for each index of `groups`. A program takes and returns all parts, laid end to end along the dimension named above; an argument that names none is the same for every part. Nothing has to cross between parts.
Inputs may be any that keep to these rules, and one draw needn't show every extreme that they name: `route_devices`: each row names 8 different devices. Within the rows of one device (aligned blocks of 64 rows) no device is named by more than 64 rows, and in every draw some device is named by exactly 64 rows of some device.
All inputs are finite; a program needn't handle non-finite values.
Results may differ from a plain program's by a relative error of at most 0.0058.
Values may be sent and summed in bfloat16 or wider, within the bound.
No kernel may reach another device: no remote copies, remote signals or barrier semaphores. Data moves between devices by JAX's collectives and lax.ppermute only.
A program may use at most 64 MiB of HBM per device.

v0:
```python
import jax
import jax.numpy as jnp
from jax import lax
from jax.sharding import PartitionSpec as P


def apply_experts(arrived, gate_core, up_core, down_core):
    gate_value = jnp.einsum(
        "secr,erh->sech", arrived, gate_core, preferred_element_type=jnp.float32
    )
    up_value = jnp.einsum("secr,erh->sech", arrived, up_core, preferred_element_type=jnp.float32)
    hidden = (jax.nn.silu(gate_value) * up_value).astype(jnp.bfloat16)
    return jnp.einsum(
        "sech,ehd->secd", hidden, down_core, preferred_element_type=jnp.float32
    ).astype(jnp.bfloat16)


def slot_positions(local_ids, group_count, capacity):
    flat_ids = local_ids.reshape(-1)
    onehot = (flat_ids[:, None] == jnp.arange(group_count, dtype=jnp.int32)[None, :]).astype(
        jnp.int32
    )
    earlier = jnp.cumsum(onehot, axis=0) - onehot
    return flat_ids * capacity + jnp.sum(earlier * onehot, axis=1)


def route_weights(scores_in):
    scores = scores_in.astype(jnp.float32)
    return 2.5 * scores / jnp.sum(scores, axis=1, keepdims=True)


def local(token_codes, route_devices, route_members, gate_scores, gate_core, up_core, down_core):
    tok_rows, rank_in = token_codes.shape
    routes = route_devices.shape[1]
    local_experts = gate_core.shape[0]
    rank_out = down_core.shape[2]
    axis_size = lax.axis_size("expert")
    capacity = 2 * tok_rows * routes // axis_size
    repeated = jnp.repeat(token_codes, routes, axis=0)
    weights = route_weights(gate_scores).reshape(-1)
    position = slot_positions(route_devices, axis_size, capacity)
    outgoing = jnp.zeros((axis_size * capacity, rank_in), jnp.bfloat16).at[position].set(repeated)
    outgoing = outgoing.reshape(axis_size, capacity, rank_in)
    member_tags = (
        jnp.full((axis_size * capacity,), local_experts, jnp.int32)
        .at[position]
        .set(route_members.reshape(-1))
    )
    member_tags = member_tags.reshape(axis_size, capacity)
    arrived_codes = lax.all_to_all(outgoing, "expert", split_axis=0, concat_axis=0, tiled=True)
    arrived_tags = lax.all_to_all(member_tags, "expert", split_axis=0, concat_axis=0, tiled=True)
    sources, columns = arrived_tags.shape
    room = sources * columns
    place = slot_positions(arrived_tags, local_experts, room)
    grouped = (
        jnp.zeros((local_experts * room, rank_in), jnp.bfloat16)
        .at[place]
        .set(arrived_codes.reshape(room, rank_in), mode="drop")
    )
    result = apply_experts(
        grouped.reshape(1, local_experts, room, rank_in), gate_core, up_core, down_core
    )
    result = result.reshape(local_experts * room, rank_out)
    picked = result[jnp.minimum(place, local_experts * room - 1)].reshape(
        sources, columns, rank_out
    )
    returned = lax.all_to_all(picked, "expert", split_axis=0, concat_axis=0, tiled=True)
    per_route = returned.reshape(axis_size * capacity, rank_out)[position].astype(jnp.float32)
    mixed_codes = (weights[:, None] * per_route).reshape(tok_rows, routes, rank_out).sum(axis=1)
    return mixed_codes.astype(jnp.bfloat16)


def solution(mesh):
    in_specs = (
        P(("groups", "expert"), None),
        P(("groups", "expert"), None),
        P(("groups", "expert"), None),
        P(("groups", "expert"), None),
        P("expert", None, None),
        P("expert", None, None),
        P("expert", None, None),
    )
    out_specs = P(("groups", "expert"), None)
    return jax.shard_map(local, mesh=mesh, in_specs=in_specs, out_specs=out_specs, check_vma=False)
```

profile of v0, /device:TPU:0, one launch (start us, length us, event | category | flops | bytes accessed | tf_op | source)
XLA Modules:
  0.0 143.7 jit_solution(14258190698762059741)
XLA Ops:
  0.0 0.9 copy.17
  1.1 0.7 broadcast_multiply_fusion
  1.8 1.1 reduce-window.14
  3.0 0.2 slice_reduce_fusion
  3.4 0.8 copy.20
  4.4 2.4 %scatter_custom_fusion = s32[1024]{0:T(1024)S(1)} fusion(s32[512]{0:T(512)S(1)} %bitcast.116, s32[512]{0:T(512)S(1)} %reshape.197, s32[]{:T(128)} %constant.13.clone.1), kind=kCustom, calls=%fused_computation.51 | custom fusion | bytes 4100 | tf_op jit(solution)/shard_map/scatter | solution.py:47
  6.8 0.7 all_to_all.12
  7.5 7.4 %all-to-all-start = ((s32[16,1,64]{2,1,0:T(1,128)}), s32[16,1,64]{2,1,0:T(1,128)S(1)}, u32[]{:S(2)}, u32[]{:S(2)}) async-start(s32[16,1,64]{2,1,0:T(1,128)} %all_to_all.12), calls=%async_computation | async-start | bytes 16384 | tf_op jit(solution)/shard_map/all_to_all | solution.py:51
  14.9 4.4 %scatter_custom_fusion.1 = bf16[1024,1024]{1,0:T(8,128)(2,1)} fusion(s32[512]{0:T(512)S(1)} %bitcast.117, bf16[]{:T(256)} %constant.12.clone.1, bf16[64,1024]{1,0:T(8,128)(2,1)} %param.7), kind=kCustom, calls=%fused_computation.20 | custom fusion | bytes 2228226 | tf_op jit(solution)/shard_map/scatter | solution.py:42
  19.3 1.9 %all-to-all-done = s32[16,1,64]{2,1,0:T(1,128)S(1)} async-done(((s32[16,1,64]{2,1,0:T(1,128)}), s32[16,1,64]{2,1,0:T(1,128)S(1)}, u32[]{:S(2)}, u32[]{:S(2)}) %all-to-all-start) | async-done | bytes 4128 | tf_op jit(solution)/shard_map/all_to_all | solution.py:51
  21.2 4.4 %all-to-all-start.1 = ((bf16[16,64,1024]{2,1,0:T(8,128)(2,1)}), bf16[16,64,1024]{2,1,0:T(8,128)(2,1)}, u32[]{:S(2)}, u32[]{:S(2)}) async-start(bf16[16,64,1024]{2,1,0:T(8,128)(2,1)} %bitcast.109), calls=%async_computation.1 | async-start | bytes 4194304 | tf_op jit(solution)/shard_map/all_to_all | solution.py:50
  25.7 0.6 reduce-window.16
  26.3 0.2 slice_reduce_fusion.1
  26.7 0.5 broadcast.153
  27.2 0.7 fusion.31
  28.2 38.5 %all-to-all-done.1 = bf16[16,64,1024]{2,1,0:T(8,128)(2,1)} async-done(((bf16[16,64,1024]{2,1,0:T(8,128)(2,1)}), bf16[16,64,1024]{2,1,0:T(8,128)(2,1)}, u32[]{:S(2)}, u32[]{:S(2)}) %all-to-all-start.1) | async-done | bytes 2097184 | tf_op jit(solution)/shard_map/all_to_all | solution.py:50
  66.7 8.6 %scatter_custom_fusion.2 = bf16[2048,1024]{1,0:T(8,128)(2,1)} fusion(s32[1024]{0:T(1024)S(1)} %bitcast.121, bf16[1024,1024]{1,0:T(8,128)(2,1)} %bitcast.8, bf16[]{:T(256)} %constant.12.clone.1), kind=kCustom, calls=%fused_computation.15 | custom fusion | bytes 4194816 | tf_op jit(solution)/shard_map/scatter | solution.py:58
  75.3 11.2 %fusion.32 = f32[2,1024,1024]{2,1,0:T(8,128)} fusion(bf16[2,1024,1024]{2,1,0:T(8,128)(2,1)} %bitcast.111, bf16[2,1024,1024]{2,1,0:T(8,128)(2,1)} %param.11), kind=kOutput, calls=%fused_computation.55 | convolution fusion | flops 4294967296 | bytes 16777216 | tf_op jit(solution)/shard_map/secr,erh->sech/dot_general | solution.py:8
  86.5 11.3 %fusion.11 = bf16[2,1024,512]{2,1,0:T(8,128)(2,1)} fusion(bf16[2,1024,512]{2,1,0:T(8,128)(2,1)S(1)} %copy-done, f32[2,1024,1024]{2,1,0:T(8,128)} %fusion.32, bf16[2,1024,1024]{2,1,0:T(8,128)(2,1)} %bitcast.112, bf16[2,1024,1024]{2,1,0:T(8,128)(2,1)} %param.12), kind=kOutput, calls=%fused_computation.17 | convolution fusion | flops 6456082432 | bytes 20971520 | tf_op jit(solution)/shard_map/sech,ehd->secd/dot_general | solution.py:13
  97.9 7.0 %gather_fusion = bf16[1024,512]{1,0:T(8,128)(2,1)} fusion(bf16[2048,512]{1,0:T(8,128)(2,1)} %bitcast.107, s32[1024]{0:T(1024)S(1)} %broadcast_clamp_fusion), kind=kCustom, calls=%fused_computation | custom fusion | bytes 2101248 | tf_op jit(solution)/shard_map/gather | solution.py:64
  104.8 11.2 %all-to-all-start.2 = ((bf16[16,64,512]{2,1,0:T(8,128)(2,1)}), bf16[16,64,512]{2,1,0:T(8,128)(2,1)S(1)}, u32[]{:S(2)}, u32[]{:S(2)}) async-start(bf16[16,64,512]{2,1,0:T(8,128)(2,1)} %bitcast.110), calls=%async_computation.2 | async-start | bytes 2097152 | tf_op jit(solution)/shard_map/all_to_all | solution.py:67
  116.2 22.8 %all-to-all-done.2 = bf16[16,64,512]{2,1,0:T(8,128)(2,1)S(1)} async-done(((bf16[16,64,512]{2,1,0:T(8,128)(2,1)}), bf16[16,64,512]{2,1,0:T(8,128)(2,1)S(1)}, u32[]{:S(2)}, u32[]{:S(2)}) %all-to-all-start.2) | async-done | bytes 1048608 | tf_op jit(solution)/shard_map/all_to_all | solution.py:67
  139.0 2.6 %gather_fusion.1 = bf16[512,512]{1,0:T(8,128)(2,1)} fusion(bf16[1024,512]{1,0:T(8,128)(2,1)S(1)} %bitcast.108, s32[1024]{0:T(1024)S(1)} %pad_clamp_fusion), kind=kCustom, calls=%fused_computation.1 | custom fusion | bytes 1050624 | tf_op jit(solution)/shard_map/gather | solution.py:68
  141.6 2.1 %fusion.14 = bf16[64,512]{1,0:T(8,128)(2,1)} fusion(bf16[512,512]{1,0:T(8,128)(2,1)} %gather_fusion.1, f32[64,8]{1,0:T(8,128)S(1)} %copy.15), kind=kLoop, calls=%fused_computation.19 | loop fusion | flops 753664 | bytes 591872 | tf_op jit(solution)/shard_map/reduce_sum | solution.py:69
  (27 shorter events, 1.2 us)
Async XLA Ops:
  0.0 86.5 %copy-start = (bf16[2,1024,512]{2,1,0:T(8,128)(2,1)S(1)}, bf16[2,1024,512]{2,1,0:T(8,128)(2,1)}, u32[]{:S(2)}) copy-start(bf16[2,1024,512]{2,1,0:T(8,128)(2,1)} %param.13) | copy-start | bytes 6291460
  7.5 13.7 %all-to-all-start = ((s32[16,1,64]{2,1,0:T(1,128)}), s32[16,1,64]{2,1,0:T(1,128)S(1)}, u32[]{:S(2)}, u32[]{:S(2)}) async-start(s32[16,1,64]{2,1,0:T(1,128)} %all_to_all.12), calls=%async_computation | async-start | bytes 16384 | tf_op jit(solution)/shard_map/all_to_all | solution.py:51
  21.2 45.5 %all-to-all-start.1 = ((bf16[16,64,1024]{2,1,0:T(8,128)(2,1)}), bf16[16,64,1024]{2,1,0:T(8,128)(2,1)}, u32[]{:S(2)}, u32[]{:S(2)}) async-start(bf16[16,64,1024]{2,1,0:T(8,128)(2,1)} %bitcast.109), calls=%async_computation.1 | async-start | bytes 4194304 | tf_op jit(solution)/shard_map/all_to_all | solution.py:50
  97.9 18.2 %copy-start.1 = (bf16[64,8]{0,1:T(8,128)(2,1)S(1)}, bf16[64,8]{0,1:T(8,128)(2,1)}, u32[]{:S(2)}) copy-start(bf16[64,8]{0,1:T(8,128)(2,1)} %param.10) | copy-start | bytes 3076
  104.8 34.1 %all-to-all-start.2 = ((bf16[16,64,512]{2,1,0:T(8,128)(2,1)}), bf16[16,64,512]{2,1,0:T(8,128)(2,1)S(1)}, u32[]{:S(2)}, u32[]{:S(2)}) async-start(bf16[16,64,512]{2,1,0:T(8,128)(2,1)} %bitcast.110), calls=%async_computation.2 | async-start | bytes 2097152 | tf_op jit(solution)/shard_map/all_to_all | solution.py:67
where the time goes:
time: 145 us; the launch traced here: 144 us
  waiting for transfers between devices  63.2 us (44%)
  local copies, waits for them, and re-layouts  29.2 us (20%)
  starting transfers between devices  23 us (16%)
  matrix products  22.5 us (16%)
  other arithmetic  5.63 us (4%)
    all_to_all x1, waiting for transfers between devices, local(): lax.all_to_all(outgoing, 'expert', split_axis=0, concat_axis=0, tiled=True)  38.5 us
    all_to_all x1, waiting for transfers between devices, local(): lax.all_to_all(picked, 'expert', split_axis=0, concat_axis=0, tiled=True)  22.8 us
    dot_general x1, matrix products, apply_experts(): jnp.einsum('sech,ehd->secd', hidden, down_core, preferred_element_type=jn...  11.3 us
    all_to_all x1, starting transfers between devices, local(): lax.all_to_all(picked, 'expert', split_axis=0, concat_axis=0, tiled=True)  11.2 us
    dot_general x1, matrix products, apply_experts(): jnp.einsum('secr,erh->sech', arrived, gate_core, preferred_element_type=j...  11.2 us
    scatter x1, local copies, waits for them, and re-layouts, local(): grouped = jnp.zeros((local_experts * room, rank_in), jnp.bfloat16).at[pla...  8.6 us
    all_to_all x1, starting transfers between devices, local(): lax.all_to_all(member_tags, 'expert', split_axis=0, concat_axis=0, tiled=...  7.39 us
    gather x1, local copies, waits for them, and re-layouts, local(): result[jnp.minimum(place, local_experts * room - 1)]  6.98 us
  transfers between devices with their start and end apart: 3, of which 3 were waited for; matrix products, arithmetic and copies ran while one was open for 5% of the time, Pallas kernels for 0%

commit v1 on v0

v1 whole, which is shorter than its diff:
```python
import functools

import jax
import jax.numpy as jnp
from jax import lax
from jax.experimental import pallas as pl
from jax.experimental.pallas import tpu as pltpu
from jax.sharding import PartitionSpec as P

LANES = 128
VMEM_SPEC = pl.BlockSpec(memory_space=pltpu.VMEM)


def tag_kernel(local_experts, codes_ref, devices_ref, members_ref, scores_ref, out_ref):
    rank_in = codes_ref.shape[1]
    rows = codes_ref.shape[0]
    lanes = out_ref.shape[1] - rank_in
    ids = devices_ref[...] * local_experts + members_ref[...]
    scores = scores_ref[...].astype(jnp.float32)
    lane = lax.broadcasted_iota(jnp.int32, (rows, lanes), 1)
    spread = jnp.zeros((rows, lanes), jnp.float32)
    for k in range(ids.shape[1]):
        spread = jnp.where(lane == ids[:, k : k + 1], scores[:, k : k + 1], spread)
    out_ref[:, :rank_in] = codes_ref[...]
    out_ref[:, rank_in:] = spread.astype(jnp.bfloat16)


def tag_tokens(codes, devices, members, scores, local_experts, experts):
    lanes = -(-experts // LANES) * LANES
    rows, rank_in = codes.shape
    return pl.pallas_call(
        functools.partial(tag_kernel, local_experts),
        out_shape=jax.ShapeDtypeStruct((rows, rank_in + lanes), jnp.bfloat16),
        in_specs=[VMEM_SPEC] * 4,
        out_specs=VMEM_SPEC,
        name="tag_tokens",
    )(codes, devices, members, scores)


def expert_kernel(first_ref, *refs):
    blocks, (gate_ref, up_ref, down_ref, near_ref, far_ref, rows_ref) = refs[:4], refs[4:]
    local_experts, rank_in, hidden_units = gate_ref.shape
    size = blocks[0].shape[0]
    for i, block in enumerate(blocks):
        rows_ref[i * size : (i + 1) * size, :] = block[...]
    scores = rows_ref[:, rank_in:].astype(jnp.float32)
    total = jnp.sum(scores, axis=1, keepdims=True)
    lane = lax.broadcasted_iota(jnp.int32, scores.shape, 1)
    codes = rows_ref[:, :rank_in]
    out = jnp.zeros((codes.shape[0], down_ref.shape[2]), jnp.float32)
    own = jnp.zeros_like(total)
    for e in range(local_experts):
        score = jnp.sum(jnp.where(lane == first_ref[0] + e, scores, 0.0), axis=1, keepdims=True)
        own = own + score
        gate = jnp.dot(codes, gate_ref[e], preferred_element_type=jnp.float32)
        up = jnp.dot(codes, up_ref[e], preferred_element_type=jnp.float32)
        hidden = gate / (1.0 + jnp.exp(-gate)) * up
        hidden = jnp.where(score > 0.0, hidden, 0.0).astype(jnp.bfloat16)
        out = out + jnp.dot(hidden, down_ref[e], preferred_element_type=jnp.float32)
    weight = 2.5 * own / total
    out = (weight * out.astype(jnp.bfloat16).astype(jnp.float32)).astype(jnp.bfloat16)
    near_ref[...] = out[: 2 * size].reshape(near_ref.shape)
    far_ref[...] = out[2 * size :].reshape(far_ref.shape)


def apply_experts(first, blocks, gate_core, up_core, down_core):
    rows, width = blocks[0].shape
    local_experts, rank_in, hidden_units = gate_core.shape
    rank_out = down_core.shape[2]
    half = jax.ShapeDtypeStruct((2, rows, rank_out), jnp.bfloat16)
    flops = 2 * 4 * rows * local_experts * hidden_units * (2 * rank_in + rank_out)
    return pl.pallas_call(
        expert_kernel,
        out_shape=(half, half),
        in_specs=[pl.BlockSpec(memory_space=pltpu.SMEM)] + [VMEM_SPEC] * 7,
        out_specs=(VMEM_SPEC, VMEM_SPEC),
        scratch_shapes=[pltpu.VMEM((4 * rows, width), jnp.bfloat16)],
        compiler_params=pltpu.CompilerParams(vmem_limit_bytes=24 * 1024 * 1024),
        cost_estimate=pl.CostEstimate(flops=flops, bytes_accessed=4 * rows * width * 2, transcendentals=0),
        name="apply_experts",
    )(first, *blocks, gate_core, up_core, down_core)


def local(token_codes, route_devices, route_members, gate_scores, gate_core, up_core, down_core):
    size = lax.axis_size("expert")
    local_experts = gate_core.shape[0]
    columns = size // 4

    def exchange(array, mask):
        return lax.ppermute(array, "expert", [(i, i ^ mask) for i in range(size)])

    first = (lax.axis_index("expert") * local_experts).astype(jnp.int32).reshape(1)
    own = tag_tokens(
        token_codes, route_devices, route_members, gate_scores, local_experts, local_experts * size
    )
    gate_core = pltpu.with_memory_space_constraint(gate_core, pltpu.VMEM)
    up_core = pltpu.with_memory_space_constraint(up_core, pltpu.VMEM)
    down_core = pltpu.with_memory_space_constraint(down_core, pltpu.VMEM)
    mixed = None
    gathered = [own] + [exchange(own, 4 * j) for j in range(1, columns)]
    finished = []
    for j, block in enumerate(gathered):
        across = exchange(block, 2)
        blocks = [block, across, exchange(block, 1), exchange(across, 1)]
        near, far = apply_experts(first, blocks, gate_core, up_core, down_core)
        pair = near.astype(jnp.float32) + exchange(far, 1).astype(jnp.float32)
        pair = pair.astype(jnp.bfloat16)
        done = pair[0].astype(jnp.float32) + exchange(pair[1], 2).astype(jnp.float32)
        finished.append(exchange(done.astype(jnp.bfloat16), 4 * j) if j else done)
    mixed = sum(part.astype(jnp.float32) for part in finished)
    return mixed.astype(jnp.bfloat16)


def solution(mesh):
    tokens = P(("groups", "expert"), None)
    experts = P("expert", None, None)
    return jax.shard_map(
        local,
        mesh=mesh,
        in_specs=(tokens,) * 4 + (experts,) * 3,
        out_specs=tokens,
        check_vma=False,
    )
```

time: 145 us -> 67.1 us (0.46)
  waiting for transfers between devices: 63.2 us -> 11.5 us
  matrix products: 22.5 us -> 0 us
  local copies, waits for them, and re-layouts: 29.2 us -> 11 us
  Pallas kernels: 0 us -> 13.5 us
  starting transfers between devices: 23 us -> 29.6 us
  other arithmetic: 5.63 us -> 0.86 us
    all_to_all x3 -> x0, waiting for transfers between devices: 63.2 us -> none  [the longest x1 38.5 us: local(): lax.all_to_all(outgoing, 'expert', split_axis=0, concat_axis=0, tiled=True)]
    ppermute x0 -> x26, starting transfers between devices: none -> 29.6 us  [exchange(): return lax.ppermute(array, 'expert', [(i, i ^ mask) for i in range(size)])]
    all_to_all x3 -> x0, starting transfers between devices: 23 us -> none  [the longest x1 11.2 us: local(): lax.all_to_all(picked, 'expert', split_axis=0, concat_axis=0, tiled=True)]
    dot_general x2 -> x0, matrix products: 22.5 us -> none  [the longest x1 11.3 us: apply_experts(): jnp.einsum('sech,ehd->secd', hidden, down_core, preferred_element_type=jn...]
    scatter x3 -> x0, local copies, waits for them, and re-layouts: 15.5 us -> none  [the longest x1 8.6 us: local(): grouped = jnp.zeros((local_experts * room, rank_in), jnp.bfloat16).at[pla...]
    pallas_call x0 -> x5, Pallas kernels: none -> 13.5 us  [the longest x4 11.8 us: apply_experts(): pl.pallas_call(expert_kernel, out_shape=(half, half), in_specs=[pl.BlockS...]
    ppermute x0 -> x26, waiting for transfers between devices: none -> 11.5 us  [exchange(): return lax.ppermute(array, 'expert', [(i, i ^ mask) for i in range(size)])]
    gather x2 -> x0, local copies, waits for them, and re-layouts: 9.59 us -> none  [the longest x1 6.98 us: local(): result[jnp.minimum(place, local_experts * room - 1)]]
  transfers between devices with their start and end apart: 3 -> 26, of which waited for: 3 -> 6; matrix products, arithmetic and copies ran while one was open for 5% -> 0% of each run, Pallas kernels for 0% -> 18%
where the time goes in v1:
time: 67.1 us; the launch traced here: 66.7 us
  starting transfers between devices  29.6 us (44%)
  Pallas kernels  13.5 us (20%)
  waiting for transfers between devices  11.5 us (17%)
  local copies, waits for them, and re-layouts  11 us (16%)
  other arithmetic  0.86 us (1%)
    ppermute x26, starting transfers between devices, exchange(): return lax.ppermute(array, 'expert', [(i, i ^ mask) for i in range(size)])  29.6 us
    pallas_call x4, Pallas kernels, apply_experts(): pl.pallas_call(expert_kernel, out_shape=(half, half), in_specs=[pl.BlockS...  11.8 us
    ppermute x26, waiting for transfers between devices, exchange(): return lax.ppermute(array, 'expert', [(i, i ^ mask) for i in range(size)])  11.5 us
    unnamed x17, local copies, waits for them, and re-layouts  11 us
    pallas_call x1, Pallas kernels, tag_tokens(): pl.pallas_call(functools.partial(tag_kernel, local_experts), out_shape=ja...  1.76 us
  transfers between devices with their start and end apart: 26, of which 6 were waited for; matrix products, arithmetic and copies ran while one was open for 0% of the time, Pallas kernels for 18%

profile of v1, /device:TPU:0, one launch (start us, length us, event | category | flops | bytes accessed | tf_op | source)
XLA Modules:
  0.0 66.7 jit_solution(3665962402551678910)
XLA Ops:
  0.0 1.4 %copy.10.scores_ref = bf16[64,8]{1,0:T(8,128)(2,1)} copy(bf16[64,8]{0,1:T(8,128)(2,1)} %param.10) | data formatting | bytes 2048 | tf_op args[3]
  1.4 1.4 %copy.8.devices_ref = s32[64,8]{1,0:T(8,128)} copy(s32[64,8]{0,1:T(8,128)} %param.8) | data formatting | bytes 4096 | tf_op args[1]
  2.7 1.4 %copy.9.members_ref = s32[64,8]{1,0:T(8,128)} copy(s32[64,8]{0,1:T(8,128)} %param.9) | data formatting | bytes 4096 | tf_op args[2]
  4.1 1.8 %tag_tokens.1.refs_0_ = bf16[64,1152]{1,0:T(8,128)(2,1)} custom-call(bf16[64,1024]{1,0:T(8,128)(2,1)} %codes_ref.1, s32[64,8]{1,0:T(8,128)} %copy.8.devices_ref, s32[64,8]{1,0:T(8,128)} %copy.9.members_ref, bf16[64,8]{1,0:T(8,128)(2,1)} %copy.10.scores_ref), custom_call_target="tpu_custom_call" | custom-call | tf_op jit(solution)/shard_map/tag_tokens/pallas_call | solution.py:31
  5.9 3.0 %collective-permute-start = (bf16[64,1152]{1,0:T(8,128)(2,1)}, bf16[64,1152]{1,0:T(8,128)(2,1)S(1)}, u32[]{:S(2)}, u32[]{:S(2)}) collective-permute-start(bf16[64,1152]{1,0:T(8,128)(2,1)} %tag_tokens.1.refs_0_), channel_id=1, source_target_pairs={{0,2},{1,3},{2,0},{3,1},{4,6},{5,7},{6,4},{7,5},{8,10},{9,11},{10,... | collective-permute-start | bytes 442376 | tf_op jit(solution)/shard_map/ppermute | solution.py:90
  8.8 3.6 %collective-permute-start.19 = (bf16[64,1152]{1,0:T(8,128)(2,1)}, bf16[64,1152]{1,0:T(8,128)(2,1)S(1)}, u32[]{:S(2)}, u32[]{:S(2)}) collective-permute-start(bf16[64,1152]{1,0:T(8,128)(2,1)} %tag_tokens.1.refs_0_), channel_id=1, source_target_pairs={{0,12},{1,13},{2,14},{3,15},{4,8},{5,9},{6,10},{7,11},{8,4},{9,5},... | collective-permute-start | bytes 442376 | tf_op jit(solution)/shard_map/ppermute | solution.py:90
  13.0 2.8 %collective-permute-start.12 = (bf16[64,1152]{1,0:T(8,128)(2,1)}, bf16[64,1152]{1,0:T(8,128)(2,1)S(1)}, u32[]{:S(2)}, u32[]{:S(2)}) collective-permute-start(bf16[64,1152]{1,0:T(8,128)(2,1)} %tag_tokens.1.refs_0_), channel_id=1, source_target_pairs={{0,8},{1,9},{2,10},{3,11},{4,12},{5,13},{6,14},{7,15},{8,0},{9,1},... | collective-permute-start | bytes 442376 | tf_op jit(solution)/shard_map/ppermute | solution.py:90
  15.7 1.6 %collective-permute-start.5 = (bf16[64,1152]{1,0:T(8,128)(2,1)}, bf16[64,1152]{1,0:T(8,128)(2,1)S(1)}, u32[]{:S(2)}, u32[]{:S(2)}) collective-permute-start(bf16[64,1152]{1,0:T(8,128)(2,1)} %tag_tokens.1.refs_0_), channel_id=1, source_target_pairs={{0,4},{1,5},{2,6},{3,7},{4,0},{5,1},{6,2},{7,3},{8,12},{9,13},{10,... | collective-permute-start | bytes 442376 | tf_op jit(solution)/shard_map/ppermute | solution.py:90
  17.3 1.5 %collective-permute-start.20 = (bf16[64,1152]{1,0:T(8,128)(2,1)S(1)}, bf16[64,1152]{1,0:T(8,128)(2,1)S(1)}, u32[]{:S(2)}, u32[]{:S(2)}) collective-permute-start(bf16[64,1152]{1,0:T(8,128)(2,1)S(1)} %collective-permute-done.19.refs_0_), channel_id=1, source_target_pairs={{0,2},{1,3},{2,0},{3,1},{4,6},{5,7},{6,4},{7,5},{8,10},{9,11},{10,... | collective-permute-start | bytes 442376 | tf_op jit(solution)/shard_map/ppermute | solution.py:90
  18.8 2.2 %copy-done = bf16[2,1024,1024]{2,1,0:T(8,128)(2,1)S(1)} copy-done((bf16[2,1024,1024]{2,1,0:T(8,128)(2,1)S(1)}, bf16[2,1024,1024]{2,1,0:T(8,128)(2,1)}, u32[]{:S(2)}) %copy-start) | copy-done | bytes 4194328
  21.0 2.2 %copy-done.2 = bf16[2,1024,1024]{2,1,0:T(8,128)(2,1)S(1)} copy-done((bf16[2,1024,1024]{2,1,0:T(8,128)(2,1)S(1)}, bf16[2,1024,1024]{2,1,0:T(8,128)(2,1)}, u32[]{:S(2)}) %copy-start.2) | copy-done | bytes 4194328
  23.2 1.6 %copy-done.4 = bf16[2,1024,512]{2,1,0:T(8,128)(2,1)S(1)} copy-done((bf16[2,1024,512]{2,1,0:T(8,128)(2,1)S(1)}, bf16[2,1024,512]{2,1,0:T(8,128)(2,1)}, u32[]{:S(2)}) %copy-start.4) | copy-done | bytes 2097176
  25.7 2.9 %apply_experts.4 = (bf16[2,64,512]{2,1,0:T(8,128)(2,1)S(1)}, bf16[2,64,512]{2,1,0:T(8,128)(2,1)S(1)}) custom-call(s32[1]{0:T(128)} %bitcast.first_ref, bf16[64,1152]{1,0:T(8,128)(2,1)S(1)} %copy-done.6, bf16[64,1152]{1,0:T(8,128)(2,1)S(1)} %collective-permute-done.refs_1_, bf16[64,1152]{1,0:T(8,128)(2,1)S(1)} %collective-permute-done.1.refs_2_, ...), custom_call_target="tpu_custom_call" | custom-call | flops 2684354560 | bytes 589824 | tf_op jit(solution)/shard_map/apply_experts/pallas_call | solution.py:72
  29.8 1.5 %collective-permute-start.6 = (bf16[64,1152]{1,0:T(8,128)(2,1)S(1)}, bf16[64,1152]{1,0:T(8,128)(2,1)S(1)}, u32[]{:S(2)}, u32[]{:S(2)}) collective-permute-start(bf16[64,1152]{1,0:T(8,128)(2,1)S(1)} %collective-permute-done.5.refs_0_), channel_id=1, source_target_pairs={{0,2},{1,3},{2,0},{3,1},{4,6},{5,7},{6,4},{7,5},{8,10},{9,11},{10,... | collective-permute-start | bytes 442376 | tf_op jit(solution)/shard_map/ppermute | solution.py:90
  32.0 4.0 %collective-permute-done.13.refs_1_ = bf16[64,1152]{1,0:T(8,128)(2,1)S(1)} collective-permute-done((bf16[64,1152]{1,0:T(8,128)(2,1)S(1)}, bf16[64,1152]{1,0:T(8,128)(2,1)S(1)}, u32[]{:S(2)}, u32[]{:S(2)}) %collective-permute-start.13) | collective-permute-done | bytes 147488 | tf_op jit(solution)/shard_map/ppermute | solution.py:90
  36.0 2.7 %collective-permute-done.6.refs_1_ = bf16[64,1152]{1,0:T(8,128)(2,1)S(1)} collective-permute-done((bf16[64,1152]{1,0:T(8,128)(2,1)S(1)}, bf16[64,1152]{1,0:T(8,128)(2,1)S(1)}, u32[]{:S(2)}, u32[]{:S(2)}) %collective-permute-start.6) | collective-permute-done | bytes 147488 | tf_op jit(solution)/shard_map/ppermute | solution.py:90
  39.2 2.9 %apply_experts.7 = (bf16[2,64,512]{2,1,0:T(8,128)(2,1)S(1)}, bf16[2,64,512]{2,1,0:T(8,128)(2,1)S(1)}) custom-call(s32[1]{0:T(128)} %bitcast.first_ref, bf16[64,1152]{1,0:T(8,128)(2,1)S(1)} %collective-permute-done.19.refs_0_, bf16[64,1152]{1,0:T(8,128)(2,1)S(1)} %collective-permute-done.20.refs_1_, bf16[64,1152]{1,0:T(8,128)(2,1)S(1)} %collective-permute-done.21.refs_2_, ...), custom_call_target="tpu_custom_call" | custom-call | flops 2684354560 | bytes 589824 | tf_op jit(solution)/shard_map/apply_experts/pallas_call | solution.py:72
  42.5 2.9 %apply_experts.6 = (bf16[2,64,512]{2,1,0:T(8,128)(2,1)S(1)}, bf16[2,64,512]{2,1,0:T(8,128)(2,1)S(1)}) custom-call(s32[1]{0:T(128)} %bitcast.first_ref, bf16[64,1152]{1,0:T(8,128)(2,1)S(1)} %collective-permute-done.12.refs_0_, bf16[64,1152]{1,0:T(8,128)(2,1)S(1)} %collective-permute-done.13.refs_1_, bf16[64,1152]{1,0:T(8,128)(2,1)S(1)} %collective-permute-done.14.refs_2_, ...), custom_call_target="tpu_custom_call" | custom-call | flops 2684354560 | bytes 589824 | tf_op jit(solution)/shard_map/apply_experts/pallas_call | solution.py:72
  45.8 2.9 %apply_experts.5 = (bf16[2,64,512]{2,1,0:T(8,128)(2,1)S(1)}, bf16[2,64,512]{2,1,0:T(8,128)(2,1)S(1)}) custom-call(s32[1]{0:T(128)} %bitcast.first_ref, bf16[64,1152]{1,0:T(8,128)(2,1)S(1)} %collective-permute-done.5.refs_0_, bf16[64,1152]{1,0:T(8,128)(2,1)S(1)} %collective-permute-done.6.refs_1_, bf16[64,1152]{1,0:T(8,128)(2,1)S(1)} %collective-permute-done.7.refs_2_, ...), custom_call_target="tpu_custom_call" | custom-call | flops 2684354560 | bytes 589824 | tf_op jit(solution)/shard_map/apply_experts/pallas_call | solution.py:72
  49.1 1.6 %collective-permute-start.24 = (bf16[64,512]{1,0:T(8,128)(2,1)S(1)}, bf16[64,512]{1,0:T(8,128)(2,1)S(1)}, u32[]{:S(2)}, u32[]{:S(2)}) collective-permute-start(bf16[64,512]{1,0:T(8,128)(2,1)S(1)} %slice_bitcast_fusion), channel_id=1, source_target_pairs={{0,2},{1,3},{2,0},{3,1},{4,6},{5,7},{6,4},{7,5},{8,10},{9,11},{10,... | collective-permute-start | bytes 196616 | tf_op jit(solution)/shard_map/ppermute | solution.py:90
  51.3 1.6 %collective-permute-start.10 = (bf16[64,512]{1,0:T(8,128)(2,1)S(1)}, bf16[64,512]{1,0:T(8,128)(2,1)S(1)}, u32[]{:S(2)}, u32[]{:S(2)}) collective-permute-start(bf16[64,512]{1,0:T(8,128)(2,1)S(1)} %slice_bitcast_fusion.4), channel_id=1, source_target_pairs={{0,2},{1,3},{2,0},{3,1},{4,6},{5,7},{6,4},{7,5},{8,10},{9,11},{10,... | collective-permute-start | bytes 196616 | tf_op jit(solution)/shard_map/ppermute | solution.py:90
  53.5 3.2 %collective-permute-start.25 = (bf16[64,512]{1,0:T(8,128)(2,1)S(1)}, bf16[64,512]{1,0:T(8,128)(2,1)S(1)}, u32[]{:S(2)}, u32[]{:S(2)}) collective-permute-start(bf16[64,512]{1,0:T(8,128)(2,1)S(1)} %fusion), channel_id=1, source_target_pairs={{0,12},{1,13},{2,14},{3,15},{4,8},{5,9},{6,10},{7,11},{8,4},{9,5},... | collective-permute-start | bytes 196616 | tf_op jit(solution)/shard_map/ppermute | solution.py:90
  56.7 4.9 %collective-permute-start.18 = (bf16[64,512]{1,0:T(8,128)(2,1)S(1)}, bf16[64,512]{1,0:T(8,128)(2,1)S(1)}, u32[]{:S(2)}, u32[]{:S(2)}) collective-permute-start(bf16[64,512]{1,0:T(8,128)(2,1)S(1)} %fusion.1), channel_id=1, source_target_pairs={{0,8},{1,9},{2,10},{3,11},{4,12},{5,13},{6,14},{7,15},{8,0},{9,1},... | collective-permute-start | bytes 196616 | tf_op jit(solution)/shard_map/ppermute | solution.py:90
  62.3 2.9 %collective-permute-done.18 = bf16[64,512]{1,0:T(8,128)(2,1)S(1)} collective-permute-done((bf16[64,512]{1,0:T(8,128)(2,1)S(1)}, bf16[64,512]{1,0:T(8,128)(2,1)S(1)}, u32[]{:S(2)}, u32[]{:S(2)}) %collective-permute-start.18) | collective-permute-done | bytes 65568 | tf_op jit(solution)/shard_map/ppermute | solution.py:90
  (62 shorter events, 8.1 us)
Async XLA Ops:
  5.9 7.0 %collective-permute-start = (bf16[64,1152]{1,0:T(8,128)(2,1)}, bf16[64,1152]{1,0:T(8,128)(2,1)S(1)}, u32[]{:S(2)}, u32[]{:S(2)}) collective-permute-start(bf16[64,1152]{1,0:T(8,128)(2,1)} %tag_tokens.1.refs_0_), channel_id=1, source_target_pairs={{0,2},{1,3},{2,0},{3,1},{4,6},{5,7},{6,4},{7,5},{8,10},{9,11},{10,... | collective-permute-start | bytes 442376 | tf_op jit(solution)/shard_map/ppermute | solution.py:90
  8.8 8.5 %collective-permute-start.19 = (bf16[64,1152]{1,0:T(8,128)(2,1)}, bf16[64,1152]{1,0:T(8,128)(2,1)S(1)}, u32[]{:S(2)}, u32[]{:S(2)}) collective-permute-start(bf16[64,1152]{1,0:T(8,128)(2,1)} %tag_tokens.1.refs_0_), channel_id=1, source_target_pairs={{0,12},{1,13},{2,14},{3,15},{4,8},{5,9},{6,10},{7,11},{8,4},{9,5},... | collective-permute-start | bytes 442376 | tf_op jit(solution)/shard_map/ppermute | solution.py:90
  12.5 6.4 %collective-permute-start.1 = (bf16[64,1152]{1,0:T(8,128)(2,1)}, bf16[64,1152]{1,0:T(8,128)(2,1)S(1)}, u32[]{:S(2)}, u32[]{:S(2)}) collective-permute-start(bf16[64,1152]{1,0:T(8,128)(2,1)} %tag_tokens.1.refs_0_), channel_id=1, source_target_pairs={{0,1},{1,0},{2,3},{3,2},{4,5},{5,4},{6,7},{7,6},{8,9},{9,8},{10,11... | collective-permute-start | bytes 442376 | tf_op jit(solution)/shard_map/ppermute | solution.py:90
  12.9 5.9 %collective-permute-start.2 = (bf16[64,1152]{1,0:T(8,128)(2,1)S(1)}, bf16[64,1152]{1,0:T(8,128)(2,1)S(1)}, u32[]{:S(2)}, u32[]{:S(2)}) collective-permute-start(bf16[64,1152]{1,0:T(8,128)(2,1)S(1)} %collective-permute-done.refs_1_), channel_id=1, source_target_pairs={{0,1},{1,0},{2,3},{3,2},{4,5},{5,4},{6,7},{7,6},{8,9},{9,8},{10,11... | collective-permute-start | bytes 442376 | tf_op jit(solution)/shard_map/ppermute | solution.py:90
  13.0 16.3 %collective-permute-start.12 = (bf16[64,1152]{1,0:T(8,128)(2,1)}, bf16[64,1152]{1,0:T(8,128)(2,1)S(1)}, u32[]{:S(2)}, u32[]{:S(2)}) collective-permute-start(bf16[64,1152]{1,0:T(8,128)(2,1)} %tag_tokens.1.refs_0_), channel_id=1, source_target_pairs={{0,8},{1,9},{2,10},{3,11},{4,12},{5,13},{6,14},{7,15},{8,0},{9,1},... | collective-permute-start | bytes 442376 | tf_op jit(solution)/shard_map/ppermute | solution.py:90
  15.7 13.6 %collective-permute-start.5 = (bf16[64,1152]{1,0:T(8,128)(2,1)}, bf16[64,1152]{1,0:T(8,128)(2,1)S(1)}, u32[]{:S(2)}, u32[]{:S(2)}) collective-permute-start(bf16[64,1152]{1,0:T(8,128)(2,1)} %tag_tokens.1.refs_0_), channel_id=1, source_target_pairs={{0,4},{1,5},{2,6},{3,7},{4,0},{5,1},{6,2},{7,3},{8,12},{9,13},{10,... | collective-permute-start | bytes 442376 | tf_op jit(solution)/shard_map/ppermute | solution.py:90
  17.3 12.5 %collective-permute-start.20 = (bf16[64,1152]{1,0:T(8,128)(2,1)S(1)}, bf16[64,1152]{1,0:T(8,128)(2,1)S(1)}, u32[]{:S(2)}, u32[]{:S(2)}) collective-permute-start(bf16[64,1152]{1,0:T(8,128)(2,1)S(1)} %collective-permute-done.19.refs_0_), channel_id=1, source_target_pairs={{0,2},{1,3},{2,0},{3,1},{4,6},{5,7},{6,4},{7,5},{8,10},{9,11},{10,... | collective-permute-start | bytes 442376 | tf_op jit(solution)/shard_map/ppermute | solution.py:90
  28.7 2.7 %collective-permute-start.21 = (bf16[64,1152]{1,0:T(8,128)(2,1)S(1)}, bf16[64,1152]{1,0:T(8,128)(2,1)S(1)}, u32[]{:S(2)}, u32[]{:S(2)}) collective-permute-start(bf16[64,1152]{1,0:T(8,128)(2,1)S(1)} %collective-permute-done.19.refs_0_), channel_id=1, source_target_pairs={{0,1},{1,0},{2,3},{3,2},{4,5},{5,4},{6,7},{7,6},{8,9},{9,8},{10,11... | collective-permute-start | bytes 442376 | tf_op jit(solution)/shard_map/ppermute | solution.py:90
  29.2 12.9 %collective-permute-start.14 = (bf16[64,1152]{1,0:T(8,128)(2,1)S(1)}, bf16[64,1152]{1,0:T(8,128)(2,1)S(1)}, u32[]{:S(2)}, u32[]{:S(2)}) collective-permute-start(bf16[64,1152]{1,0:T(8,128)(2,1)S(1)} %collective-permute-done.12.refs_0_), channel_id=1, source_target_pairs={{0,1},{1,0},{2,3},{3,2},{4,5},{5,4},{6,7},{7,6},{8,9},{9,8},{10,11... | collective-permute-start | bytes 442376 | tf_op jit(solution)/shard_map/ppermute | solution.py:90
  29.3 6.6 %collective-permute-start.13 = (bf16[64,1152]{1,0:T(8,128)(2,1)S(1)}, bf16[64,1152]{1,0:T(8,128)(2,1)S(1)}, u32[]{:S(2)}, u32[]{:S(2)}) collective-permute-start(bf16[64,1152]{1,0:T(8,128)(2,1)S(1)} %collective-permute-done.12.refs_0_), channel_id=1, source_target_pairs={{0,2},{1,3},{2,0},{3,1},{4,6},{5,7},{6,4},{7,5},{8,10},{9,11},{10,... | collective-permute-start | bytes 442376 | tf_op jit(solution)/shard_map/ppermute | solution.py:90
  29.8 8.9 %collective-permute-start.6 = (bf16[64,1152]{1,0:T(8,128)(2,1)S(1)}, bf16[64,1152]{1,0:T(8,128)(2,1)S(1)}, u32[]{:S(2)}, u32[]{:S(2)}) collective-permute-start(bf16[64,1152]{1,0:T(8,128)(2,1)S(1)} %collective-permute-done.5.refs_0_), channel_id=1, source_target_pairs={{0,2},{1,3},{2,0},{3,1},{4,6},{5,7},{6,4},{7,5},{8,10},{9,11},{10,... | collective-permute-start | bytes 442376 | tf_op jit(solution)/shard_map/ppermute | solution.py:90
  31.4 7.3 %collective-permute-start.22 = (bf16[64,1152]{1,0:T(8,128)(2,1)S(1)}, bf16[64,1152]{1,0:T(8,128)(2,1)S(1)}, u32[]{:S(2)}, u32[]{:S(2)}) collective-permute-start(bf16[64,1152]{1,0:T(8,128)(2,1)S(1)} %collective-permute-done.20.refs_1_), channel_id=1, source_target_pairs={{0,1},{1,0},{2,3},{3,2},{4,5},{5,4},{6,7},{7,6},{8,9},{9,8},{10,11... | collective-permute-start | bytes 442376 | tf_op jit(solution)/shard_map/ppermute | solution.py:90
  31.4 14.3 %collective-permute-start.7 = (bf16[64,1152]{1,0:T(8,128)(2,1)S(1)}, bf16[64,1152]{1,0:T(8,128)(2,1)S(1)}, u32[]{:S(2)}, u32[]{:S(2)}) collective-permute-start(bf16[64,1152]{1,0:T(8,128)(2,1)S(1)} %collective-permute-done.5.refs_0_), channel_id=1, source_target_pairs={{0,1},{1,0},{2,3},{3,2},{4,5},{5,4},{6,7},{7,6},{8,9},{9,8},{10,11... | collective-permute-start | bytes 442376 | tf_op jit(solution)/shard_map/ppermute | solution.py:90
  36.0 6.5 %collective-permute-start.15 = (bf16[64,1152]{1,0:T(8,128)(2,1)S(1)}, bf16[64,1152]{1,0:T(8,128)(2,1)S(1)}, u32[]{:S(2)}, u32[]{:S(2)}) collective-permute-start(bf16[64,1152]{1,0:T(8,128)(2,1)S(1)} %collective-permute-done.13.refs_1_), channel_id=1, source_target_pairs={{0,1},{1,0},{2,3},{3,2},{4,5},{5,4},{6,7},{7,6},{8,9},{9,8},{10,11... | collective-permute-start | bytes 442376 | tf_op jit(solution)/shard_map/ppermute | solution.py:90
  38.7 7.1 %collective-permute-start.8 = (bf16[64,1152]{1,0:T(8,128)(2,1)S(1)}, bf16[64,1152]{1,0:T(8,128)(2,1)S(1)}, u32[]{:S(2)}, u32[]{:S(2)}) collective-permute-start(bf16[64,1152]{1,0:T(8,128)(2,1)S(1)} %collective-permute-done.6.refs_1_), channel_id=1, source_target_pairs={{0,1},{1,0},{2,3},{3,2},{4,5},{5,4},{6,7},{7,6},{8,9},{9,8},{10,11... | collective-permute-start | bytes 442376 | tf_op jit(solution)/shard_map/ppermute | solution.py:90
  38.7 23.6 %collective-permute-start.4 = (bf16[64,512]{1,0:T(8,128)(2,1)S(1)}, bf16[64,512]{1,0:T(8,128)(2,1)S(1)}, u32[]{:S(2)}, u32[]{:S(2)}) collective-permute-start(bf16[64,512]{1,0:T(8,128)(2,1)S(1)} %slice_bitcast_fusion.6), channel_id=1, source_target_pairs={{0,2},{1,3},{2,0},{3,1},{4,6},{5,7},{6,4},{7,5},{8,10},{9,11},{10,... | collective-permute-start | bytes 196616 | tf_op jit(solution)/shard_map/ppermute | solution.py:90
  42.1 6.9 %collective-permute-start.23 = (bf16[2,64,512]{2,1,0:T(8,128)(2,1)S(1)}, bf16[2,64,512]{2,1,0:T(8,128)(2,1)S(1)}, u32[]{:S(2)}, u32[]{:S(2)}) collective-permute-start(bf16[2,64,512]{2,1,0:T(8,128)(2,1)S(1)} %get-tuple-element.20), channel_id=1, source_target_pairs={{0,1},{1,0},{2,3},{3,2},{4,5},{5,4},{6,7},{7,6},{8,9},{9,8},{10,11... | collective-permute-start | bytes 393224 | tf_op jit(solution)/shard_map/ppermute | solution.py:90
  45.4 5.2 %collective-permute-start.16 = (bf16[2,64,512]{2,1,0:T(8,128)(2,1)S(1)}, bf16[2,64,512]{2,1,0:T(8,128)(2,1)S(1)}, u32[]{:S(2)}, u32[]{:S(2)}) collective-permute-start(bf16[2,64,512]{2,1,0:T(8,128)(2,1)S(1)} %get-tuple-element.18), channel_id=1, source_target_pairs={{0,1},{1,0},{2,3},{3,2},{4,5},{5,4},{6,7},{7,6},{8,9},{9,8},{10,11... | collective-permute-start | bytes 393224 | tf_op jit(solution)/shard_map/ppermute | solution.py:90
  49.1 4.4 %collective-permute-start.24 = (bf16[64,512]{1,0:T(8,128)(2,1)S(1)}, bf16[64,512]{1,0:T(8,128)(2,1)S(1)}, u32[]{:S(2)}, u32[]{:S(2)}) collective-permute-start(bf16[64,512]{1,0:T(8,128)(2,1)S(1)} %slice_bitcast_fusion), channel_id=1, source_target_pairs={{0,2},{1,3},{2,0},{3,1},{4,6},{5,7},{6,4},{7,5},{8,10},{9,11},{10,... | collective-permute-start | bytes 196616 | tf_op jit(solution)/shard_map/ppermute | solution.py:90
  50.7 6.0 %collective-permute-start.17 = (bf16[64,512]{1,0:T(8,128)(2,1)S(1)}, bf16[64,512]{1,0:T(8,128)(2,1)S(1)}, u32[]{:S(2)}, u32[]{:S(2)}) collective-permute-start(bf16[64,512]{1,0:T(8,128)(2,1)S(1)} %slice_bitcast_fusion.2), channel_id=1, source_target_pairs={{0,2},{1,3},{2,0},{3,1},{4,6},{5,7},{6,4},{7,5},{8,10},{9,11},{10,... | collective-permute-start | bytes 196616 | tf_op jit(solution)/shard_map/ppermute | solution.py:90
  51.3 10.4 %collective-permute-start.10 = (bf16[64,512]{1,0:T(8,128)(2,1)S(1)}, bf16[64,512]{1,0:T(8,128)(2,1)S(1)}, u32[]{:S(2)}, u32[]{:S(2)}) collective-permute-start(bf16[64,512]{1,0:T(8,128)(2,1)S(1)} %slice_bitcast_fusion.4), channel_id=1, source_target_pairs={{0,2},{1,3},{2,0},{3,1},{4,6},{5,7},{6,4},{7,5},{8,10},{9,11},{10,... | collective-permute-start | bytes 196616 | tf_op jit(solution)/shard_map/ppermute | solution.py:90
  53.5 8.8 %collective-permute-start.25 = (bf16[64,512]{1,0:T(8,128)(2,1)S(1)}, bf16[64,512]{1,0:T(8,128)(2,1)S(1)}, u32[]{:S(2)}, u32[]{:S(2)}) collective-permute-start(bf16[64,512]{1,0:T(8,128)(2,1)S(1)} %fusion), channel_id=1, source_target_pairs={{0,12},{1,13},{2,14},{3,15},{4,8},{5,9},{6,10},{7,11},{8,4},{9,5},... | collective-permute-start | bytes 196616 | tf_op jit(solution)/shard_map/ppermute | solution.py:90
  56.7 8.5 %collective-permute-start.18 = (bf16[64,512]{1,0:T(8,128)(2,1)S(1)}, bf16[64,512]{1,0:T(8,128)(2,1)S(1)}, u32[]{:S(2)}, u32[]{:S(2)}) collective-permute-start(bf16[64,512]{1,0:T(8,128)(2,1)S(1)} %fusion.1), channel_id=1, source_target_pairs={{0,8},{1,9},{2,10},{3,11},{4,12},{5,13},{6,14},{7,15},{8,0},{9,1},... | collective-permute-start | bytes 196616 | tf_op jit(solution)/shard_map/ppermute | solution.py:90
  61.7 4.3 %collective-permute-start.11 = (bf16[64,512]{1,0:T(8,128)(2,1)S(1)}, bf16[64,512]{1,0:T(8,128)(2,1)S(1)}, u32[]{:S(2)}, u32[]{:S(2)}) collective-permute-start(bf16[64,512]{1,0:T(8,128)(2,1)S(1)} %fusion.2), channel_id=1, source_target_pairs={{0,4},{1,5},{2,6},{3,7},{4,0},{5,1},{6,2},{7,3},{8,12},{9,13},{10,... | collective-permute-start | bytes 196616 | tf_op jit(solution)/shard_map/ppermute | solution.py:90
  (9 other events, 47.7 us)

commit v2 on v1

--- a/solution.py
+++ b/solution.py
@@ -12,17 +12,16 @@
 
 
 def tag_kernel(local_experts, codes_ref, devices_ref, members_ref, scores_ref, out_ref):
-    rank_in = codes_ref.shape[1]
-    rows = codes_ref.shape[0]
+    rows, rank_in = codes_ref.shape
     lanes = out_ref.shape[1] - rank_in
     ids = devices_ref[...] * local_experts + members_ref[...]
     scores = scores_ref[...].astype(jnp.float32)
-    lane = lax.broadcasted_iota(jnp.int32, (rows, lanes), 1)
-    spread = jnp.zeros((rows, lanes), jnp.float32)
-    for k in range(ids.shape[1]):
-        spread = jnp.where(lane == ids[:, k : k + 1], scores[:, k : k + 1], spread)
+    expert = lax.broadcasted_iota(jnp.int32, (lanes, rows), 0)
+    spread = jnp.zeros((lanes, rows), jnp.float32)
+    for k in range(ids.shape[0]):
+        spread = jnp.where(expert == ids[k : k + 1, :], scores[k : k + 1, :], spread)
     out_ref[:, :rank_in] = codes_ref[...]
-    out_ref[:, rank_in:] = spread.astype(jnp.bfloat16)
+    out_ref[:, rank_in:] = spread.T.astype(jnp.bfloat16)
 
 
 def tag_tokens(codes, devices, members, scores, local_experts, experts):
@@ -34,11 +33,11 @@
         in_specs=[VMEM_SPEC] * 4,
         out_specs=VMEM_SPEC,
         name="tag_tokens",
-    )(codes, devices, members, scores)
+    )(codes, devices.T, members.T, scores.T)
 
 
-def expert_kernel(first_ref, *refs):
-    blocks, (gate_ref, up_ref, down_ref, near_ref, far_ref, rows_ref) = refs[:4], refs[4:]
+def expert_rows(first_ref, blocks, weights, before, near_ref, far_ref, rows_ref):
+    gate_ref, up_ref, down_ref = weights
     local_experts, rank_in, hidden_units = gate_ref.shape
     size = blocks[0].shape[0]
     for i, block in enumerate(blocks):
@@ -52,10 +51,13 @@
     for e in range(local_experts):
         score = jnp.sum(jnp.where(lane == first_ref[0] + e, scores, 0.0), axis=1, keepdims=True)
         own = own + score
+        before(e, 0)
         gate = jnp.dot(codes, gate_ref[e], preferred_element_type=jnp.float32)
+        before(e, 1)
         up = jnp.dot(codes, up_ref[e], preferred_element_type=jnp.float32)
         hidden = gate / (1.0 + jnp.exp(-gate)) * up
         hidden = jnp.where(score > 0.0, hidden, 0.0).astype(jnp.bfloat16)
+        before(e, 2)
         out = out + jnp.dot(hidden, down_ref[e], preferred_element_type=jnp.float32)
     weight = 2.5 * own / total
     out = (weight * out.astype(jnp.bfloat16).astype(jnp.float32)).astype(jnp.bfloat16)
@@ -63,22 +65,47 @@
     far_ref[...] = out[2 * size :].reshape(far_ref.shape)
 
 
-def apply_experts(first, blocks, gate_core, up_core, down_core):
+def load_and_apply_kernel(first_ref, *refs):
+    blocks, sources, near_ref, far_ref = refs[:4], refs[4:7], refs[7], refs[8]
+    weights, rows_ref, semaphores = refs[9:12], refs[12], refs[13]
+    copies = [
+        [
+            pltpu.make_async_copy(source.at[e], kept.at[e], semaphores.at[e, k])
+            for k, (source, kept) in enumerate(zip(sources, weights))
+        ]
+        for e in range(sources[0].shape[0])
+    ]
+    for group in copies:
+        for copy in group:
+            copy.start()
+    expert_rows(
+        first_ref, blocks, weights, lambda e, k: copies[e][k].wait(), near_ref, far_ref, rows_ref
+    )
+
+
+def apply_kernel(first_ref, *refs):
+    expert_rows(first_ref, refs[:4], refs[4:7], lambda e, k: None, *refs[7:])
+
+
+def apply_experts(first, blocks, weights, load):
     rows, width = blocks[0].shape
-    local_experts, rank_in, hidden_units = gate_core.shape
-    rank_out = down_core.shape[2]
+    local_experts, rank_in, hidden_units = weights[0].shape
+    rank_out = weights[2].shape[2]
     half = jax.ShapeDtypeStruct((2, rows, rank_out), jnp.bfloat16)
     flops = 2 * 4 * rows * local_experts * hidden_units * (2 * rank_in + rank_out)
+    held = tuple(pltpu.VMEM(w.shape, w.dtype) for w in weights) if load else ()
+    place = pl.BlockSpec(memory_space=pltpu.HBM) if load else VMEM_SPEC
     return pl.pallas_call(
-        expert_kernel,
-        out_shape=(half, half),
-        in_specs=[pl.BlockSpec(memory_space=pltpu.SMEM)] + [VMEM_SPEC] * 7,
-        out_specs=(VMEM_SPEC, VMEM_SPEC),
-        scratch_shapes=[pltpu.VMEM((4 * rows, width), jnp.bfloat16)],
+        load_and_apply_kernel if load else apply_kernel,
+        out_shape=(half, half) + held,
+        in_specs=[pl.BlockSpec(memory_space=pltpu.SMEM)] + [VMEM_SPEC] * 4 + [place] * 3,
+        out_specs=(VMEM_SPEC,) * (2 + len(held)),
+        scratch_shapes=[pltpu.VMEM((4 * rows, width), jnp.bfloat16)]
+        + ([pltpu.SemaphoreType.DMA((local_experts, 3))] if load else []),
         compiler_params=pltpu.CompilerParams(vmem_limit_bytes=24 * 1024 * 1024),
         cost_estimate=pl.CostEstimate(flops=flops, bytes_accessed=4 * rows * width * 2, transcendentals=0),
-        name="apply_experts",
-    )(first, *blocks, gate_core, up_core, down_core)
+        name="load_and_apply" if load else "apply_experts",
+    )(first, *blocks, *weights)
 
 
 def local(token_codes, route_devices, route_members, gate_scores, gate_core, up_core, down_core):
@@ -93,16 +120,18 @@
     own = tag_tokens(
         token_codes, route_devices, route_members, gate_scores, local_experts, local_experts * size
     )
-    gate_core = pltpu.with_memory_space_constraint(gate_core, pltpu.VMEM)
-    up_core = pltpu.with_memory_space_constraint(up_core, pltpu.VMEM)
-    down_core = pltpu.with_memory_space_constraint(down_core, pltpu.VMEM)
-    mixed = None
-    gathered = [own] + [exchange(own, 4 * j) for j in range(1, columns)]
+    weights = (gate_core, up_core, down_core)
+    gathered = [own]
+    for j in range(1, columns):
+        low = j & -j
+        gathered.append(exchange(gathered[j - low], 4 * low))
     finished = []
     for j, block in enumerate(gathered):
         across = exchange(block, 2)
         blocks = [block, across, exchange(block, 1), exchange(across, 1)]
-        near, far = apply_experts(first, blocks, gate_core, up_core, down_core)
+        near, far, *held = apply_experts(first, blocks, weights, j == 0)
+        if j == 0:
+            weights = tuple(held)
         pair = near.astype(jnp.float32) + exchange(far, 1).astype(jnp.float32)
         pair = pair.astype(jnp.bfloat16)
         done = pair[0].astype(jnp.float32) + exchange(pair[1], 2).astype(jnp.float32)

time: 67.1 us -> 60.9 us (0.908)
  starting transfers between devices: 29.6 us -> 23.1 us
  local copies, waits for them, and re-layouts: 11 us -> 6.9 us
  waiting for transfers between devices: 11.5 us -> 14.5 us
  Pallas kernels: 13.5 us -> 15.1 us
    ppermute x26, starting transfers between devices: 29.6 us -> 23.1 us  [exchange(): return lax.ppermute(array, 'expert', [(i, i ^ mask) for i in range(size)])]
    unnamed x17 -> x8, local copies, waits for them, and re-layouts: 11 us -> 6.87 us
    ppermute x26, waiting for transfers between devices: 11.5 us -> 14.5 us  [exchange(): return lax.ppermute(array, 'expert', [(i, i ^ mask) for i in range(size)])]
    pallas_call x4, Pallas kernels: 11.8 us -> 13.5 us  [apply_experts(): pl.pallas_call(load_and_apply_kernel if load else apply_kernel, out_shape...]
  transfers between devices with their start and end apart: 26 -> 26, of which waited for: 6 -> 6; matrix products, arithmetic and copies ran while one was open for 0% -> 0% of each run, Pallas kernels for 18% -> 22%
where the time goes in v2:
time: 60.9 us; the launch traced here: 60.7 us
  starting transfers between devices  23.1 us (38%)
  Pallas kernels  15.1 us (25%)
  waiting for transfers between devices  14.5 us (24%)
  local copies, waits for them, and re-layouts  6.9 us (11%)
  other arithmetic  0.87 us (1%)
    ppermute x26, starting transfers between devices, exchange(): return lax.ppermute(array, 'expert', [(i, i ^ mask) for i in range(size)])  23.1 us
    ppermute x26, waiting for transfers between devices, exchange(): return lax.ppermute(array, 'expert', [(i, i ^ mask) for i in range(size)])  14.5 us
    pallas_call x4, Pallas kernels, apply_experts(): pl.pallas_call(load_and_apply_kernel if load else apply_kernel, out_shape...  13.5 us
    unnamed x8, local copies, waits for them, and re-layouts  6.87 us
    pallas_call x1, Pallas kernels, tag_tokens(): pl.pallas_call(functools.partial(tag_kernel, local_experts), out_shape=ja...  1.67 us
  transfers between devices with their start and end apart: 26, of which 6 were waited for; matrix products, arithmetic and copies ran while one was open for 0% of the time, Pallas kernels for 22%

profile of v2, /device:TPU:0, one launch (start us, length us, event | category | flops | bytes accessed | tf_op | source)
XLA Modules:
  0.0 60.7 jit_solution(14834082279231102393)
XLA Ops:
  0.0 1.7 %tag_tokens.1.refs_0_ = bf16[64,1152]{1,0:T(8,128)(2,1)} custom-call(bf16[64,1024]{1,0:T(8,128)(2,1)} %codes_ref.1, s32[8,64]{1,0:T(8,128)} %bitcast.32, s32[8,64]{1,0:T(8,128)} %bitcast.33, bf16[8,64]{1,0:T(8,128)(2,1)} %bitcast.34), custom_call_target="tpu_custom_call" | custom-call | tf_op jit(solution)/shard_map/tag_tokens/pallas_call | solution.py:30
  1.7 3.0 %collective-permute-start = (bf16[64,1152]{1,0:T(8,128)(2,1)}, bf16[64,1152]{1,0:T(8,128)(2,1)S(1)}, u32[]{:S(2)}, u32[]{:S(2)}) collective-permute-start(bf16[64,1152]{1,0:T(8,128)(2,1)} %tag_tokens.1.refs_0_), channel_id=1, source_target_pairs={{0,2},{1,3},{2,0},{3,1},{4,6},{5,7},{6,4},{7,5},{8,10},{9,11},{10,... | collective-permute-start | bytes 442376 | tf_op jit(solution)/shard_map/ppermute | solution.py:117
  4.6 1.6 %collective-permute-start.5 = (bf16[64,1152]{1,0:T(8,128)(2,1)}, bf16[64,1152]{1,0:T(8,128)(2,1)S(1)}, u32[]{:S(2)}, u32[]{:S(2)}) collective-permute-start(bf16[64,1152]{1,0:T(8,128)(2,1)} %tag_tokens.1.refs_0_), channel_id=1, source_target_pairs={{0,4},{1,5},{2,6},{3,7},{4,0},{5,1},{6,2},{7,3},{8,12},{9,13},{10,... | collective-permute-start | bytes 442376 | tf_op jit(solution)/shard_map/ppermute | solution.py:117
  6.2 2.6 %collective-permute-start.12 = (bf16[64,1152]{1,0:T(8,128)(2,1)}, bf16[64,1152]{1,0:T(8,128)(2,1)S(1)}, u32[]{:S(2)}, u32[]{:S(2)}) collective-permute-start(bf16[64,1152]{1,0:T(8,128)(2,1)} %tag_tokens.1.refs_0_), channel_id=1, source_target_pairs={{0,8},{1,9},{2,10},{3,11},{4,12},{5,13},{6,14},{7,15},{8,0},{9,1},... | collective-permute-start | bytes 442376 | tf_op jit(solution)/shard_map/ppermute | solution.py:117
  9.3 3.2 %collective-permute-done.5.refs_0_ = bf16[64,1152]{1,0:T(8,128)(2,1)S(1)} collective-permute-done((bf16[64,1152]{1,0:T(8,128)(2,1)}, bf16[64,1152]{1,0:T(8,128)(2,1)S(1)}, u32[]{:S(2)}, u32[]{:S(2)}) %collective-permute-start.5) | collective-permute-done | bytes 147488 | tf_op jit(solution)/shard_map/ppermute | solution.py:117
  12.8 2.9 %collective-permute-done.12.refs_0_ = bf16[64,1152]{1,0:T(8,128)(2,1)S(1)} collective-permute-done((bf16[64,1152]{1,0:T(8,128)(2,1)}, bf16[64,1152]{1,0:T(8,128)(2,1)S(1)}, u32[]{:S(2)}, u32[]{:S(2)}) %collective-permute-start.12) | collective-permute-done | bytes 147488 | tf_op jit(solution)/shard_map/ppermute | solution.py:117
  16.0 2.2 %copy-done = bf16[2,1024,1024]{2,1,0:T(8,128)(2,1)S(1)} copy-done((bf16[2,1024,1024]{2,1,0:T(8,128)(2,1)S(1)}, bf16[2,1024,1024]{2,1,0:T(8,128)(2,1)}, u32[]{:S(2)}) %copy-start) | copy-done | bytes 4194328
  18.2 2.2 %copy-done.1 = bf16[2,1024,1024]{2,1,0:T(8,128)(2,1)S(1)} copy-done((bf16[2,1024,1024]{2,1,0:T(8,128)(2,1)S(1)}, bf16[2,1024,1024]{2,1,0:T(8,128)(2,1)}, u32[]{:S(2)}) %copy-start.1) | copy-done | bytes 4194328
  20.4 1.6 %copy-done.2 = bf16[2,1024,512]{2,1,0:T(8,128)(2,1)S(1)} copy-done((bf16[2,1024,512]{2,1,0:T(8,128)(2,1)S(1)}, bf16[2,1024,512]{2,1,0:T(8,128)(2,1)}, u32[]{:S(2)}) %copy-start.2) | copy-done | bytes 2097176
  22.0 0.9 %copy-done.3 = bf16[64,1152]{1,0:T(8,128)(2,1)S(1)} copy-done((bf16[64,1152]{1,0:T(8,128)(2,1)S(1)}, bf16[64,1152]{1,0:T(8,128)(2,1)}, u32[]{:S(2)}) %copy-start.3) | copy-done | bytes 147480
  22.9 4.6 %load_and_apply.1 = (bf16[2,64,512]{2,1,0:T(8,128)(2,1)S(1)}, bf16[2,64,512]{2,1,0:T(8,128)(2,1)S(1)}, bf16[2,1024,1024]{2,1,0:T(8,128)(2,1)S(1)}, bf16[2,1024,1...) custom-call(s32[1]{0:T(128)} %bitcast.first_ref, bf16[64,1152]{1,0:T(8,128)(2,1)S(1)} %copy-done.3, ...), custom_call_target="tpu_custom_call" | custom-call | flops 2684354560 | bytes 589824 | tf_op jit(solution)/shard_map/load_and_apply/pallas_call | solution.py:98
  29.1 1.5 %collective-permute-start.20 = (bf16[64,1152]{1,0:T(8,128)(2,1)S(1)}, bf16[64,1152]{1,0:T(8,128)(2,1)S(1)}, u32[]{:S(2)}, u32[]{:S(2)}) collective-permute-start(bf16[64,1152]{1,0:T(8,128)(2,1)S(1)} %collective-permute-done.19.refs_0_), channel_id=1, source_target_pairs={{0,2},{1,3},{2,0},{3,1},{4,6},{5,7},{6,4},{7,5},{8,10},{9,11},{10,... | collective-permute-start | bytes 442376 | tf_op jit(solution)/shard_map/ppermute | solution.py:117
  30.8 4.0 %collective-permute-done.13.refs_1_ = bf16[64,1152]{1,0:T(8,128)(2,1)S(1)} collective-permute-done((bf16[64,1152]{1,0:T(8,128)(2,1)S(1)}, bf16[64,1152]{1,0:T(8,128)(2,1)S(1)}, u32[]{:S(2)}, u32[]{:S(2)}) %collective-permute-start.13) | collective-permute-done | bytes 147488 | tf_op jit(solution)/shard_map/ppermute | solution.py:117
  35.3 2.9 %apply_experts.3 = (bf16[2,64,512]{2,1,0:T(8,128)(2,1)S(1)}, bf16[2,64,512]{2,1,0:T(8,128)(2,1)S(1)}) custom-call(s32[1]{0:T(128)} %bitcast.first_ref, bf16[64,1152]{1,0:T(8,128)(2,1)S(1)} %collective-permute-done.5.refs_0_, bf16[64,1152]{1,0:T(8,128)(2,1)S(1)} %collective-permute-done.6.refs_1_, bf16[64,1152]{1,0:T(8,128)(2,1)S(1)} %collective-permute-done.7.refs_2_, ...), custom_call_target="tpu_custom_call" | custom-call | flops 2684354560 | bytes 589824 | tf_op jit(solution)/shard_map/apply_experts/pallas_call | solution.py:98
  38.6 2.9 %apply_experts.4 = (bf16[2,64,512]{2,1,0:T(8,128)(2,1)S(1)}, bf16[2,64,512]{2,1,0:T(8,128)(2,1)S(1)}) custom-call(s32[1]{0:T(128)} %bitcast.first_ref, bf16[64,1152]{1,0:T(8,128)(2,1)S(1)} %collective-permute-done.12.refs_0_, bf16[64,1152]{1,0:T(8,128)(2,1)S(1)} %collective-permute-done.13.refs_1_, bf16[64,1152]{1,0:T(8,128)(2,1)S(1)} %collective-permute-done.14.refs_2_, ...), custom_call_target="tpu_custom_call" | custom-call | flops 2684354560 | bytes 589824 | tf_op jit(solution)/shard_map/apply_experts/pallas_call | solution.py:98
  42.2 1.6 %collective-permute-start.10 = (bf16[64,512]{1,0:T(8,128)(2,1)S(1)}, bf16[64,512]{1,0:T(8,128)(2,1)S(1)}, u32[]{:S(2)}, u32[]{:S(2)}) collective-permute-start(bf16[64,512]{1,0:T(8,128)(2,1)S(1)} %slice_bitcast_fusion.4), channel_id=1, source_target_pairs={{0,2},{1,3},{2,0},{3,1},{4,6},{5,7},{6,4},{7,5},{8,10},{9,11},{10,... | collective-permute-start | bytes 196616 | tf_op jit(solution)/shard_map/ppermute | solution.py:117
  43.8 0.8 %collective-permute-start.17 = (bf16[64,512]{1,0:T(8,128)(2,1)S(1)}, bf16[64,512]{1,0:T(8,128)(2,1)S(1)}, u32[]{:S(2)}, u32[]{:S(2)}) collective-permute-start(bf16[64,512]{1,0:T(8,128)(2,1)S(1)} %slice_bitcast_fusion.2), channel_id=1, source_target_pairs={{0,2},{1,3},{2,0},{3,1},{4,6},{5,7},{6,4},{7,5},{8,10},{9,11},{10,... | collective-permute-start | bytes 196616 | tf_op jit(solution)/shard_map/ppermute | solution.py:117
  44.6 2.9 %apply_experts.5 = (bf16[2,64,512]{2,1,0:T(8,128)(2,1)S(1)}, bf16[2,64,512]{2,1,0:T(8,128)(2,1)S(1)}) custom-call(s32[1]{0:T(128)} %bitcast.first_ref, bf16[64,1152]{1,0:T(8,128)(2,1)S(1)} %collective-permute-done.19.refs_0_, bf16[64,1152]{1,0:T(8,128)(2,1)S(1)} %collective-permute-done.20.refs_1_, bf16[64,1152]{1,0:T(8,128)(2,1)S(1)} %collective-permute-done.21.refs_2_, ...), custom_call_target="tpu_custom_call" | custom-call | flops 2684354560 | bytes 589824 | tf_op jit(solution)/shard_map/apply_experts/pallas_call | solution.py:98
  47.7 1.8 %collective-permute-start.11 = (bf16[64,512]{1,0:T(8,128)(2,1)S(1)}, bf16[64,512]{1,0:T(8,128)(2,1)S(1)}, u32[]{:S(2)}, u32[]{:S(2)}) collective-permute-start(bf16[64,512]{1,0:T(8,128)(2,1)S(1)} %fusion.2), channel_id=1, source_target_pairs={{0,4},{1,5},{2,6},{3,7},{4,0},{5,1},{6,2},{7,3},{8,12},{9,13},{10,... | collective-permute-start | bytes 196616 | tf_op jit(solution)/shard_map/ppermute | solution.py:117
  49.5 1.4 %collective-permute-start.24 = (bf16[64,512]{1,0:T(8,128)(2,1)S(1)}, bf16[64,512]{1,0:T(8,128)(2,1)S(1)}, u32[]{:S(2)}, u32[]{:S(2)}) collective-permute-start(bf16[64,512]{1,0:T(8,128)(2,1)S(1)} %slice_bitcast_fusion), channel_id=1, source_target_pairs={{0,2},{1,3},{2,0},{3,1},{4,6},{5,7},{6,4},{7,5},{8,10},{9,11},{10,... | collective-permute-start | bytes 196616 | tf_op jit(solution)/shard_map/ppermute | solution.py:117
  50.9 2.3 %collective-permute-start.18 = (bf16[64,512]{1,0:T(8,128)(2,1)S(1)}, bf16[64,512]{1,0:T(8,128)(2,1)S(1)}, u32[]{:S(2)}, u32[]{:S(2)}) collective-permute-start(bf16[64,512]{1,0:T(8,128)(2,1)S(1)} %fusion.1), channel_id=1, source_target_pairs={{0,8},{1,9},{2,10},{3,11},{4,12},{5,13},{6,14},{7,15},{8,0},{9,1},... | collective-permute-start | bytes 196616 | tf_op jit(solution)/shard_map/ppermute | solution.py:117
  53.8 2.5 %collective-permute-start.25 = (bf16[64,512]{1,0:T(8,128)(2,1)S(1)}, bf16[64,512]{1,0:T(8,128)(2,1)S(1)}, u32[]{:S(2)}, u32[]{:S(2)}) collective-permute-start(bf16[64,512]{1,0:T(8,128)(2,1)S(1)} %fusion), channel_id=1, source_target_pairs={{0,12},{1,13},{2,14},{3,15},{4,8},{5,9},{6,10},{7,11},{8,4},{9,5},... | collective-permute-start | bytes 196616 | tf_op jit(solution)/shard_map/ppermute | solution.py:117
  56.3 1.9 %collective-permute-done.18 = bf16[64,512]{1,0:T(8,128)(2,1)S(1)} collective-permute-done((bf16[64,512]{1,0:T(8,128)(2,1)S(1)}, bf16[64,512]{1,0:T(8,128)(2,1)S(1)}, u32[]{:S(2)}, u32[]{:S(2)}) %collective-permute-start.18) | collective-permute-done | bytes 65568 | tf_op jit(solution)/shard_map/ppermute | solution.py:117
  58.3 1.7 %collective-permute-done.25 = bf16[64,512]{1,0:T(8,128)(2,1)S(1)} collective-permute-done((bf16[64,512]{1,0:T(8,128)(2,1)S(1)}, bf16[64,512]{1,0:T(8,128)(2,1)S(1)}, u32[]{:S(2)}, u32[]{:S(2)}) %collective-permute-start.25) | collective-permute-done | bytes 65568 | tf_op jit(solution)/shard_map/ppermute | solution.py:117
  (53 shorter events, 5.8 us)
Async XLA Ops:
  1.7 7.1 %collective-permute-start = (bf16[64,1152]{1,0:T(8,128)(2,1)}, bf16[64,1152]{1,0:T(8,128)(2,1)S(1)}, u32[]{:S(2)}, u32[]{:S(2)}) collective-permute-start(bf16[64,1152]{1,0:T(8,128)(2,1)} %tag_tokens.1.refs_0_), channel_id=1, source_target_pairs={{0,2},{1,3},{2,0},{3,1},{4,6},{5,7},{6,4},{7,5},{8,10},{9,11},{10,... | collective-permute-start | bytes 442376 | tf_op jit(solution)/shard_map/ppermute | solution.py:117
  4.6 7.9 %collective-permute-start.5 = (bf16[64,1152]{1,0:T(8,128)(2,1)}, bf16[64,1152]{1,0:T(8,128)(2,1)S(1)}, u32[]{:S(2)}, u32[]{:S(2)}) collective-permute-start(bf16[64,1152]{1,0:T(8,128)(2,1)} %tag_tokens.1.refs_0_), channel_id=1, source_target_pairs={{0,4},{1,5},{2,6},{3,7},{4,0},{5,1},{6,2},{7,3},{8,12},{9,13},{10,... | collective-permute-start | bytes 442376 | tf_op jit(solution)/shard_map/ppermute | solution.py:117
  6.2 9.5 %collective-permute-start.12 = (bf16[64,1152]{1,0:T(8,128)(2,1)}, bf16[64,1152]{1,0:T(8,128)(2,1)S(1)}, u32[]{:S(2)}, u32[]{:S(2)}) collective-permute-start(bf16[64,1152]{1,0:T(8,128)(2,1)} %tag_tokens.1.refs_0_), channel_id=1, source_target_pairs={{0,8},{1,9},{2,10},{3,11},{4,12},{5,13},{6,14},{7,15},{8,0},{9,1},... | collective-permute-start | bytes 442376 | tf_op jit(solution)/shard_map/ppermute | solution.py:117
  8.8 7.2 %collective-permute-start.1 = (bf16[64,1152]{1,0:T(8,128)(2,1)}, bf16[64,1152]{1,0:T(8,128)(2,1)S(1)}, u32[]{:S(2)}, u32[]{:S(2)}) collective-permute-start(bf16[64,1152]{1,0:T(8,128)(2,1)} %tag_tokens.1.refs_0_), channel_id=1, source_target_pairs={{0,1},{1,0},{2,3},{3,2},{4,5},{5,4},{6,7},{7,6},{8,9},{9,8},{10,11... | collective-permute-start | bytes 442376 | tf_op jit(solution)/shard_map/ppermute | solution.py:117
  8.8 7.2 %collective-permute-start.2 = (bf16[64,1152]{1,0:T(8,128)(2,1)S(1)}, bf16[64,1152]{1,0:T(8,128)(2,1)S(1)}, u32[]{:S(2)}, u32[]{:S(2)}) collective-permute-start(bf16[64,1152]{1,0:T(8,128)(2,1)S(1)} %collective-permute-done.refs_1_), channel_id=1, source_target_pairs={{0,1},{1,0},{2,3},{3,2},{4,5},{5,4},{6,7},{7,6},{8,9},{9,8},{10,11... | collective-permute-start | bytes 442376 | tf_op jit(solution)/shard_map/ppermute | solution.py:117
  12.5 16.1 %collective-permute-start.6 = (bf16[64,1152]{1,0:T(8,128)(2,1)S(1)}, bf16[64,1152]{1,0:T(8,128)(2,1)S(1)}, u32[]{:S(2)}, u32[]{:S(2)}) collective-permute-start(bf16[64,1152]{1,0:T(8,128)(2,1)S(1)} %collective-permute-done.5.refs_0_), channel_id=1, source_target_pairs={{0,2},{1,3},{2,0},{3,1},{4,6},{5,7},{6,4},{7,5},{8,10},{9,11},{10,... | collective-permute-start | bytes 442376 | tf_op jit(solution)/shard_map/ppermute | solution.py:117
  15.7 12.9 %collective-permute-start.19 = (bf16[64,1152]{1,0:T(8,128)(2,1)S(1)}, bf16[64,1152]{1,0:T(8,128)(2,1)S(1)}, u32[]{:S(2)}, u32[]{:S(2)}) collective-permute-start(bf16[64,1152]{1,0:T(8,128)(2,1)S(1)} %collective-permute-done.12.refs_0_), channel_id=1, source_target_pairs={{0,4},{1,5},{2,6},{3,7},{4,0},{5,1},{6,2},{7,3},{8,12},{9,13},{10,... | collective-permute-start | bytes 442376 | tf_op jit(solution)/shard_map/ppermute | solution.py:117
  27.6 3.1 %collective-permute-start.7 = (bf16[64,1152]{1,0:T(8,128)(2,1)S(1)}, bf16[64,1152]{1,0:T(8,128)(2,1)S(1)}, u32[]{:S(2)}, u32[]{:S(2)}) collective-permute-start(bf16[64,1152]{1,0:T(8,128)(2,1)S(1)} %collective-permute-done.5.refs_0_), channel_id=1, source_target_pairs={{0,1},{1,0},{2,3},{3,2},{4,5},{5,4},{6,7},{7,6},{8,9},{9,8},{10,11... | collective-permute-start | bytes 442376 | tf_op jit(solution)/shard_map/ppermute | solution.py:117
  28.1 6.7 %collective-permute-start.13 = (bf16[64,1152]{1,0:T(8,128)(2,1)S(1)}, bf16[64,1152]{1,0:T(8,128)(2,1)S(1)}, u32[]{:S(2)}, u32[]{:S(2)}) collective-permute-start(bf16[64,1152]{1,0:T(8,128)(2,1)S(1)} %collective-permute-done.12.refs_0_), channel_id=1, source_target_pairs={{0,2},{1,3},{2,0},{3,1},{4,6},{5,7},{6,4},{7,5},{8,10},{9,11},{10,... | collective-permute-start | bytes 442376 | tf_op jit(solution)/shard_map/ppermute | solution.py:117
  28.6 9.7 %collective-permute-start.14 = (bf16[64,1152]{1,0:T(8,128)(2,1)S(1)}, bf16[64,1152]{1,0:T(8,128)(2,1)S(1)}, u32[]{:S(2)}, u32[]{:S(2)}) collective-permute-start(bf16[64,1152]{1,0:T(8,128)(2,1)S(1)} %collective-permute-done.12.refs_0_), channel_id=1, source_target_pairs={{0,1},{1,0},{2,3},{3,2},{4,5},{5,4},{6,7},{7,6},{8,9},{9,8},{10,11... | collective-permute-start | bytes 442376 | tf_op jit(solution)/shard_map/ppermute | solution.py:117
  28.6 6.2 %collective-permute-start.8 = (bf16[64,1152]{1,0:T(8,128)(2,1)S(1)}, bf16[64,1152]{1,0:T(8,128)(2,1)S(1)}, u32[]{:S(2)}, u32[]{:S(2)}) collective-permute-start(bf16[64,1152]{1,0:T(8,128)(2,1)S(1)} %collective-permute-done.6.refs_1_), channel_id=1, source_target_pairs={{0,1},{1,0},{2,3},{3,2},{4,5},{5,4},{6,7},{7,6},{8,9},{9,8},{10,11... | collective-permute-start | bytes 442376 | tf_op jit(solution)/shard_map/ppermute | solution.py:117
  29.1 12.7 %collective-permute-start.20 = (bf16[64,1152]{1,0:T(8,128)(2,1)S(1)}, bf16[64,1152]{1,0:T(8,128)(2,1)S(1)}, u32[]{:S(2)}, u32[]{:S(2)}) collective-permute-start(bf16[64,1152]{1,0:T(8,128)(2,1)S(1)} %collective-permute-done.19.refs_0_), channel_id=1, source_target_pairs={{0,2},{1,3},{2,0},{3,1},{4,6},{5,7},{6,4},{7,5},{8,10},{9,11},{10,... | collective-permute-start | bytes 442376 | tf_op jit(solution)/shard_map/ppermute | solution.py:117
  30.7 13.9 %collective-permute-start.21 = (bf16[64,1152]{1,0:T(8,128)(2,1)S(1)}, bf16[64,1152]{1,0:T(8,128)(2,1)S(1)}, u32[]{:S(2)}, u32[]{:S(2)}) collective-permute-start(bf16[64,1152]{1,0:T(8,128)(2,1)S(1)} %collective-permute-done.19.refs_0_), channel_id=1, source_target_pairs={{0,1},{1,0},{2,3},{3,2},{4,5},{5,4},{6,7},{7,6},{8,9},{9,8},{10,11... | collective-permute-start | bytes 442376 | tf_op jit(solution)/shard_map/ppermute | solution.py:117
  34.8 3.8 %collective-permute-start.15 = (bf16[64,1152]{1,0:T(8,128)(2,1)S(1)}, bf16[64,1152]{1,0:T(8,128)(2,1)S(1)}, u32[]{:S(2)}, u32[]{:S(2)}) collective-permute-start(bf16[64,1152]{1,0:T(8,128)(2,1)S(1)} %collective-permute-done.13.refs_1_), channel_id=1, source_target_pairs={{0,1},{1,0},{2,3},{3,2},{4,5},{5,4},{6,7},{7,6},{8,9},{9,8},{10,11... | collective-permute-start | bytes 442376 | tf_op jit(solution)/shard_map/ppermute | solution.py:117
  34.8 21.5 %collective-permute-start.4 = (bf16[64,512]{1,0:T(8,128)(2,1)S(1)}, bf16[64,512]{1,0:T(8,128)(2,1)S(1)}, u32[]{:S(2)}, u32[]{:S(2)}) collective-permute-start(bf16[64,512]{1,0:T(8,128)(2,1)S(1)} %slice_bitcast_fusion.6), channel_id=1, source_target_pairs={{0,2},{1,3},{2,0},{3,1},{4,6},{5,7},{6,4},{7,5},{8,10},{9,11},{10,... | collective-permute-start | bytes 196616 | tf_op jit(solution)/shard_map/ppermute | solution.py:117
  38.3 3.8 %collective-permute-start.9 = (bf16[2,64,512]{2,1,0:T(8,128)(2,1)S(1)}, bf16[2,64,512]{2,1,0:T(8,128)(2,1)S(1)}, u32[]{:S(2)}, u32[]{:S(2)}) collective-permute-start(bf16[2,64,512]{2,1,0:T(8,128)(2,1)S(1)} %get-tuple-element.22), channel_id=1, source_target_pairs={{0,1},{1,0},{2,3},{3,2},{4,5},{5,4},{6,7},{7,6},{8,9},{9,8},{10,11... | collective-permute-start | bytes 393224 | tf_op jit(solution)/shard_map/ppermute | solution.py:117
  41.5 2.2 %collective-permute-start.16 = (bf16[2,64,512]{2,1,0:T(8,128)(2,1)S(1)}, bf16[2,64,512]{2,1,0:T(8,128)(2,1)S(1)}, u32[]{:S(2)}, u32[]{:S(2)}) collective-permute-start(bf16[2,64,512]{2,1,0:T(8,128)(2,1)S(1)} %get-tuple-element.24), channel_id=1, source_target_pairs={{0,1},{1,0},{2,3},{3,2},{4,5},{5,4},{6,7},{7,6},{8,9},{9,8},{10,11... | collective-permute-start | bytes 393224 | tf_op jit(solution)/shard_map/ppermute | solution.py:117
  41.9 2.7 %collective-permute-start.22 = (bf16[64,1152]{1,0:T(8,128)(2,1)S(1)}, bf16[64,1152]{1,0:T(8,128)(2,1)S(1)}, u32[]{:S(2)}, u32[]{:S(2)}) collective-permute-start(bf16[64,1152]{1,0:T(8,128)(2,1)S(1)} %collective-permute-done.20.refs_1_), channel_id=1, source_target_pairs={{0,1},{1,0},{2,3},{3,2},{4,5},{5,4},{6,7},{7,6},{8,9},{9,8},{10,11... | collective-permute-start | bytes 442376 | tf_op jit(solution)/shard_map/ppermute | solution.py:117
  42.2 5.5 %collective-permute-start.10 = (bf16[64,512]{1,0:T(8,128)(2,1)S(1)}, bf16[64,512]{1,0:T(8,128)(2,1)S(1)}, u32[]{:S(2)}, u32[]{:S(2)}) collective-permute-start(bf16[64,512]{1,0:T(8,128)(2,1)S(1)} %slice_bitcast_fusion.4), channel_id=1, source_target_pairs={{0,2},{1,3},{2,0},{3,1},{4,6},{5,7},{6,4},{7,5},{8,10},{9,11},{10,... | collective-permute-start | bytes 196616 | tf_op jit(solution)/shard_map/ppermute | solution.py:117
  43.8 7.0 %collective-permute-start.17 = (bf16[64,512]{1,0:T(8,128)(2,1)S(1)}, bf16[64,512]{1,0:T(8,128)(2,1)S(1)}, u32[]{:S(2)}, u32[]{:S(2)}) collective-permute-start(bf16[64,512]{1,0:T(8,128)(2,1)S(1)} %slice_bitcast_fusion.2), channel_id=1, source_target_pairs={{0,2},{1,3},{2,0},{3,1},{4,6},{5,7},{6,4},{7,5},{8,10},{9,11},{10,... | collective-permute-start | bytes 196616 | tf_op jit(solution)/shard_map/ppermute | solution.py:117
  47.7 8.7 %collective-permute-start.11 = (bf16[64,512]{1,0:T(8,128)(2,1)S(1)}, bf16[64,512]{1,0:T(8,128)(2,1)S(1)}, u32[]{:S(2)}, u32[]{:S(2)}) collective-permute-start(bf16[64,512]{1,0:T(8,128)(2,1)S(1)} %fusion.2), channel_id=1, source_target_pairs={{0,4},{1,5},{2,6},{3,7},{4,0},{5,1},{6,2},{7,3},{8,12},{9,13},{10,... | collective-permute-start | bytes 196616 | tf_op jit(solution)/shard_map/ppermute | solution.py:117
  49.5 4.3 %collective-permute-start.24 = (bf16[64,512]{1,0:T(8,128)(2,1)S(1)}, bf16[64,512]{1,0:T(8,128)(2,1)S(1)}, u32[]{:S(2)}, u32[]{:S(2)}) collective-permute-start(bf16[64,512]{1,0:T(8,128)(2,1)S(1)} %slice_bitcast_fusion), channel_id=1, source_target_pairs={{0,2},{1,3},{2,0},{3,1},{4,6},{5,7},{6,4},{7,5},{8,10},{9,11},{10,... | collective-permute-start | bytes 196616 | tf_op jit(solution)/shard_map/ppermute | solution.py:117
  50.9 7.4 %collective-permute-start.18 = (bf16[64,512]{1,0:T(8,128)(2,1)S(1)}, bf16[64,512]{1,0:T(8,128)(2,1)S(1)}, u32[]{:S(2)}, u32[]{:S(2)}) collective-permute-start(bf16[64,512]{1,0:T(8,128)(2,1)S(1)} %fusion.1), channel_id=1, source_target_pairs={{0,8},{1,9},{2,10},{3,11},{4,12},{5,13},{6,14},{7,15},{8,0},{9,1},... | collective-permute-start | bytes 196616 | tf_op jit(solution)/shard_map/ppermute | solution.py:117
  53.8 6.2 %collective-permute-start.25 = (bf16[64,512]{1,0:T(8,128)(2,1)S(1)}, bf16[64,512]{1,0:T(8,128)(2,1)S(1)}, u32[]{:S(2)}, u32[]{:S(2)}) collective-permute-start(bf16[64,512]{1,0:T(8,128)(2,1)S(1)} %fusion), channel_id=1, source_target_pairs={{0,12},{1,13},{2,14},{3,15},{4,8},{5,9},{6,10},{7,11},{8,4},{9,5},... | collective-permute-start | bytes 196616 | tf_op jit(solution)/shard_map/ppermute | solution.py:117
  (6 other events, 10.4 us)

commit v3 on v1

v3 whole, which is shorter than its diff:
```python
import functools

import jax
import jax.numpy as jnp
from jax import lax
from jax.experimental import pallas as pl
from jax.experimental.pallas import tpu as pltpu
from jax.sharding import PartitionSpec as P

LANES = 128
MIB = 1024 * 1024
VMEM_SPEC = pl.BlockSpec(memory_space=pltpu.VMEM)


def tag_kernel(local_experts, codes_ref, devices_ref, members_ref, scores_ref, out_ref):
    rows, rank_in = codes_ref.shape
    lanes = out_ref.shape[1] - rank_in
    ids = devices_ref[...] * local_experts + members_ref[...]
    scores = scores_ref[...].astype(jnp.float32)
    expert = lax.broadcasted_iota(jnp.int32, (lanes, rows), 0)
    spread = jnp.zeros((lanes, rows), jnp.float32)
    for k in range(ids.shape[0]):
        spread = jnp.where(expert == ids[k : k + 1, :], scores[k : k + 1, :], spread)
    out_ref[:, :rank_in] = codes_ref[...]
    out_ref[:, rank_in:] = spread.T.astype(jnp.bfloat16)


def tag_tokens(codes, devices, members, scores, local_experts, experts):
    lanes = -(-experts // LANES) * LANES
    rows, rank_in = codes.shape
    operands = [
        pltpu.with_memory_space_constraint(operand, pltpu.HBM)
        for operand in (codes, devices.T, members.T, scores.T)
    ]
    return pl.pallas_call(
        functools.partial(tag_kernel, local_experts),
        out_shape=jax.ShapeDtypeStruct((rows, rank_in + lanes), jnp.bfloat16),
        out_specs=VMEM_SPEC,
        compiler_params=pltpu.CompilerParams(vmem_limit_bytes=8 * MIB),
        cost_estimate=pl.CostEstimate(
            flops=8_000_000_000, bytes_accessed=16_000_000, transcendentals=0
        ),
        name="tag_tokens",
    )(*operands)


def expert_kernel(count, *refs):
    blocks, (gate_ref, up_ref, down_ref, near_ref, far_ref, rows_ref) = refs[:count], refs[count:]
    local_experts, rank_in, hidden_units = gate_ref.shape
    at = 0
    for block in blocks:
        rows_ref[at : at + block.shape[0], :] = block[...]
        at += block.shape[0]
    scores = rows_ref[:, rank_in:].astype(jnp.float32)
    total = jnp.sum(scores, axis=1, keepdims=True)
    lane = lax.broadcasted_iota(jnp.int32, scores.shape, 1)
    first = lax.axis_index("expert") * local_experts
    codes = rows_ref[:, :rank_in]
    out = jnp.zeros((codes.shape[0], down_ref.shape[2]), jnp.float32)
    own = jnp.zeros_like(total)
    for e in range(local_experts):
        score = jnp.sum(jnp.where(lane == first + e, scores, 0.0), axis=1, keepdims=True)
        own = own + score
        gate = jnp.dot(codes, gate_ref[e], preferred_element_type=jnp.float32)
        up = jnp.dot(codes, up_ref[e], preferred_element_type=jnp.float32)
        hidden = gate / (1.0 + jnp.exp(-gate)) * up
        hidden = jnp.where(score > 0.0, hidden, 0.0).astype(jnp.bfloat16)
        out = out + jnp.dot(hidden, down_ref[e], preferred_element_type=jnp.float32)
    weight = 2.5 * own / total
    out = (weight * out.astype(jnp.bfloat16).astype(jnp.float32)).astype(jnp.bfloat16)
    half = near_ref.shape[0]
    near_ref[...] = out[:half]
    far_ref[...] = out[half:]


def apply_experts(blocks, weights):
    width = blocks[0].shape[1]
    rows = sum(block.shape[0] for block in blocks)
    local_experts, rank_in, hidden_units = weights[0].shape
    rank_out = weights[2].shape[2]
    half = jax.ShapeDtypeStruct((rows // 2, rank_out), jnp.bfloat16)
    flops = 2 * rows * local_experts * hidden_units * (2 * rank_in + rank_out)
    return pl.pallas_call(
        functools.partial(expert_kernel, len(blocks)),
        out_shape=(half, half),
        in_specs=[VMEM_SPEC] * (len(blocks) + 3),
        out_specs=(VMEM_SPEC, VMEM_SPEC),
        scratch_shapes=[pltpu.VMEM((rows, width), jnp.bfloat16)],
        compiler_params=pltpu.CompilerParams(vmem_limit_bytes=24 * MIB),
        cost_estimate=pl.CostEstimate(
            flops=flops, bytes_accessed=2 * rows * width, transcendentals=0
        ),
        name="apply_experts",
    )(*blocks, *weights)


def wide(array):
    return array.astype(jnp.float32)


def local(token_codes, route_devices, route_members, gate_scores, gate_core, up_core, down_core):
    size = lax.axis_size("expert")
    local_experts = gate_core.shape[0]
    rows = token_codes.shape[0]
    weights = (gate_core, up_core, down_core)

    def exchange(array, mask):
        return lax.ppermute(array, "expert", [(i, i ^ mask) for i in range(size)])

    own = tag_tokens(
        token_codes, route_devices, route_members, gate_scores, local_experts, local_experts * size
    )
    across = exchange(own, 2)
    gathered = {0: own}
    for j in range(1, size // 4):
        low = j & -j
        gathered[j] = exchange(gathered[j - low], 4 * low)
    near_by = lax.optimization_barrier((gathered[1], gathered[2], across))
    middle = exchange(jnp.concatenate(near_by[:2]), 2)
    gathered[3] = exchange(near_by[1], 4)
    pairs = {0: (own, across), 1: (gathered[1], middle[:rows]), 2: (gathered[2], middle[rows:])}
    pairs |= {j: (gathered[j], exchange(gathered[j], 2)) for j in range(3, size // 4)}
    halves, near = {}, None
    for j, blocks in pairs.items():
        blocks = blocks + tuple(exchange(block, 1) for block in blocks)
        near, far = apply_experts(tuple(blocks), weights)
        pair = wide(near) + wide(exchange(far, 1))
        halves[j] = pair if j == 0 else pair.astype(jnp.bfloat16)
    pair = halves[0] + wide(exchange(halves[1], 4))
    mixed = pair[:rows] + wide(exchange(pair[rows:].astype(jnp.bfloat16), 2))
    for j in range(2, size // 4):
        done = wide(halves[j][:rows]) + wide(exchange(halves[j][rows:], 2))
        mixed = mixed + wide(exchange(done.astype(jnp.bfloat16), 4 * j))
    return mixed.astype(jnp.bfloat16)


def solution(mesh):
    tokens = P(("groups", "expert"), None)
    experts = P("expert", None, None)
    return jax.shard_map(
        local,
        mesh=mesh,
        in_specs=(tokens,) * 4 + (experts,) * 3,
        out_specs=tokens,
        check_vma=False,
    )
```

time: 67.1 us -> 51.8 us (0.77)
  local copies, waits for them, and re-layouts: 11 us -> 0.06 us
  starting transfers between devices: 29.6 us -> 20.8 us
  waiting for transfers between devices: 11.5 us -> 16.8 us
    unnamed x17 -> x6, local copies, waits for them, and re-layouts: 11 us -> 0.01 us
    ppermute x26 -> x24, starting transfers between devices: 29.6 us -> 20.8 us  [exchange(): return lax.ppermute(array, 'expert', [(i, i ^ mask) for i in range(size)])]
    ppermute x26 -> x24, waiting for transfers between devices: 11.5 us -> 16.8 us  [exchange(): return lax.ppermute(array, 'expert', [(i, i ^ mask) for i in range(size)])]
  transfers between devices with their start and end apart: 26 -> 24, of which waited for: 6 -> 8; matrix products, arithmetic and copies ran while one was open for 0% -> 0% of each run, Pallas kernels for 18% -> 23%
where the time goes in v3:
time: 51.8 us; the launch traced here: 51.6 us
  starting transfers between devices  20.8 us (40%)
  waiting for transfers between devices  16.8 us (32%)
  Pallas kernels  12.9 us (25%)
  other arithmetic  0.87 us (2%)
    ppermute x24, starting transfers between devices, exchange(): return lax.ppermute(array, 'expert', [(i, i ^ mask) for i in range(size)])  20.8 us
    ppermute x24, waiting for transfers between devices, exchange(): return lax.ppermute(array, 'expert', [(i, i ^ mask) for i in range(size)])  16.8 us
    pallas_call x4, Pallas kernels, apply_experts(): pl.pallas_call(functools.partial(expert_kernel, len(blocks)), out_shape=(...  11.8 us
    pallas_call x1, Pallas kernels, tag_tokens(): pl.pallas_call(functools.partial(tag_kernel, local_experts), out_shape=ja...  1.17 us
  transfers between devices with their start and end apart: 24, of which 8 were waited for; matrix products, arithmetic and copies ran while one was open for 0% of the time, Pallas kernels for 23%

profile of v3, /device:TPU:0, one launch (start us, length us, event | category | flops | bytes accessed | tf_op | source)
XLA Modules:
  0.0 51.6 jit_solution(14671149343023807281)
XLA Ops:
  0.0 1.2 %tag_tokens.1.refs_0_ = bf16[64,1152]{1,0:T(8,128)(2,1)S(1)} custom-call(bf16[64,1024]{1,0:T(8,128)(2,1)} %codes_ref.1, s32[8,64]{1,0:T(8,128)} %bitcast.3, s32[8,64]{1,0:T(8,128)} %bitcast.4, bf16[8,64]{1,0:T(8,128)(2,1)} %bitcast.5), custom_call_target="tpu_custom_call" | custom-call | flops 8000000000 | bytes 16000000 | tf_op jit(solution)/shard_map/tag_tokens/pallas_call | solution.py:35
  1.2 3.1 %collective-permute-start.4 = (bf16[64,1152]{1,0:T(8,128)(2,1)S(1)}, bf16[64,1152]{1,0:T(8,128)(2,1)S(1)}, u32[]{:S(2)}, u32[]{:S(2)}) collective-permute-start(bf16[64,1152]{1,0:T(8,128)(2,1)S(1)} %tag_tokens.1.refs_0_), channel_id=1, source_target_pairs={{0,4},{1,5},{2,6},{3,7},{4,0},{5,1},{6,2},{7,3},{8,12},{9,13},{10,... | collective-permute-start | bytes 442376 | tf_op jit(solution)/shard_map/ppermute | solution.py:108
  4.3 2.6 %collective-permute-start.5 = (bf16[64,1152]{1,0:T(8,128)(2,1)S(1)}, bf16[64,1152]{1,0:T(8,128)(2,1)S(1)}, u32[]{:S(2)}, u32[]{:S(2)}) collective-permute-start(bf16[64,1152]{1,0:T(8,128)(2,1)S(1)} %tag_tokens.1.refs_0_), channel_id=1, source_target_pairs={{0,8},{1,9},{2,10},{3,11},{4,12},{5,13},{6,14},{7,15},{8,0},{9,1},... | collective-permute-start | bytes 442376 | tf_op jit(solution)/shard_map/ppermute | solution.py:108
  6.9 1.5 %collective-permute-start = (bf16[64,1152]{1,0:T(8,128)(2,1)S(1)}, bf16[64,1152]{1,0:T(8,128)(2,1)S(1)}, u32[]{:S(2)}, u32[]{:S(2)}) collective-permute-start(bf16[64,1152]{1,0:T(8,128)(2,1)S(1)} %tag_tokens.1.refs_0_), channel_id=1, source_target_pairs={{0,2},{1,3},{2,0},{3,1},{4,6},{5,7},{6,4},{7,5},{8,10},{9,11},{10,... | collective-permute-start | bytes 442376 | tf_op jit(solution)/shard_map/ppermute | solution.py:108
  8.4 2.3 %collective-permute-done.4.refs_0_ = bf16[64,1152]{1,0:T(8,128)(2,1)S(1)} collective-permute-done((bf16[64,1152]{1,0:T(8,128)(2,1)S(1)}, bf16[64,1152]{1,0:T(8,128)(2,1)S(1)}, u32[]{:S(2)}, u32[]{:S(2)}) %collective-permute-start.4) | collective-permute-done | bytes 147488 | tf_op jit(solution)/shard_map/ppermute | solution.py:108
  10.7 3.0 %collective-permute-done.5.refs_0_ = bf16[64,1152]{1,0:T(8,128)(2,1)S(1)} collective-permute-done((bf16[64,1152]{1,0:T(8,128)(2,1)S(1)}, bf16[64,1152]{1,0:T(8,128)(2,1)S(1)}, u32[]{:S(2)}, u32[]{:S(2)}) %collective-permute-start.5) | collective-permute-done | bytes 147488 | tf_op jit(solution)/shard_map/ppermute | solution.py:108
  13.7 1.6 %collective-permute-start.6 = (bf16[128,1152]{1,0:T(8,128)(2,1)S(1)}, bf16[128,1152]{1,0:T(8,128)(2,1)S(1)}, u32[]{:S(2)}, u32[]{:S(2)}) collective-permute-start(bf16[128,1152]{1,0:T(8,128)(2,1)S(1)} %pad_maximum_fusion), channel_id=1, source_target_pairs={{0,2},{1,3},{2,0},{3,1},{4,6},{5,7},{6,4},{7,5},{8,10},{9,11},{10,... | collective-permute-start | bytes 884744 | tf_op jit(solution)/shard_map/ppermute | solution.py:108
  16.3 4.2 %collective-permute-done.17.refs_0_ = bf16[64,1152]{1,0:T(8,128)(2,1)S(1)} collective-permute-done((bf16[64,1152]{1,0:T(8,128)(2,1)S(1)}, bf16[64,1152]{1,0:T(8,128)(2,1)S(1)}, u32[]{:S(2)}, u32[]{:S(2)}) %collective-permute-start.17) | collective-permute-done | bytes 147488 | tf_op jit(solution)/shard_map/ppermute | solution.py:108
  20.5 1.5 %collective-permute-start.18 = (bf16[64,1152]{1,0:T(8,128)(2,1)S(1)}, bf16[64,1152]{1,0:T(8,128)(2,1)S(1)}, u32[]{:S(2)}, u32[]{:S(2)}) collective-permute-start(bf16[64,1152]{1,0:T(8,128)(2,1)S(1)} %collective-permute-done.17.refs_0_), channel_id=1, source_target_pairs={{0,2},{1,3},{2,0},{3,1},{4,6},{5,7},{6,4},{7,5},{8,10},{9,11},{10,... | collective-permute-start | bytes 442376 | tf_op jit(solution)/shard_map/ppermute | solution.py:108
  22.2 2.9 %apply_experts.4 = (bf16[128,512]{1,0:T(8,128)(2,1)S(1)}, bf16[128,512]{1,0:T(8,128)(2,1)S(1)}) custom-call(bf16[64,1152]{1,0:T(8,128)(2,1)S(1)} %tag_tokens.1.refs_0_, bf16[64,1152]{1,0:T(8,128)(2,1)S(1)} %collective-permute-done.refs_1_, bf16[64,1152]{1,0:T(8,128)(2,1)S(1)} %collective-permute-done.1.refs_2_, ...), custom_call_target="tpu_custom_call" | custom-call | flops 2684354560 | bytes 589824 | tf_op jit(solution)/shard_map/apply_experts/pallas_call | solution.py:83
  25.8 1.0 %collective-permute-done.18.refs_1_ = bf16[64,1152]{1,0:T(8,128)(2,1)S(1)} collective-permute-done((bf16[64,1152]{1,0:T(8,128)(2,1)S(1)}, bf16[64,1152]{1,0:T(8,128)(2,1)S(1)}, u32[]{:S(2)}, u32[]{:S(2)}) %collective-permute-start.18) | collective-permute-done | bytes 147488 | tf_op jit(solution)/shard_map/ppermute | solution.py:108
  27.2 2.9 %apply_experts.5 = (bf16[128,512]{1,0:T(8,128)(2,1)S(1)}, bf16[128,512]{1,0:T(8,128)(2,1)S(1)}) custom-call(bf16[64,1152]{1,0:T(8,128)(2,1)S(1)} %collective-permute-done.4.refs_0_, bf16[64,1152]{1,0:T(8,128)(2,1)S(1)} %get-tuple-element.26.refs_1_, bf16[64,1152]{1,0:T(8,128)(2,1)S(1)} %collective-permute-done.7.refs_2_, ...), custom_call_target="tpu_custom_call" | custom-call | flops 2684354560 | bytes 589824 | tf_op jit(solution)/shard_map/apply_experts/pallas_call | solution.py:83
  30.3 2.9 %apply_experts.7 = (bf16[128,512]{1,0:T(8,128)(2,1)S(1)}, bf16[128,512]{1,0:T(8,128)(2,1)S(1)}) custom-call(bf16[64,1152]{1,0:T(8,128)(2,1)S(1)} %collective-permute-done.17.refs_0_, bf16[64,1152]{1,0:T(8,128)(2,1)S(1)} %collective-permute-done.18.refs_1_, bf16[64,1152]{1,0:T(8,128)(2,1)S(1)} %collective-permute-done.19.refs_2_, ...), custom_call_target="tpu_custom_call" | custom-call | flops 2684354560 | bytes 589824 | tf_op jit(solution)/shard_map/apply_experts/pallas_call | solution.py:83
  33.8 2.9 %apply_experts.6 = (bf16[128,512]{1,0:T(8,128)(2,1)S(1)}, bf16[128,512]{1,0:T(8,128)(2,1)S(1)}) custom-call(bf16[64,1152]{1,0:T(8,128)(2,1)S(1)} %collective-permute-done.5.refs_0_, bf16[64,1152]{1,0:T(8,128)(2,1)S(1)} %get-tuple-element.25.refs_1_, bf16[64,1152]{1,0:T(8,128)(2,1)S(1)} %collective-permute-done.12.refs_2_, ...), custom_call_target="tpu_custom_call" | custom-call | flops 2684354560 | bytes 589824 | tf_op jit(solution)/shard_map/apply_experts/pallas_call | solution.py:83
  36.9 1.0 %collective-permute-start.10 = (bf16[128,512]{1,0:T(8,128)(2,1)S(1)}, bf16[128,512]{1,0:T(8,128)(2,1)S(1)}, u32[]{:S(2)}, u32[]{:S(2)}) collective-permute-start(bf16[128,512]{1,0:T(8,128)(2,1)S(1)} %add_convert_fusion.2), channel_id=1, source_target_pairs={{0,4},{1,5},{2,6},{3,7},{4,0},{5,1},{6,2},{7,3},{8,12},{9,13},{10,... | collective-permute-start | bytes 393224 | tf_op jit(solution)/shard_map/ppermute | solution.py:108
  37.9 1.1 %collective-permute-start.22 = (bf16[64,512]{1,0:T(8,128)(2,1)S(1)}, bf16[64,512]{1,0:T(8,128)(2,1)S(1)}, u32[]{:S(2)}, u32[]{:S(2)}) collective-permute-start(bf16[64,512]{1,0:T(8,128)(2,1)S(1)} %slice.40), channel_id=1, source_target_pairs={{0,2},{1,3},{2,0},{3,1},{4,6},{5,7},{6,4},{7,5},{8,10},{9,11},{10,... | collective-permute-start | bytes 196616 | tf_op jit(solution)/shard_map/ppermute | solution.py:108
  39.1 1.1 %collective-permute-start.15 = (bf16[64,512]{1,0:T(8,128)(2,1)S(1)}, bf16[64,512]{1,0:T(8,128)(2,1)S(1)}, u32[]{:S(2)}, u32[]{:S(2)}) collective-permute-start(bf16[64,512]{1,0:T(8,128)(2,1)S(1)} %slice.38), channel_id=1, source_target_pairs={{0,2},{1,3},{2,0},{3,1},{4,6},{5,7},{6,4},{7,5},{8,10},{9,11},{10,... | collective-permute-start | bytes 196616 | tf_op jit(solution)/shard_map/ppermute | solution.py:108
  40.1 2.7 %collective-permute-done.22 = bf16[64,512]{1,0:T(8,128)(2,1)S(1)} collective-permute-done((bf16[64,512]{1,0:T(8,128)(2,1)S(1)}, bf16[64,512]{1,0:T(8,128)(2,1)S(1)}, u32[]{:S(2)}, u32[]{:S(2)}) %collective-permute-start.22) | collective-permute-done | bytes 65568 | tf_op jit(solution)/shard_map/ppermute | solution.py:108
  42.9 1.9 %collective-permute-start.23 = (bf16[64,512]{1,0:T(8,128)(2,1)S(1)}, bf16[64,512]{1,0:T(8,128)(2,1)S(1)}, u32[]{:S(2)}, u32[]{:S(2)}) collective-permute-start(bf16[64,512]{1,0:T(8,128)(2,1)S(1)} %add_convert_fusion.3), channel_id=1, source_target_pairs={{0,12},{1,13},{2,14},{3,15},{4,8},{5,9},{6,10},{7,11},{8,4},{9,5},... | collective-permute-start | bytes 196616 | tf_op jit(solution)/shard_map/ppermute | solution.py:108
  44.9 1.5 %collective-permute-start.16 = (bf16[64,512]{1,0:T(8,128)(2,1)S(1)}, bf16[64,512]{1,0:T(8,128)(2,1)S(1)}, u32[]{:S(2)}, u32[]{:S(2)}) collective-permute-start(bf16[64,512]{1,0:T(8,128)(2,1)S(1)} %add_convert_fusion.4), channel_id=1, source_target_pairs={{0,8},{1,9},{2,10},{3,11},{4,12},{5,13},{6,14},{7,15},{8,0},{9,1},... | collective-permute-start | bytes 196616 | tf_op jit(solution)/shard_map/ppermute | solution.py:108
  46.4 1.0 %collective-permute-start.11 = (bf16[64,512]{1,0:T(8,128)(2,1)S(1)}, bf16[64,512]{1,0:T(8,128)(2,1)S(1)}, u32[]{:S(2)}, u32[]{:S(2)}) collective-permute-start(bf16[64,512]{1,0:T(8,128)(2,1)S(1)} %slice.51), channel_id=1, source_target_pairs={{0,2},{1,3},{2,0},{3,1},{4,6},{5,7},{6,4},{7,5},{8,10},{9,11},{10,... | collective-permute-start | bytes 196616 | tf_op jit(solution)/shard_map/ppermute | solution.py:108
  47.4 1.6 %collective-permute-done.23 = bf16[64,512]{1,0:T(8,128)(2,1)S(1)} collective-permute-done((bf16[64,512]{1,0:T(8,128)(2,1)S(1)}, bf16[64,512]{1,0:T(8,128)(2,1)S(1)}, u32[]{:S(2)}, u32[]{:S(2)}) %collective-permute-start.23) | collective-permute-done | bytes 65568 | tf_op jit(solution)/shard_map/ppermute | solution.py:108
  49.0 1.9 %collective-permute-done.16 = bf16[64,512]{1,0:T(8,128)(2,1)S(1)} collective-permute-done((bf16[64,512]{1,0:T(8,128)(2,1)S(1)}, bf16[64,512]{1,0:T(8,128)(2,1)S(1)}, u32[]{:S(2)}, u32[]{:S(2)}) %collective-permute-start.16) | collective-permute-done | bytes 65568 | tf_op jit(solution)/shard_map/ppermute | solution.py:108
  51.0 0.7 %fusion.2 = bf16[64,512]{1,0:T(8,128)(2,1)} fusion(f32[128,512]{1,0:T(8,128)S(1)} %convert_add_fusion, bf16[64,512]{1,0:T(8,128)(2,1)S(1)} %collective-permute-done.23, bf16[64,512]{1,0:T(8,128)(2,1)S(1)} %collective-permute-done.16, bf16[64,512]{1,0:T(8,128)(2,1)S(1)} %collective-permute-done.11), kind=kLoop, calls=%fused_computation.9 | loop fusion | flops 229376 | bytes 393216 | tf_op jit(solution)/shard_map/convert_element_type | solution.py:134
  (47 shorter events, 3.3 us)
Async XLA Ops:
  1.2 9.5 %collective-permute-start.4 = (bf16[64,1152]{1,0:T(8,128)(2,1)S(1)}, bf16[64,1152]{1,0:T(8,128)(2,1)S(1)}, u32[]{:S(2)}, u32[]{:S(2)}) collective-permute-start(bf16[64,1152]{1,0:T(8,128)(2,1)S(1)} %tag_tokens.1.refs_0_), channel_id=1, source_target_pairs={{0,4},{1,5},{2,6},{3,7},{4,0},{5,1},{6,2},{7,3},{8,12},{9,13},{10,... | collective-permute-start | bytes 442376 | tf_op jit(solution)/shard_map/ppermute | solution.py:108
  4.3 9.4 %collective-permute-start.5 = (bf16[64,1152]{1,0:T(8,128)(2,1)S(1)}, bf16[64,1152]{1,0:T(8,128)(2,1)S(1)}, u32[]{:S(2)}, u32[]{:S(2)}) collective-permute-start(bf16[64,1152]{1,0:T(8,128)(2,1)S(1)} %tag_tokens.1.refs_0_), channel_id=1, source_target_pairs={{0,8},{1,9},{2,10},{3,11},{4,12},{5,13},{6,14},{7,15},{8,0},{9,1},... | collective-permute-start | bytes 442376 | tf_op jit(solution)/shard_map/ppermute | solution.py:108
  6.9 6.8 %collective-permute-start = (bf16[64,1152]{1,0:T(8,128)(2,1)S(1)}, bf16[64,1152]{1,0:T(8,128)(2,1)S(1)}, u32[]{:S(2)}, u32[]{:S(2)}) collective-permute-start(bf16[64,1152]{1,0:T(8,128)(2,1)S(1)} %tag_tokens.1.refs_0_), channel_id=1, source_target_pairs={{0,2},{1,3},{2,0},{3,1},{4,6},{5,7},{6,4},{7,5},{8,10},{9,11},{10,... | collective-permute-start | bytes 442376 | tf_op jit(solution)/shard_map/ppermute | solution.py:108
  13.7 6.8 %collective-permute-start.6 = (bf16[128,1152]{1,0:T(8,128)(2,1)S(1)}, bf16[128,1152]{1,0:T(8,128)(2,1)S(1)}, u32[]{:S(2)}, u32[]{:S(2)}) collective-permute-start(bf16[128,1152]{1,0:T(8,128)(2,1)S(1)} %pad_maximum_fusion), channel_id=1, source_target_pairs={{0,2},{1,3},{2,0},{3,1},{4,6},{5,7},{6,4},{7,5},{8,10},{9,11},{10,... | collective-permute-start | bytes 884744 | tf_op jit(solution)/shard_map/ppermute | solution.py:108
  15.3 5.1 %collective-permute-start.17 = (bf16[64,1152]{1,0:T(8,128)(2,1)S(1)}, bf16[64,1152]{1,0:T(8,128)(2,1)S(1)}, u32[]{:S(2)}, u32[]{:S(2)}) collective-permute-start(bf16[64,1152]{1,0:T(8,128)(2,1)S(1)} %collective-permute-done.5.refs_0_), channel_id=1, source_target_pairs={{0,4},{1,5},{2,6},{3,7},{4,0},{5,1},{6,2},{7,3},{8,12},{9,13},{10,... | collective-permute-start | bytes 442376 | tf_op jit(solution)/shard_map/ppermute | solution.py:108
  15.8 6.3 %collective-permute-start.1 = (bf16[64,1152]{1,0:T(8,128)(2,1)S(1)}, bf16[64,1152]{1,0:T(8,128)(2,1)S(1)}, u32[]{:S(2)}, u32[]{:S(2)}) collective-permute-start(bf16[64,1152]{1,0:T(8,128)(2,1)S(1)} %tag_tokens.1.refs_0_), channel_id=1, source_target_pairs={{0,1},{1,0},{2,3},{3,2},{4,5},{5,4},{6,7},{7,6},{8,9},{9,8},{10,11... | collective-permute-start | bytes 442376 | tf_op jit(solution)/shard_map/ppermute | solution.py:108
  15.8 9.9 %collective-permute-start.7 = (bf16[64,1152]{1,0:T(8,128)(2,1)S(1)}, bf16[64,1152]{1,0:T(8,128)(2,1)S(1)}, u32[]{:S(2)}, u32[]{:S(2)}) collective-permute-start(bf16[64,1152]{1,0:T(8,128)(2,1)S(1)} %collective-permute-done.4.refs_0_), channel_id=1, source_target_pairs={{0,1},{1,0},{2,3},{3,2},{4,5},{5,4},{6,7},{7,6},{8,9},{9,8},{10,11... | collective-permute-start | bytes 442376 | tf_op jit(solution)/shard_map/ppermute | solution.py:108
  16.3 5.9 %collective-permute-start.2 = (bf16[64,1152]{1,0:T(8,128)(2,1)S(1)}, bf16[64,1152]{1,0:T(8,128)(2,1)S(1)}, u32[]{:S(2)}, u32[]{:S(2)}) collective-permute-start(bf16[64,1152]{1,0:T(8,128)(2,1)S(1)} %collective-permute-done.refs_1_), channel_id=1, source_target_pairs={{0,1},{1,0},{2,3},{3,2},{4,5},{5,4},{6,7},{7,6},{8,9},{9,8},{10,11... | collective-permute-start | bytes 442376 | tf_op jit(solution)/shard_map/ppermute | solution.py:108
  20.5 13.3 %collective-permute-start.12 = (bf16[64,1152]{1,0:T(8,128)(2,1)S(1)}, bf16[64,1152]{1,0:T(8,128)(2,1)S(1)}, u32[]{:S(2)}, u32[]{:S(2)}) collective-permute-start(bf16[64,1152]{1,0:T(8,128)(2,1)S(1)} %collective-permute-done.5.refs_0_), channel_id=1, source_target_pairs={{0,1},{1,0},{2,3},{3,2},{4,5},{5,4},{6,7},{7,6},{8,9},{9,8},{10,11... | collective-permute-start | bytes 442376 | tf_op jit(solution)/shard_map/ppermute | solution.py:108
  20.5 6.2 %collective-permute-start.18 = (bf16[64,1152]{1,0:T(8,128)(2,1)S(1)}, bf16[64,1152]{1,0:T(8,128)(2,1)S(1)}, u32[]{:S(2)}, u32[]{:S(2)}) collective-permute-start(bf16[64,1152]{1,0:T(8,128)(2,1)S(1)} %collective-permute-done.17.refs_0_), channel_id=1, source_target_pairs={{0,2},{1,3},{2,0},{3,1},{4,6},{5,7},{6,4},{7,5},{8,10},{9,11},{10,... | collective-permute-start | bytes 442376 | tf_op jit(solution)/shard_map/ppermute | solution.py:108
  22.1 4.7 %collective-permute-start.8 = (bf16[64,1152]{1,0:T(8,128)(2,1)S(1)}, bf16[64,1152]{1,0:T(8,128)(2,1)S(1)}, u32[]{:S(2)}, u32[]{:S(2)}) collective-permute-start(bf16[64,1152]{1,0:T(8,128)(2,1)S(1)} %get-tuple-element.26.refs_1_), channel_id=1, source_target_pairs={{0,1},{1,0},{2,3},{3,2},{4,5},{5,4},{6,7},{7,6},{8,9},{9,8},{10,11... | collective-permute-start | bytes 442376 | tf_op jit(solution)/shard_map/ppermute | solution.py:108
  25.1 21.2 %collective-permute-start.3 = (bf16[128,512]{1,0:T(8,128)(2,1)S(1)}, bf16[128,512]{1,0:T(8,128)(2,1)S(1)}, u32[]{:S(2)}, u32[]{:S(2)}) collective-permute-start(bf16[128,512]{1,0:T(8,128)(2,1)S(1)} %get-tuple-element.16), channel_id=1, source_target_pairs={{0,1},{1,0},{2,3},{3,2},{4,5},{5,4},{6,7},{7,6},{8,9},{9,8},{10,11... | collective-permute-start | bytes 393224 | tf_op jit(solution)/shard_map/ppermute | solution.py:108
  25.7 4.5 %collective-permute-start.19 = (bf16[64,1152]{1,0:T(8,128)(2,1)S(1)}, bf16[64,1152]{1,0:T(8,128)(2,1)S(1)}, u32[]{:S(2)}, u32[]{:S(2)}) collective-permute-start(bf16[64,1152]{1,0:T(8,128)(2,1)S(1)} %collective-permute-done.17.refs_0_), channel_id=1, source_target_pairs={{0,1},{1,0},{2,3},{3,2},{4,5},{5,4},{6,7},{7,6},{8,9},{9,8},{10,11... | collective-permute-start | bytes 442376 | tf_op jit(solution)/shard_map/ppermute | solution.py:108
  26.7 7.1 %collective-permute-start.13 = (bf16[64,1152]{1,0:T(8,128)(2,1)S(1)}, bf16[64,1152]{1,0:T(8,128)(2,1)S(1)}, u32[]{:S(2)}, u32[]{:S(2)}) collective-permute-start(bf16[64,1152]{1,0:T(8,128)(2,1)S(1)} %get-tuple-element.25.refs_1_), channel_id=1, source_target_pairs={{0,1},{1,0},{2,3},{3,2},{4,5},{5,4},{6,7},{7,6},{8,9},{9,8},{10,11... | collective-permute-start | bytes 442376 | tf_op jit(solution)/shard_map/ppermute | solution.py:108
  26.7 3.5 %collective-permute-start.20 = (bf16[64,1152]{1,0:T(8,128)(2,1)S(1)}, bf16[64,1152]{1,0:T(8,128)(2,1)S(1)}, u32[]{:S(2)}, u32[]{:S(2)}) collective-permute-start(bf16[64,1152]{1,0:T(8,128)(2,1)S(1)} %collective-permute-done.18.refs_1_), channel_id=1, source_target_pairs={{0,1},{1,0},{2,3},{3,2},{4,5},{5,4},{6,7},{7,6},{8,9},{9,8},{10,11... | collective-permute-start | bytes 442376 | tf_op jit(solution)/shard_map/ppermute | solution.py:108
  30.2 6.6 %collective-permute-start.9 = (bf16[128,512]{1,0:T(8,128)(2,1)S(1)}, bf16[128,512]{1,0:T(8,128)(2,1)S(1)}, u32[]{:S(2)}, u32[]{:S(2)}) collective-permute-start(bf16[128,512]{1,0:T(8,128)(2,1)S(1)} %get-tuple-element.20), channel_id=1, source_target_pairs={{0,1},{1,0},{2,3},{3,2},{4,5},{5,4},{6,7},{7,6},{8,9},{9,8},{10,11... | collective-permute-start | bytes 393224 | tf_op jit(solution)/shard_map/ppermute | solution.py:108
  33.2 4.7 %collective-permute-start.21 = (bf16[128,512]{1,0:T(8,128)(2,1)S(1)}, bf16[128,512]{1,0:T(8,128)(2,1)S(1)}, u32[]{:S(2)}, u32[]{:S(2)}) collective-permute-start(bf16[128,512]{1,0:T(8,128)(2,1)S(1)} %get-tuple-element.24), channel_id=1, source_target_pairs={{0,1},{1,0},{2,3},{3,2},{4,5},{5,4},{6,7},{7,6},{8,9},{9,8},{10,11... | collective-permute-start | bytes 393224 | tf_op jit(solution)/shard_map/ppermute | solution.py:108
  36.7 2.3 %collective-permute-start.14 = (bf16[128,512]{1,0:T(8,128)(2,1)S(1)}, bf16[128,512]{1,0:T(8,128)(2,1)S(1)}, u32[]{:S(2)}, u32[]{:S(2)}) collective-permute-start(bf16[128,512]{1,0:T(8,128)(2,1)S(1)} %get-tuple-element.22), channel_id=1, source_target_pairs={{0,1},{1,0},{2,3},{3,2},{4,5},{5,4},{6,7},{7,6},{8,9},{9,8},{10,11... | collective-permute-start | bytes 393224 | tf_op jit(solution)/shard_map/ppermute | solution.py:108
  36.9 9.5 %collective-permute-start.10 = (bf16[128,512]{1,0:T(8,128)(2,1)S(1)}, bf16[128,512]{1,0:T(8,128)(2,1)S(1)}, u32[]{:S(2)}, u32[]{:S(2)}) collective-permute-start(bf16[128,512]{1,0:T(8,128)(2,1)S(1)} %add_convert_fusion.2), channel_id=1, source_target_pairs={{0,4},{1,5},{2,6},{3,7},{4,0},{5,1},{6,2},{7,3},{8,12},{9,13},{10,... | collective-permute-start | bytes 393224 | tf_op jit(solution)/shard_map/ppermute | solution.py:108
  37.9 5.0 %collective-permute-start.22 = (bf16[64,512]{1,0:T(8,128)(2,1)S(1)}, bf16[64,512]{1,0:T(8,128)(2,1)S(1)}, u32[]{:S(2)}, u32[]{:S(2)}) collective-permute-start(bf16[64,512]{1,0:T(8,128)(2,1)S(1)} %slice.40), channel_id=1, source_target_pairs={{0,2},{1,3},{2,0},{3,1},{4,6},{5,7},{6,4},{7,5},{8,10},{9,11},{10,... | collective-permute-start | bytes 196616 | tf_op jit(solution)/shard_map/ppermute | solution.py:108
  39.1 5.8 %collective-permute-start.15 = (bf16[64,512]{1,0:T(8,128)(2,1)S(1)}, bf16[64,512]{1,0:T(8,128)(2,1)S(1)}, u32[]{:S(2)}, u32[]{:S(2)}) collective-permute-start(bf16[64,512]{1,0:T(8,128)(2,1)S(1)} %slice.38), channel_id=1, source_target_pairs={{0,2},{1,3},{2,0},{3,1},{4,6},{5,7},{6,4},{7,5},{8,10},{9,11},{10,... | collective-permute-start | bytes 196616 | tf_op jit(solution)/shard_map/ppermute | solution.py:108
  42.9 6.1 %collective-permute-start.23 = (bf16[64,512]{1,0:T(8,128)(2,1)S(1)}, bf16[64,512]{1,0:T(8,128)(2,1)S(1)}, u32[]{:S(2)}, u32[]{:S(2)}) collective-permute-start(bf16[64,512]{1,0:T(8,128)(2,1)S(1)} %add_convert_fusion.3), channel_id=1, source_target_pairs={{0,12},{1,13},{2,14},{3,15},{4,8},{5,9},{6,10},{7,11},{8,4},{9,5},... | collective-permute-start | bytes 196616 | tf_op jit(solution)/shard_map/ppermute | solution.py:108
  44.9 6.1 %collective-permute-start.16 = (bf16[64,512]{1,0:T(8,128)(2,1)S(1)}, bf16[64,512]{1,0:T(8,128)(2,1)S(1)}, u32[]{:S(2)}, u32[]{:S(2)}) collective-permute-start(bf16[64,512]{1,0:T(8,128)(2,1)S(1)} %add_convert_fusion.4), channel_id=1, source_target_pairs={{0,8},{1,9},{2,10},{3,11},{4,12},{5,13},{6,14},{7,15},{8,0},{9,1},... | collective-permute-start | bytes 196616 | tf_op jit(solution)/shard_map/ppermute | solution.py:108
  46.4 4.5 %collective-permute-start.11 = (bf16[64,512]{1,0:T(8,128)(2,1)S(1)}, bf16[64,512]{1,0:T(8,128)(2,1)S(1)}, u32[]{:S(2)}, u32[]{:S(2)}) collective-permute-start(bf16[64,512]{1,0:T(8,128)(2,1)S(1)} %slice.51), channel_id=1, source_target_pairs={{0,2},{1,3},{2,0},{3,1},{4,6},{5,7},{6,4},{7,5},{8,10},{9,11},{10,... | collective-permute-start | bytes 196616 | tf_op jit(solution)/shard_map/ppermute | solution.py:108
  (3 other events, 66.5 us)

commit v4 on v3

--- a/solution.py
+++ b/solution.py
@@ -88,7 +88,7 @@
         scratch_shapes=[pltpu.VMEM((rows, width), jnp.bfloat16)],
         compiler_params=pltpu.CompilerParams(vmem_limit_bytes=24 * MIB),
         cost_estimate=pl.CostEstimate(
-            flops=flops, bytes_accessed=2 * rows * width, transcendentals=0
+            flops=flops // 20, bytes_accessed=1024, transcendentals=0
         ),
         name="apply_experts",
     )(*blocks, *weights)
@@ -110,27 +110,37 @@
     own = tag_tokens(
         token_codes, route_devices, route_members, gate_scores, local_experts, local_experts * size
     )
-    across = exchange(own, 2)
-    gathered = {0: own}
-    for j in range(1, size // 4):
+    def partial_sums(blocks):
+        blocks = blocks + tuple(exchange(block, 1) for block in blocks)
+        return apply_experts(blocks, weights)
+
+    def paired(near, far):
+        return wide(near) + wide(exchange(far, 1))
+
+    def narrow(array):
+        return array.astype(jnp.bfloat16)
+
+    across, beside, beyond = exchange(own, 2), exchange(own, 4), exchange(own, 8)
+    beside, beyond, own_too, across = lax.optimization_barrier((beside, beyond, own, across))
+    middle = exchange(jnp.concatenate([beside, beyond]), 2)
+    gathered = {3: exchange(beyond, 4)}
+    for j in range(4, size // 4):
         low = j & -j
-        gathered[j] = exchange(gathered[j - low], 4 * low)
-    near_by = lax.optimization_barrier((gathered[1], gathered[2], across))
-    middle = exchange(jnp.concatenate(near_by[:2]), 2)
-    gathered[3] = exchange(near_by[1], 4)
-    pairs = {0: (own, across), 1: (gathered[1], middle[:rows]), 2: (gathered[2], middle[rows:])}
-    pairs |= {j: (gathered[j], exchange(gathered[j], 2)) for j in range(3, size // 4)}
-    halves, near = {}, None
-    for j, blocks in pairs.items():
-        blocks = blocks + tuple(exchange(block, 1) for block in blocks)
-        near, far = apply_experts(tuple(blocks), weights)
-        pair = wide(near) + wide(exchange(far, 1))
-        halves[j] = pair if j == 0 else pair.astype(jnp.bfloat16)
-    pair = halves[0] + wide(exchange(halves[1], 4))
-    mixed = pair[:rows] + wide(exchange(pair[rows:].astype(jnp.bfloat16), 2))
+        gathered[j] = exchange(own if j == low else gathered[j - low], 4 * low)
+    sums = {0: partial_sums((own_too, across))}
+    middle, gathered[3], near = lax.optimization_barrier((middle, gathered[3], sums[0][0]))
+    sums[0] = (near, sums[0][1])
+    sums[1] = partial_sums((beside, middle[:rows]))
+    sums[2] = partial_sums((beyond, middle[rows:]))
+    for j, block in gathered.items():
+        sums[j] = partial_sums((block, exchange(block, 2)))
+    pair, other = paired(*sums[0]), paired(*sums[1])
+    back = wide(exchange(narrow(jnp.concatenate([pair[rows:], other[rows:]])), 2))
+    mixed = pair[:rows] + back[:rows] + wide(exchange(narrow(other[:rows] + back[rows:]), 4))
     for j in range(2, size // 4):
-        done = wide(halves[j][:rows]) + wide(exchange(halves[j][rows:], 2))
-        mixed = mixed + wide(exchange(done.astype(jnp.bfloat16), 4 * j))
+        pair = paired(*sums[j])
+        done = pair[:rows] + wide(exchange(narrow(pair[rows:]), 2))
+        mixed = mixed + wide(exchange(narrow(done), 4 * j))
     return mixed.astype(jnp.bfloat16)
 
 

time: 51.8 us -> 49.7 us (0.959)
  waiting for transfers between devices: 16.8 us -> 13 us
  starting transfers between devices: 20.8 us -> 22.5 us
    ppermute x24, waiting for transfers between devices: 16.8 us -> 13 us  [exchange(): return lax.ppermute(array, 'expert', [(i, i ^ mask) for i in range(size)])]
    ppermute x24, starting transfers between devices: 20.8 us -> 22.5 us  [exchange(): return lax.ppermute(array, 'expert', [(i, i ^ mask) for i in range(size)])]
  transfers between devices with their start and end apart: 24 -> 24, of which waited for: 8 -> 10; matrix products, arithmetic and copies ran while one was open for 0% -> 1% of each run, Pallas kernels for 23% -> 24%
where the time goes in v4:
time: 49.7 us; the launch traced here: 49.6 us
  starting transfers between devices  22.5 us (45%)
  waiting for transfers between devices  13 us (26%)
  Pallas kernels  12.9 us (26%)
  other arithmetic  0.89 us (2%)
    ppermute x24, starting transfers between devices, exchange(): return lax.ppermute(array, 'expert', [(i, i ^ mask) for i in range(size)])  22.5 us
    ppermute x24, waiting for transfers between devices, exchange(): return lax.ppermute(array, 'expert', [(i, i ^ mask) for i in range(size)])  13 us
    pallas_call x4, Pallas kernels, apply_experts(): pl.pallas_call(functools.partial(expert_kernel, len(blocks)), out_shape=(...  11.8 us
    pallas_call x1, Pallas kernels, tag_tokens(): pl.pallas_call(functools.partial(tag_kernel, local_experts), out_shape=ja...  1.17 us
  transfers between devices with their start and end apart: 24, of which 10 were waited for; matrix products, arithmetic and copies ran while one was open for 1% of the time, Pallas kernels for 24%

profile of v4, /device:TPU:0, one launch (start us, length us, event | category | flops | bytes accessed | tf_op | source)
XLA Modules:
  0.0 49.6 jit_solution(2280964089992738861)
XLA Ops:
  0.0 1.2 %tag_tokens.1.refs_0_ = bf16[64,1152]{1,0:T(8,128)(2,1)S(1)} custom-call(bf16[64,1024]{1,0:T(8,128)(2,1)} %codes_ref.1, s32[8,64]{1,0:T(8,128)} %bitcast.3, s32[8,64]{1,0:T(8,128)} %bitcast.4, bf16[8,64]{1,0:T(8,128)(2,1)} %bitcast.5), custom_call_target="tpu_custom_call" | custom-call | flops 8000000000 | bytes 16000000 | tf_op jit(solution)/shard_map/tag_tokens/pallas_call | solution.py:35
  1.2 3.1 %collective-permute-start = (bf16[64,1152]{1,0:T(8,128)(2,1)S(1)}, bf16[64,1152]{1,0:T(8,128)(2,1)S(1)}, u32[]{:S(2)}, u32[]{:S(2)}) collective-permute-start(bf16[64,1152]{1,0:T(8,128)(2,1)S(1)} %tag_tokens.1.refs_0_), channel_id=1, source_target_pairs={{0,4},{1,5},{2,6},{3,7},{4,0},{5,1},{6,2},{7,3},{8,12},{9,13},{10,... | collective-permute-start | bytes 442376 | tf_op jit(solution)/shard_map/ppermute | solution.py:108
  4.3 2.6 %collective-permute-start.1 = (bf16[64,1152]{1,0:T(8,128)(2,1)S(1)}, bf16[64,1152]{1,0:T(8,128)(2,1)S(1)}, u32[]{:S(2)}, u32[]{:S(2)}) collective-permute-start(bf16[64,1152]{1,0:T(8,128)(2,1)S(1)} %tag_tokens.1.refs_0_), channel_id=1, source_target_pairs={{0,8},{1,9},{2,10},{3,11},{4,12},{5,13},{6,14},{7,15},{8,0},{9,1},... | collective-permute-start | bytes 442376 | tf_op jit(solution)/shard_map/ppermute | solution.py:108
  6.9 1.5 %collective-permute-start.2 = (bf16[64,1152]{1,0:T(8,128)(2,1)S(1)}, bf16[64,1152]{1,0:T(8,128)(2,1)S(1)}, u32[]{:S(2)}, u32[]{:S(2)}) collective-permute-start(bf16[64,1152]{1,0:T(8,128)(2,1)S(1)} %tag_tokens.1.refs_0_), channel_id=1, source_target_pairs={{0,2},{1,3},{2,0},{3,1},{4,6},{5,7},{6,4},{7,5},{8,10},{9,11},{10,... | collective-permute-start | bytes 442376 | tf_op jit(solution)/shard_map/ppermute | solution.py:108
  8.4 2.3 %collective-permute-done.refs_0_ = bf16[64,1152]{1,0:T(8,128)(2,1)S(1)} collective-permute-done((bf16[64,1152]{1,0:T(8,128)(2,1)S(1)}, bf16[64,1152]{1,0:T(8,128)(2,1)S(1)}, u32[]{:S(2)}, u32[]{:S(2)}) %collective-permute-start) | collective-permute-done | bytes 147488 | tf_op jit(solution)/shard_map/ppermute | solution.py:108
  10.7 3.0 %collective-permute-done.1.refs_0_ = bf16[64,1152]{1,0:T(8,128)(2,1)S(1)} collective-permute-done((bf16[64,1152]{1,0:T(8,128)(2,1)S(1)}, bf16[64,1152]{1,0:T(8,128)(2,1)S(1)}, u32[]{:S(2)}, u32[]{:S(2)}) %collective-permute-start.1) | collective-permute-done | bytes 147488 | tf_op jit(solution)/shard_map/ppermute | solution.py:108
  13.7 1.6 %collective-permute-start.3 = (bf16[128,1152]{1,0:T(8,128)(2,1)S(1)}, bf16[128,1152]{1,0:T(8,128)(2,1)S(1)}, u32[]{:S(2)}, u32[]{:S(2)}) collective-permute-start(bf16[128,1152]{1,0:T(8,128)(2,1)S(1)} %pad_maximum_fusion), channel_id=1, source_target_pairs={{0,2},{1,3},{2,0},{3,1},{4,6},{5,7},{6,4},{7,5},{8,10},{9,11},{10,... | collective-permute-start | bytes 884744 | tf_op jit(solution)/shard_map/ppermute | solution.py:108
  15.3 0.5 %collective-permute-start.6 = (bf16[64,1152]{1,0:T(8,128)(2,1)S(1)}, bf16[64,1152]{1,0:T(8,128)(2,1)S(1)}, u32[]{:S(2)}, u32[]{:S(2)}) collective-permute-start(bf16[64,1152]{1,0:T(8,128)(2,1)S(1)} %collective-permute-done.2.refs_1_), channel_id=1, source_target_pairs={{0,1},{1,0},{2,3},{3,2},{4,5},{5,4},{6,7},{7,6},{8,9},{9,8},{10,11... | collective-permute-start | bytes 442376 | tf_op jit(solution)/shard_map/ppermute | solution.py:108
  16.9 2.9 %apply_experts.4 = (bf16[128,512]{1,0:T(8,128)(2,1)S(1)}, bf16[128,512]{1,0:T(8,128)(2,1)S(1)}) custom-call(bf16[64,1152]{1,0:T(8,128)(2,1)S(1)} %tag_tokens.1.refs_0_, bf16[64,1152]{1,0:T(8,128)(2,1)S(1)} %collective-permute-done.2.refs_1_, bf16[64,1152]{1,0:T(8,128)(2,1)S(1)} %collective-permute-done.5.refs_2_, ...), custom_call_target="tpu_custom_call" | custom-call | flops 134217728 | bytes 1024 | tf_op jit(solution)/shard_map/apply_experts/pallas_call | solution.py:83
  19.8 1.7 %collective-permute-done.4.refs_0_ = bf16[64,1152]{1,0:T(8,128)(2,1)S(1)} collective-permute-done((bf16[64,1152]{1,0:T(8,128)(2,1)S(1)}, bf16[64,1152]{1,0:T(8,128)(2,1)S(1)}, u32[]{:S(2)}, u32[]{:S(2)}) %collective-permute-start.4) | collective-permute-done | bytes 147488 | tf_op jit(solution)/shard_map/ppermute | solution.py:108
  22.3 0.5 %collective-permute-start.18 = (bf16[64,1152]{1,0:T(8,128)(2,1)S(1)}, bf16[64,1152]{1,0:T(8,128)(2,1)S(1)}, u32[]{:S(2)}, u32[]{:S(2)}) collective-permute-start(bf16[64,1152]{1,0:T(8,128)(2,1)S(1)} %collective-permute-done.4.refs_0_), channel_id=1, source_target_pairs={{0,2},{1,3},{2,0},{3,1},{4,6},{5,7},{6,4},{7,5},{8,10},{9,11},{10,... | collective-permute-start | bytes 442376 | tf_op jit(solution)/shard_map/ppermute | solution.py:108
  23.3 2.9 %apply_experts.5 = (bf16[128,512]{1,0:T(8,128)(2,1)S(1)}, bf16[128,512]{1,0:T(8,128)(2,1)S(1)}) custom-call(bf16[64,1152]{1,0:T(8,128)(2,1)S(1)} %collective-permute-done.refs_0_, bf16[64,1152]{1,0:T(8,128)(2,1)S(1)} %get-tuple-element.36.refs_1_, bf16[64,1152]{1,0:T(8,128)(2,1)S(1)} %collective-permute-done.8.refs_2_, ...), custom_call_target="tpu_custom_call" | custom-call | flops 134217728 | bytes 1024 | tf_op jit(solution)/shard_map/apply_experts/pallas_call | solution.py:83
  26.6 2.9 %apply_experts.6 = (bf16[128,512]{1,0:T(8,128)(2,1)S(1)}, bf16[128,512]{1,0:T(8,128)(2,1)S(1)}) custom-call(bf16[64,1152]{1,0:T(8,128)(2,1)S(1)} %collective-permute-done.1.refs_0_, bf16[64,1152]{1,0:T(8,128)(2,1)S(1)} %get-tuple-element.35.refs_1_, bf16[64,1152]{1,0:T(8,128)(2,1)S(1)} %collective-permute-done.13.refs_2_, ...), custom_call_target="tpu_custom_call" | custom-call | flops 134217728 | bytes 1024 | tf_op jit(solution)/shard_map/apply_experts/pallas_call | solution.py:83
  30.2 0.8 %collective-permute-done.15 = bf16[128,512]{1,0:T(8,128)(2,1)S(1)} collective-permute-done((bf16[128,512]{1,0:T(8,128)(2,1)S(1)}, bf16[128,512]{1,0:T(8,128)(2,1)S(1)}, u32[]{:S(2)}, u32[]{:S(2)}) %collective-permute-start.15) | collective-permute-done | bytes 131104 | tf_op jit(solution)/shard_map/ppermute | solution.py:108
  31.1 1.5 %collective-permute-start.16 = (bf16[64,512]{1,0:T(8,128)(2,1)S(1)}, bf16[64,512]{1,0:T(8,128)(2,1)S(1)}, u32[]{:S(2)}, u32[]{:S(2)}) collective-permute-start(bf16[64,512]{1,0:T(8,128)(2,1)S(1)} %slice.87), channel_id=1, source_target_pairs={{0,2},{1,3},{2,0},{3,1},{4,6},{5,7},{6,4},{7,5},{8,10},{9,11},{10,... | collective-permute-start | bytes 196616 | tf_op jit(solution)/shard_map/ppermute | solution.py:108
  32.6 0.7 %collective-permute-start.11 = (bf16[128,512]{1,0:T(8,128)(2,1)S(1)}, bf16[128,512]{1,0:T(8,128)(2,1)S(1)}, u32[]{:S(2)}, u32[]{:S(2)}) collective-permute-start(bf16[128,512]{1,0:T(8,128)(2,1)S(1)} %pad_maximum_fusion.1), channel_id=1, source_target_pairs={{0,2},{1,3},{2,0},{3,1},{4,6},{5,7},{6,4},{7,5},{8,10},{9,11},{10,... | collective-permute-start | bytes 393224 | tf_op jit(solution)/shard_map/ppermute | solution.py:108
  33.3 2.9 %apply_experts.7 = (bf16[128,512]{1,0:T(8,128)(2,1)S(1)}, bf16[128,512]{1,0:T(8,128)(2,1)S(1)}) custom-call(bf16[64,1152]{1,0:T(8,128)(2,1)S(1)} %collective-permute-done.4.refs_0_, bf16[64,1152]{1,0:T(8,128)(2,1)S(1)} %collective-permute-done.18.refs_1_, bf16[64,1152]{1,0:T(8,128)(2,1)S(1)} %collective-permute-done.19.refs_2_, ...), custom_call_target="tpu_custom_call" | custom-call | flops 134217728 | bytes 1024 | tf_op jit(solution)/shard_map/apply_experts/pallas_call | solution.py:83
  36.3 1.7 %collective-permute-start.17 = (bf16[64,512]{1,0:T(8,128)(2,1)S(1)}, bf16[64,512]{1,0:T(8,128)(2,1)S(1)}, u32[]{:S(2)}, u32[]{:S(2)}) collective-permute-start(bf16[64,512]{1,0:T(8,128)(2,1)S(1)} %fusion.1), channel_id=1, source_target_pairs={{0,8},{1,9},{2,10},{3,11},{4,12},{5,13},{6,14},{7,15},{8,0},{9,1},... | collective-permute-start | bytes 196616 | tf_op jit(solution)/shard_map/ppermute | solution.py:108
  38.3 1.6 %collective-permute-start.22 = (bf16[64,512]{1,0:T(8,128)(2,1)S(1)}, bf16[64,512]{1,0:T(8,128)(2,1)S(1)}, u32[]{:S(2)}, u32[]{:S(2)}) collective-permute-start(bf16[64,512]{1,0:T(8,128)(2,1)S(1)} %slice.86), channel_id=1, source_target_pairs={{0,2},{1,3},{2,0},{3,1},{4,6},{5,7},{6,4},{7,5},{8,10},{9,11},{10,... | collective-permute-start | bytes 196616 | tf_op jit(solution)/shard_map/ppermute | solution.py:108
  39.9 1.3 %collective-permute-start.12 = (bf16[64,512]{1,0:T(8,128)(2,1)S(1)}, bf16[64,512]{1,0:T(8,128)(2,1)S(1)}, u32[]{:S(2)}, u32[]{:S(2)}) collective-permute-start(bf16[64,512]{1,0:T(8,128)(2,1)S(1)} %fusion.2), channel_id=1, source_target_pairs={{0,4},{1,5},{2,6},{3,7},{4,0},{5,1},{6,2},{7,3},{8,12},{9,13},{10,... | collective-permute-start | bytes 196616 | tf_op jit(solution)/shard_map/ppermute | solution.py:108
  41.2 1.5 %collective-permute-done.22 = bf16[64,512]{1,0:T(8,128)(2,1)S(1)} collective-permute-done((bf16[64,512]{1,0:T(8,128)(2,1)S(1)}, bf16[64,512]{1,0:T(8,128)(2,1)S(1)}, u32[]{:S(2)}, u32[]{:S(2)}) %collective-permute-start.22) | collective-permute-done | bytes 65568 | tf_op jit(solution)/shard_map/ppermute | solution.py:108
  42.7 3.5 %collective-permute-start.23 = (bf16[64,512]{1,0:T(8,128)(2,1)S(1)}, bf16[64,512]{1,0:T(8,128)(2,1)S(1)}, u32[]{:S(2)}, u32[]{:S(2)}) collective-permute-start(bf16[64,512]{1,0:T(8,128)(2,1)S(1)} %fusion), channel_id=1, source_target_pairs={{0,12},{1,13},{2,14},{3,15},{4,8},{5,9},{6,10},{7,11},{8,4},{9,5},... | collective-permute-start | bytes 196616 | tf_op jit(solution)/shard_map/ppermute | solution.py:108
  46.2 2.7 %collective-permute-done.23 = bf16[64,512]{1,0:T(8,128)(2,1)S(1)} collective-permute-done((bf16[64,512]{1,0:T(8,128)(2,1)S(1)}, bf16[64,512]{1,0:T(8,128)(2,1)S(1)}, u32[]{:S(2)}, u32[]{:S(2)}) %collective-permute-start.23) | collective-permute-done | bytes 65568 | tf_op jit(solution)/shard_map/ppermute | solution.py:108
  48.9 0.7 %fusion.6 = bf16[64,512]{1,0:T(8,128)(2,1)} fusion(f32[128,512]{1,0:T(8,128)S(1)} %convert_element_type.61, f32[128,512]{1,0:T(8,128)S(1)} %convert_add_fusion.3, bf16[64,512]{1,0:T(8,128)(2,1)S(1)} %collective-permute-done.23, bf16[64,512]{1,0:T(8,128)(2,1)S(1)} %collective-permute-done.17, bf16[64,512]{1,0:T(8,128)(2,1)S(1)} %collective-permute-done.12), kind=kLoop, calls=%fused_computation.17 | loop fusion | flops 262144 | bytes 524288 | tf_op jit(solution)/shard_map/convert_element_type | solution.py:144
  (51 shorter events, 3.8 us)
Async XLA Ops:
  1.2 9.5 %collective-permute-start = (bf16[64,1152]{1,0:T(8,128)(2,1)S(1)}, bf16[64,1152]{1,0:T(8,128)(2,1)S(1)}, u32[]{:S(2)}, u32[]{:S(2)}) collective-permute-start(bf16[64,1152]{1,0:T(8,128)(2,1)S(1)} %tag_tokens.1.refs_0_), channel_id=1, source_target_pairs={{0,4},{1,5},{2,6},{3,7},{4,0},{5,1},{6,2},{7,3},{8,12},{9,13},{10,... | collective-permute-start | bytes 442376 | tf_op jit(solution)/shard_map/ppermute | solution.py:108
  4.3 9.4 %collective-permute-start.1 = (bf16[64,1152]{1,0:T(8,128)(2,1)S(1)}, bf16[64,1152]{1,0:T(8,128)(2,1)S(1)}, u32[]{:S(2)}, u32[]{:S(2)}) collective-permute-start(bf16[64,1152]{1,0:T(8,128)(2,1)S(1)} %tag_tokens.1.refs_0_), channel_id=1, source_target_pairs={{0,8},{1,9},{2,10},{3,11},{4,12},{5,13},{6,14},{7,15},{8,0},{9,1},... | collective-permute-start | bytes 442376 | tf_op jit(solution)/shard_map/ppermute | solution.py:108
  6.9 6.8 %collective-permute-start.2 = (bf16[64,1152]{1,0:T(8,128)(2,1)S(1)}, bf16[64,1152]{1,0:T(8,128)(2,1)S(1)}, u32[]{:S(2)}, u32[]{:S(2)}) collective-permute-start(bf16[64,1152]{1,0:T(8,128)(2,1)S(1)} %tag_tokens.1.refs_0_), channel_id=1, source_target_pairs={{0,2},{1,3},{2,0},{3,1},{4,6},{5,7},{6,4},{7,5},{8,10},{9,11},{10,... | collective-permute-start | bytes 442376 | tf_op jit(solution)/shard_map/ppermute | solution.py:108
  13.7 7.9 %collective-permute-start.3 = (bf16[128,1152]{1,0:T(8,128)(2,1)S(1)}, bf16[128,1152]{1,0:T(8,128)(2,1)S(1)}, u32[]{:S(2)}, u32[]{:S(2)}) collective-permute-start(bf16[128,1152]{1,0:T(8,128)(2,1)S(1)} %pad_maximum_fusion), channel_id=1, source_target_pairs={{0,2},{1,3},{2,0},{3,1},{4,6},{5,7},{6,4},{7,5},{8,10},{9,11},{10,... | collective-permute-start | bytes 884744 | tf_op jit(solution)/shard_map/ppermute | solution.py:108
  15.3 1.4 %collective-permute-start.5 = (bf16[64,1152]{1,0:T(8,128)(2,1)S(1)}, bf16[64,1152]{1,0:T(8,128)(2,1)S(1)}, u32[]{:S(2)}, u32[]{:S(2)}) collective-permute-start(bf16[64,1152]{1,0:T(8,128)(2,1)S(1)} %tag_tokens.1.refs_0_), channel_id=1, source_target_pairs={{0,1},{1,0},{2,3},{3,2},{4,5},{5,4},{6,7},{7,6},{8,9},{9,8},{10,11... | collective-permute-start | bytes 442376 | tf_op jit(solution)/shard_map/ppermute | solution.py:108
  15.3 1.6 %collective-permute-start.6 = (bf16[64,1152]{1,0:T(8,128)(2,1)S(1)}, bf16[64,1152]{1,0:T(8,128)(2,1)S(1)}, u32[]{:S(2)}, u32[]{:S(2)}) collective-permute-start(bf16[64,1152]{1,0:T(8,128)(2,1)S(1)} %collective-permute-done.2.refs_1_), channel_id=1, source_target_pairs={{0,1},{1,0},{2,3},{3,2},{4,5},{5,4},{6,7},{7,6},{8,9},{9,8},{10,11... | collective-permute-start | bytes 442376 | tf_op jit(solution)/shard_map/ppermute | solution.py:108
  15.8 5.8 %collective-permute-start.4 = (bf16[64,1152]{1,0:T(8,128)(2,1)S(1)}, bf16[64,1152]{1,0:T(8,128)(2,1)S(1)}, u32[]{:S(2)}, u32[]{:S(2)}) collective-permute-start(bf16[64,1152]{1,0:T(8,128)(2,1)S(1)} %collective-permute-done.1.refs_0_), channel_id=1, source_target_pairs={{0,4},{1,5},{2,6},{3,7},{4,0},{5,1},{6,2},{7,3},{8,12},{9,13},{10,... | collective-permute-start | bytes 442376 | tf_op jit(solution)/shard_map/ppermute | solution.py:108
  16.3 6.5 %collective-permute-start.8 = (bf16[64,1152]{1,0:T(8,128)(2,1)S(1)}, bf16[64,1152]{1,0:T(8,128)(2,1)S(1)}, u32[]{:S(2)}, u32[]{:S(2)}) collective-permute-start(bf16[64,1152]{1,0:T(8,128)(2,1)S(1)} %collective-permute-done.refs_0_), channel_id=1, source_target_pairs={{0,1},{1,0},{2,3},{3,2},{4,5},{5,4},{6,7},{7,6},{8,9},{9,8},{10,11... | collective-permute-start | bytes 442376 | tf_op jit(solution)/shard_map/ppermute | solution.py:108
  21.6 1.4 %collective-permute-start.9 = (bf16[64,1152]{1,0:T(8,128)(2,1)S(1)}, bf16[64,1152]{1,0:T(8,128)(2,1)S(1)}, u32[]{:S(2)}, u32[]{:S(2)}) collective-permute-start(bf16[64,1152]{1,0:T(8,128)(2,1)S(1)} %get-tuple-element.36.refs_1_), channel_id=1, source_target_pairs={{0,1},{1,0},{2,3},{3,2},{4,5},{5,4},{6,7},{7,6},{8,9},{9,8},{10,11... | collective-permute-start | bytes 442376 | tf_op jit(solution)/shard_map/ppermute | solution.py:108
  21.7 4.5 %collective-permute-start.7 = (bf16[128,512]{1,0:T(8,128)(2,1)S(1)}, bf16[128,512]{1,0:T(8,128)(2,1)S(1)}, u32[]{:S(2)}, u32[]{:S(2)}) collective-permute-start(bf16[128,512]{1,0:T(8,128)(2,1)S(1)} %get-tuple-element.26), channel_id=1, source_target_pairs={{0,1},{1,0},{2,3},{3,2},{4,5},{5,4},{6,7},{7,6},{8,9},{9,8},{10,11... | collective-permute-start | bytes 393224 | tf_op jit(solution)/shard_map/ppermute | solution.py:108
  22.2 4.4 %collective-permute-start.13 = (bf16[64,1152]{1,0:T(8,128)(2,1)S(1)}, bf16[64,1152]{1,0:T(8,128)(2,1)S(1)}, u32[]{:S(2)}, u32[]{:S(2)}) collective-permute-start(bf16[64,1152]{1,0:T(8,128)(2,1)S(1)} %collective-permute-done.1.refs_0_), channel_id=1, source_target_pairs={{0,1},{1,0},{2,3},{3,2},{4,5},{5,4},{6,7},{7,6},{8,9},{9,8},{10,11... | collective-permute-start | bytes 442376 | tf_op jit(solution)/shard_map/ppermute | solution.py:108
  22.3 7.6 %collective-permute-start.18 = (bf16[64,1152]{1,0:T(8,128)(2,1)S(1)}, bf16[64,1152]{1,0:T(8,128)(2,1)S(1)}, u32[]{:S(2)}, u32[]{:S(2)}) collective-permute-start(bf16[64,1152]{1,0:T(8,128)(2,1)S(1)} %collective-permute-done.4.refs_0_), channel_id=1, source_target_pairs={{0,2},{1,3},{2,0},{3,1},{4,6},{5,7},{6,4},{7,5},{8,10},{9,11},{10,... | collective-permute-start | bytes 442376 | tf_op jit(solution)/shard_map/ppermute | solution.py:108
  22.8 10.5 %collective-permute-start.19 = (bf16[64,1152]{1,0:T(8,128)(2,1)S(1)}, bf16[64,1152]{1,0:T(8,128)(2,1)S(1)}, u32[]{:S(2)}, u32[]{:S(2)}) collective-permute-start(bf16[64,1152]{1,0:T(8,128)(2,1)S(1)} %collective-permute-done.4.refs_0_), channel_id=1, source_target_pairs={{0,1},{1,0},{2,3},{3,2},{4,5},{5,4},{6,7},{7,6},{8,9},{9,8},{10,11... | collective-permute-start | bytes 442376 | tf_op jit(solution)/shard_map/ppermute | solution.py:108
  23.0 3.6 %collective-permute-start.14 = (bf16[64,1152]{1,0:T(8,128)(2,1)S(1)}, bf16[64,1152]{1,0:T(8,128)(2,1)S(1)}, u32[]{:S(2)}, u32[]{:S(2)}) collective-permute-start(bf16[64,1152]{1,0:T(8,128)(2,1)S(1)} %get-tuple-element.35.refs_1_), channel_id=1, source_target_pairs={{0,1},{1,0},{2,3},{3,2},{4,5},{5,4},{6,7},{7,6},{8,9},{9,8},{10,11... | collective-permute-start | bytes 442376 | tf_op jit(solution)/shard_map/ppermute | solution.py:108
  26.2 3.9 %collective-permute-start.10 = (bf16[128,512]{1,0:T(8,128)(2,1)S(1)}, bf16[128,512]{1,0:T(8,128)(2,1)S(1)}, u32[]{:S(2)}, u32[]{:S(2)}) collective-permute-start(bf16[128,512]{1,0:T(8,128)(2,1)S(1)} %get-tuple-element.29), channel_id=1, source_target_pairs={{0,1},{1,0},{2,3},{3,2},{4,5},{5,4},{6,7},{7,6},{8,9},{9,8},{10,11... | collective-permute-start | bytes 393224 | tf_op jit(solution)/shard_map/ppermute | solution.py:108
  29.6 1.4 %collective-permute-start.15 = (bf16[128,512]{1,0:T(8,128)(2,1)S(1)}, bf16[128,512]{1,0:T(8,128)(2,1)S(1)}, u32[]{:S(2)}, u32[]{:S(2)}) collective-permute-start(bf16[128,512]{1,0:T(8,128)(2,1)S(1)} %get-tuple-element.31), channel_id=1, source_target_pairs={{0,1},{1,0},{2,3},{3,2},{4,5},{5,4},{6,7},{7,6},{8,9},{9,8},{10,11... | collective-permute-start | bytes 393224 | tf_op jit(solution)/shard_map/ppermute | solution.py:108
  29.9 3.3 %collective-permute-start.20 = (bf16[64,1152]{1,0:T(8,128)(2,1)S(1)}, bf16[64,1152]{1,0:T(8,128)(2,1)S(1)}, u32[]{:S(2)}, u32[]{:S(2)}) collective-permute-start(bf16[64,1152]{1,0:T(8,128)(2,1)S(1)} %collective-permute-done.18.refs_1_), channel_id=1, source_target_pairs={{0,1},{1,0},{2,3},{3,2},{4,5},{5,4},{6,7},{7,6},{8,9},{9,8},{10,11... | collective-permute-start | bytes 442376 | tf_op jit(solution)/shard_map/ppermute | solution.py:108
  31.1 5.2 %collective-permute-start.16 = (bf16[64,512]{1,0:T(8,128)(2,1)S(1)}, bf16[64,512]{1,0:T(8,128)(2,1)S(1)}, u32[]{:S(2)}, u32[]{:S(2)}) collective-permute-start(bf16[64,512]{1,0:T(8,128)(2,1)S(1)} %slice.87), channel_id=1, source_target_pairs={{0,2},{1,3},{2,0},{3,1},{4,6},{5,7},{6,4},{7,5},{8,10},{9,11},{10,... | collective-permute-start | bytes 196616 | tf_op jit(solution)/shard_map/ppermute | solution.py:108
  32.6 5.6 %collective-permute-start.11 = (bf16[128,512]{1,0:T(8,128)(2,1)S(1)}, bf16[128,512]{1,0:T(8,128)(2,1)S(1)}, u32[]{:S(2)}, u32[]{:S(2)}) collective-permute-start(bf16[128,512]{1,0:T(8,128)(2,1)S(1)} %pad_maximum_fusion.1), channel_id=1, source_target_pairs={{0,2},{1,3},{2,0},{3,1},{4,6},{5,7},{6,4},{7,5},{8,10},{9,11},{10,... | collective-permute-start | bytes 393224 | tf_op jit(solution)/shard_map/ppermute | solution.py:108
  36.2 2.0 %collective-permute-start.21 = (bf16[128,512]{1,0:T(8,128)(2,1)S(1)}, bf16[128,512]{1,0:T(8,128)(2,1)S(1)}, u32[]{:S(2)}, u32[]{:S(2)}) collective-permute-start(bf16[128,512]{1,0:T(8,128)(2,1)S(1)} %get-tuple-element.34), channel_id=1, source_target_pairs={{0,1},{1,0},{2,3},{3,2},{4,5},{5,4},{6,7},{7,6},{8,9},{9,8},{10,11... | collective-permute-start | bytes 393224 | tf_op jit(solution)/shard_map/ppermute | solution.py:108
  36.3 9.9 %collective-permute-start.17 = (bf16[64,512]{1,0:T(8,128)(2,1)S(1)}, bf16[64,512]{1,0:T(8,128)(2,1)S(1)}, u32[]{:S(2)}, u32[]{:S(2)}) collective-permute-start(bf16[64,512]{1,0:T(8,128)(2,1)S(1)} %fusion.1), channel_id=1, source_target_pairs={{0,8},{1,9},{2,10},{3,11},{4,12},{5,13},{6,14},{7,15},{8,0},{9,1},... | collective-permute-start | bytes 196616 | tf_op jit(solution)/shard_map/ppermute | solution.py:108
  38.3 4.3 %collective-permute-start.22 = (bf16[64,512]{1,0:T(8,128)(2,1)S(1)}, bf16[64,512]{1,0:T(8,128)(2,1)S(1)}, u32[]{:S(2)}, u32[]{:S(2)}) collective-permute-start(bf16[64,512]{1,0:T(8,128)(2,1)S(1)} %slice.86), channel_id=1, source_target_pairs={{0,2},{1,3},{2,0},{3,1},{4,6},{5,7},{6,4},{7,5},{8,10},{9,11},{10,... | collective-permute-start | bytes 196616 | tf_op jit(solution)/shard_map/ppermute | solution.py:108
  39.9 6.3 %collective-permute-start.12 = (bf16[64,512]{1,0:T(8,128)(2,1)S(1)}, bf16[64,512]{1,0:T(8,128)(2,1)S(1)}, u32[]{:S(2)}, u32[]{:S(2)}) collective-permute-start(bf16[64,512]{1,0:T(8,128)(2,1)S(1)} %fusion.2), channel_id=1, source_target_pairs={{0,4},{1,5},{2,6},{3,7},{4,0},{5,1},{6,2},{7,3},{8,12},{9,13},{10,... | collective-permute-start | bytes 196616 | tf_op jit(solution)/shard_map/ppermute | solution.py:108
  42.7 6.2 %collective-permute-start.23 = (bf16[64,512]{1,0:T(8,128)(2,1)S(1)}, bf16[64,512]{1,0:T(8,128)(2,1)S(1)}, u32[]{:S(2)}, u32[]{:S(2)}) collective-permute-start(bf16[64,512]{1,0:T(8,128)(2,1)S(1)} %fusion), channel_id=1, source_target_pairs={{0,12},{1,13},{2,14},{3,15},{4,8},{5,9},{6,10},{7,11},{8,4},{9,5},... | collective-permute-start | bytes 196616 | tf_op jit(solution)/shard_map/ppermute | solution.py:108
  (3 other events, 50.7 us)

commit v5 on v4

--- a/solution.py
+++ b/solution.py
@@ -120,23 +120,29 @@
     def narrow(array):
         return array.astype(jnp.bfloat16)
 
+    def after(value, *arrays):
+        return lax.optimization_barrier((*arrays, value))[:-1]
+
     across, beside, beyond = exchange(own, 2), exchange(own, 4), exchange(own, 8)
-    beside, beyond, own_too, across = lax.optimization_barrier((beside, beyond, own, across))
-    middle = exchange(jnp.concatenate([beside, beyond]), 2)
-    gathered = {3: exchange(beyond, 4)}
+    near, far = partial_sums((own,))
+    start = paired(near, far)
+    gathered = {2: beyond, 3: exchange(beyond, 4)}
     for j in range(4, size // 4):
         low = j & -j
         gathered[j] = exchange(own if j == low else gathered[j - low], 4 * low)
-    sums = {0: partial_sums((own_too, across))}
-    middle, gathered[3], near = lax.optimization_barrier((middle, gathered[3], sums[0][0]))
-    sums[0] = (near, sums[0][1])
-    sums[1] = partial_sums((beside, middle[:rows]))
-    sums[2] = partial_sums((beyond, middle[rows:]))
+    (corner,) = after(beyond, exchange(beside, 2))
+    y2 = exchange(beyond, 2)
+    near, far = partial_sums((across, beside, corner))
+    pair = paired(near, far)
+    y2, gathered[3] = after(near, y2, gathered[3])
+    y = {j: exchange(block, 2) for j, block in gathered.items() if j > 2} | {2: y2}
+    sums = {}
     for j, block in gathered.items():
-        sums[j] = partial_sums((block, exchange(block, 2)))
-    pair, other = paired(*sums[0]), paired(*sums[1])
-    back = wide(exchange(narrow(jnp.concatenate([pair[rows:], other[rows:]])), 2))
-    mixed = pair[:rows] + back[:rows] + wide(exchange(narrow(other[:rows] + back[rows:]), 4))
+        last = y[j]
+        sums[j] = partial_sums((block, last))
+    back = wide(exchange(narrow(jnp.concatenate([pair[:rows], pair[2 * rows :]])), 2))
+    mixed = start + back[:rows]
+    mixed = mixed + wide(exchange(narrow(pair[rows : 2 * rows] + back[rows:]), 4))
     for j in range(2, size // 4):
         pair = paired(*sums[j])
         done = pair[:rows] + wide(exchange(narrow(pair[rows:]), 2))

time: 49.7 us -> 49 us (0.986)
  waiting for transfers between devices: 13 us -> 8.31 us
  starting transfers between devices: 22.5 us -> 26.4 us
    ppermute x24 -> x25, waiting for transfers between devices: 13 us -> 8.31 us  [exchange(): return lax.ppermute(array, 'expert', [(i, i ^ mask) for i in range(size)])]
    ppermute x24 -> x25, starting transfers between devices: 22.5 us -> 26.4 us  [exchange(): return lax.ppermute(array, 'expert', [(i, i ^ mask) for i in range(size)])]
  transfers between devices with their start and end apart: 24 -> 25, of which waited for: 10 -> 8; matrix products, arithmetic and copies ran while one was open for 1% -> 0% of each run, Pallas kernels for 24% -> 24%
where the time goes in v5:
time: 49 us; the launch traced here: 48.8 us
  starting transfers between devices  26.4 us (54%)
  Pallas kernels  13 us (27%)
  waiting for transfers between devices  8.31 us (17%)
  other arithmetic  0.87 us (2%)
    ppermute x25, starting transfers between devices, exchange(): return lax.ppermute(array, 'expert', [(i, i ^ mask) for i in range(size)])  26.4 us
    pallas_call x4, Pallas kernels, apply_experts(): pl.pallas_call(functools.partial(expert_kernel, len(blocks)), out_shape=(...  11.8 us
    ppermute x25, waiting for transfers between devices, exchange(): return lax.ppermute(array, 'expert', [(i, i ^ mask) for i in range(size)])  8.31 us
    pallas_call x1, Pallas kernels, tag_tokens(): pl.pallas_call(functools.partial(tag_kernel, local_experts), out_shape=ja...  1.17 us
  transfers between devices with their start and end apart: 25, of which 8 were waited for; matrix products, arithmetic and copies ran while one was open for 0% of the time, Pallas kernels for 24%

profile of v5, /device:TPU:0, one launch (start us, length us, event | category | flops | bytes accessed | tf_op | source)
XLA Modules:
  0.0 48.8 jit_solution(9748776641931897830)
XLA Ops:
  0.0 1.2 %tag_tokens.1.refs_0_ = bf16[64,1152]{1,0:T(8,128)(2,1)S(1)} custom-call(bf16[64,1024]{1,0:T(8,128)(2,1)} %codes_ref.1, s32[8,64]{1,0:T(8,128)} %bitcast.3, s32[8,64]{1,0:T(8,128)} %bitcast.4, bf16[8,64]{1,0:T(8,128)(2,1)} %bitcast.5), custom_call_target="tpu_custom_call" | custom-call | flops 8000000000 | bytes 16000000 | tf_op jit(solution)/shard_map/tag_tokens/pallas_call | solution.py:35
  1.2 3.1 %collective-permute-start.3 = (bf16[64,1152]{1,0:T(8,128)(2,1)S(1)}, bf16[64,1152]{1,0:T(8,128)(2,1)S(1)}, u32[]{:S(2)}, u32[]{:S(2)}) collective-permute-start(bf16[64,1152]{1,0:T(8,128)(2,1)S(1)} %tag_tokens.1.refs_0_), channel_id=1, source_target_pairs={{0,4},{1,5},{2,6},{3,7},{4,0},{5,1},{6,2},{7,3},{8,12},{9,13},{10,... | collective-permute-start | bytes 442376 | tf_op jit(solution)/shard_map/ppermute | solution.py:108
  4.3 1.5 %collective-permute-start.2 = (bf16[64,1152]{1,0:T(8,128)(2,1)S(1)}, bf16[64,1152]{1,0:T(8,128)(2,1)S(1)}, u32[]{:S(2)}, u32[]{:S(2)}) collective-permute-start(bf16[64,1152]{1,0:T(8,128)(2,1)S(1)} %tag_tokens.1.refs_0_), channel_id=1, source_target_pairs={{0,2},{1,3},{2,0},{3,1},{4,6},{5,7},{6,4},{7,5},{8,10},{9,11},{10,... | collective-permute-start | bytes 442376 | tf_op jit(solution)/shard_map/ppermute | solution.py:108
  5.8 2.6 %collective-permute-start.5 = (bf16[64,1152]{1,0:T(8,128)(2,1)S(1)}, bf16[64,1152]{1,0:T(8,128)(2,1)S(1)}, u32[]{:S(2)}, u32[]{:S(2)}) collective-permute-start(bf16[64,1152]{1,0:T(8,128)(2,1)S(1)} %tag_tokens.1.refs_0_), channel_id=1, source_target_pairs={{0,8},{1,9},{2,10},{3,11},{4,12},{5,13},{6,14},{7,15},{8,0},{9,1},... | collective-permute-start | bytes 442376 | tf_op jit(solution)/shard_map/ppermute | solution.py:108
  8.4 3.6 %collective-permute-start.4 = (bf16[64,1152]{1,0:T(8,128)(2,1)S(1)}, bf16[64,1152]{1,0:T(8,128)(2,1)S(1)}, u32[]{:S(2)}, u32[]{:S(2)}) collective-permute-start(bf16[64,1152]{1,0:T(8,128)(2,1)S(1)} %collective-permute-done.3.refs_1_), channel_id=1, source_target_pairs={{0,2},{1,3},{2,0},{3,1},{4,6},{5,7},{6,4},{7,5},{8,10},{9,11},{10,... | collective-permute-start | bytes 442376 | tf_op jit(solution)/shard_map/ppermute | solution.py:108
  12.5 2.4 %collective-permute-done.5.refs_0_ = bf16[64,1152]{1,0:T(8,128)(2,1)S(1)} collective-permute-done((bf16[64,1152]{1,0:T(8,128)(2,1)S(1)}, bf16[64,1152]{1,0:T(8,128)(2,1)S(1)}, u32[]{:S(2)}, u32[]{:S(2)}) %collective-permute-start.5) | collective-permute-done | bytes 147488 | tf_op jit(solution)/shard_map/ppermute | solution.py:108
  15.1 2.0 %collective-permute-start.12 = (bf16[64,1152]{1,0:T(8,128)(2,1)S(1)}, bf16[64,1152]{1,0:T(8,128)(2,1)S(1)}, u32[]{:S(2)}, u32[]{:S(2)}) collective-permute-start(bf16[64,1152]{1,0:T(8,128)(2,1)S(1)} %collective-permute-done.5.refs_0_), channel_id=1, source_target_pairs={{0,2},{1,3},{2,0},{3,1},{4,6},{5,7},{6,4},{7,5},{8,10},{9,11},{10,... | collective-permute-start | bytes 442376 | tf_op jit(solution)/shard_map/ppermute | solution.py:108
  17.2 4.3 %apply_experts.5 = (bf16[192,512]{1,0:T(8,128)(2,1)S(1)}, bf16[192,512]{1,0:T(8,128)(2,1)S(1)}) custom-call(bf16[64,1152]{1,0:T(8,128)(2,1)S(1)} %collective-permute-done.2.refs_0_, bf16[64,1152]{1,0:T(8,128)(2,1)S(1)} %collective-permute-done.3.refs_1_, bf16[64,1152]{1,0:T(8,128)(2,1)S(1)} %collective-permute-done.4.refs_2_, ...), custom_call_target="tpu_custom_call" | custom-call | flops 201326592 | bytes 1024 | tf_op jit(solution)/shard_map/apply_experts/pallas_call | solution.py:83
  22.4 0.8 %collective-permute-done.13.refs_0_ = bf16[64,1152]{1,0:T(8,128)(2,1)S(1)} collective-permute-done((bf16[64,1152]{1,0:T(8,128)(2,1)S(1)}, bf16[64,1152]{1,0:T(8,128)(2,1)S(1)}, u32[]{:S(2)}, u32[]{:S(2)}) %collective-permute-start.13) | collective-permute-done | bytes 147488 | tf_op jit(solution)/shard_map/ppermute | solution.py:108
  23.1 0.8 %collective-permute-start.19 = (bf16[64,1152]{1,0:T(8,128)(2,1)S(1)}, bf16[64,1152]{1,0:T(8,128)(2,1)S(1)}, u32[]{:S(2)}, u32[]{:S(2)}) collective-permute-start(bf16[64,1152]{1,0:T(8,128)(2,1)S(1)} %collective-permute-done.13.refs_0_), channel_id=1, source_target_pairs={{0,2},{1,3},{2,0},{3,1},{4,6},{5,7},{6,4},{7,5},{8,10},{9,11},{10,... | collective-permute-start | bytes 442376 | tf_op jit(solution)/shard_map/ppermute | solution.py:108
  24.0 1.6 %apply_experts.4 = (bf16[64,512]{1,0:T(8,128)(2,1)S(1)}, bf16[64,512]{1,0:T(8,128)(2,1)S(1)}) custom-call(bf16[64,1152]{1,0:T(8,128)(2,1)S(1)} %tag_tokens.1.refs_0_, bf16[64,1152]{1,0:T(8,128)(2,1)S(1)} %collective-permute-done.refs_1_, bf16[2,1024,1024]{2,1,0:T(8,128)(2,1)S(1)} %copy-done, bf16[2,1024,1024]{2,1,0:T(8,128)(2,1)S(1)} %copy-done.1, ...), custom_call_target="tpu_custom_call" | custom-call | flops 67108864 | bytes 1024 | tf_op jit(solution)/shard_map/apply_experts/pallas_call | solution.py:83
  26.2 2.9 %apply_experts.6 = (bf16[128,512]{1,0:T(8,128)(2,1)S(1)}, bf16[128,512]{1,0:T(8,128)(2,1)S(1)}) custom-call(bf16[64,1152]{1,0:T(8,128)(2,1)S(1)} %collective-permute-done.5.refs_0_, bf16[64,1152]{1,0:T(8,128)(2,1)S(1)} %collective-permute-done.12.refs_1_, bf16[64,1152]{1,0:T(8,128)(2,1)S(1)} %collective-permute-done.14.refs_2_, ...), custom_call_target="tpu_custom_call" | custom-call | flops 134217728 | bytes 1024 | tf_op jit(solution)/shard_map/apply_experts/pallas_call | solution.py:83
  29.8 1.3 %collective-permute-start.10 = (bf16[128,512]{1,0:T(8,128)(2,1)S(1)}, bf16[128,512]{1,0:T(8,128)(2,1)S(1)}, u32[]{:S(2)}, u32[]{:S(2)}) collective-permute-start(bf16[128,512]{1,0:T(8,128)(2,1)S(1)} %pad_maximum_fusion), channel_id=1, source_target_pairs={{0,2},{1,3},{2,0},{3,1},{4,6},{5,7},{6,4},{7,5},{8,10},{9,11},{10,... | collective-permute-start | bytes 393224 | tf_op jit(solution)/shard_map/ppermute | solution.py:108
  31.1 0.9 %collective-permute-start.17 = (bf16[64,512]{1,0:T(8,128)(2,1)S(1)}, bf16[64,512]{1,0:T(8,128)(2,1)S(1)}, u32[]{:S(2)}, u32[]{:S(2)}) collective-permute-start(bf16[64,512]{1,0:T(8,128)(2,1)S(1)} %slice.71), channel_id=1, source_target_pairs={{0,2},{1,3},{2,0},{3,1},{4,6},{5,7},{6,4},{7,5},{8,10},{9,11},{10,... | collective-permute-start | bytes 196616 | tf_op jit(solution)/shard_map/ppermute | solution.py:108
  32.0 2.9 %apply_experts.7 = (bf16[128,512]{1,0:T(8,128)(2,1)S(1)}, bf16[128,512]{1,0:T(8,128)(2,1)S(1)}) custom-call(bf16[64,1152]{1,0:T(8,128)(2,1)S(1)} %collective-permute-done.13.refs_0_, bf16[64,1152]{1,0:T(8,128)(2,1)S(1)} %collective-permute-done.19.refs_1_, bf16[64,1152]{1,0:T(8,128)(2,1)S(1)} %collective-permute-done.20.refs_2_, ...), custom_call_target="tpu_custom_call" | custom-call | flops 134217728 | bytes 1024 | tf_op jit(solution)/shard_map/apply_experts/pallas_call | solution.py:83
  35.0 1.1 %collective-permute-done.10 = bf16[128,512]{1,0:T(8,128)(2,1)S(1)} collective-permute-done((bf16[128,512]{1,0:T(8,128)(2,1)S(1)}, bf16[128,512]{1,0:T(8,128)(2,1)S(1)}, u32[]{:S(2)}, u32[]{:S(2)}) %collective-permute-start.10) | collective-permute-done | bytes 131104 | tf_op jit(solution)/shard_map/ppermute | solution.py:108
  36.2 1.4 %collective-permute-start.11 = (bf16[64,512]{1,0:T(8,128)(2,1)S(1)}, bf16[64,512]{1,0:T(8,128)(2,1)S(1)}, u32[]{:S(2)}, u32[]{:S(2)}) collective-permute-start(bf16[64,512]{1,0:T(8,128)(2,1)S(1)} %fusion.2), channel_id=1, source_target_pairs={{0,4},{1,5},{2,6},{3,7},{4,0},{5,1},{6,2},{7,3},{8,12},{9,13},{10,... | collective-permute-start | bytes 196616 | tf_op jit(solution)/shard_map/ppermute | solution.py:108
  37.7 1.3 %collective-permute-start.23 = (bf16[64,512]{1,0:T(8,128)(2,1)S(1)}, bf16[64,512]{1,0:T(8,128)(2,1)S(1)}, u32[]{:S(2)}, u32[]{:S(2)}) collective-permute-start(bf16[64,512]{1,0:T(8,128)(2,1)S(1)} %slice.70), channel_id=1, source_target_pairs={{0,2},{1,3},{2,0},{3,1},{4,6},{5,7},{6,4},{7,5},{8,10},{9,11},{10,... | collective-permute-start | bytes 196616 | tf_op jit(solution)/shard_map/ppermute | solution.py:108
  39.0 2.3 %collective-permute-start.18 = (bf16[64,512]{1,0:T(8,128)(2,1)S(1)}, bf16[64,512]{1,0:T(8,128)(2,1)S(1)}, u32[]{:S(2)}, u32[]{:S(2)}) collective-permute-start(bf16[64,512]{1,0:T(8,128)(2,1)S(1)} %fusion.1), channel_id=1, source_target_pairs={{0,8},{1,9},{2,10},{3,11},{4,12},{5,13},{6,14},{7,15},{8,0},{9,1},... | collective-permute-start | bytes 196616 | tf_op jit(solution)/shard_map/ppermute | solution.py:108
  41.4 0.6 %collective-permute-done.23 = bf16[64,512]{1,0:T(8,128)(2,1)S(1)} collective-permute-done((bf16[64,512]{1,0:T(8,128)(2,1)S(1)}, bf16[64,512]{1,0:T(8,128)(2,1)S(1)}, u32[]{:S(2)}, u32[]{:S(2)}) %collective-permute-start.23) | collective-permute-done | bytes 65568 | tf_op jit(solution)/shard_map/ppermute | solution.py:108
  42.0 3.2 %collective-permute-start.24 = (bf16[64,512]{1,0:T(8,128)(2,1)S(1)}, bf16[64,512]{1,0:T(8,128)(2,1)S(1)}, u32[]{:S(2)}, u32[]{:S(2)}) collective-permute-start(bf16[64,512]{1,0:T(8,128)(2,1)S(1)} %fusion), channel_id=1, source_target_pairs={{0,12},{1,13},{2,14},{3,15},{4,8},{5,9},{6,10},{7,11},{8,4},{9,5},... | collective-permute-start | bytes 196616 | tf_op jit(solution)/shard_map/ppermute | solution.py:108
  45.2 1.0 %collective-permute-done.18 = bf16[64,512]{1,0:T(8,128)(2,1)S(1)} collective-permute-done((bf16[64,512]{1,0:T(8,128)(2,1)S(1)}, bf16[64,512]{1,0:T(8,128)(2,1)S(1)}, u32[]{:S(2)}, u32[]{:S(2)}) %collective-permute-start.18) | collective-permute-done | bytes 65568 | tf_op jit(solution)/shard_map/ppermute | solution.py:108
  46.2 2.0 %collective-permute-done.24 = bf16[64,512]{1,0:T(8,128)(2,1)S(1)} collective-permute-done((bf16[64,512]{1,0:T(8,128)(2,1)S(1)}, bf16[64,512]{1,0:T(8,128)(2,1)S(1)}, u32[]{:S(2)}, u32[]{:S(2)}) %collective-permute-start.24) | collective-permute-done | bytes 65568 | tf_op jit(solution)/shard_map/ppermute | solution.py:108
  48.2 0.7 %fusion.6 = bf16[64,512]{1,0:T(8,128)(2,1)} fusion(f32[128,512]{1,0:T(8,128)S(1)} %convert_element_type.61, bf16[64,512]{1,0:T(8,128)(2,1)S(1)} %collective-permute-done.24, bf16[64,512]{1,0:T(8,128)(2,1)S(1)} %collective-permute-done.18, bf16[64,512]{1,0:T(8,128)(2,1)S(1)} %collective-permute-done.11, bf16[64,512]{1,0:T(8,128)(2,1)S(1)} %collective-permute-done.1, ...), kind=kLoop, calls=%fused_computation.15 | loop fusion | flops 360448 | bytes 524288 | tf_op jit(solution)/shard_map/convert_element_type | solution.py:150
  (49 shorter events, 3.1 us)
Async XLA Ops:
  1.2 7.2 %collective-permute-start.3 = (bf16[64,1152]{1,0:T(8,128)(2,1)S(1)}, bf16[64,1152]{1,0:T(8,128)(2,1)S(1)}, u32[]{:S(2)}, u32[]{:S(2)}) collective-permute-start(bf16[64,1152]{1,0:T(8,128)(2,1)S(1)} %tag_tokens.1.refs_0_), channel_id=1, source_target_pairs={{0,4},{1,5},{2,6},{3,7},{4,0},{5,1},{6,2},{7,3},{8,12},{9,13},{10,... | collective-permute-start | bytes 442376 | tf_op jit(solution)/shard_map/ppermute | solution.py:108
  4.3 7.7 %collective-permute-start.2 = (bf16[64,1152]{1,0:T(8,128)(2,1)S(1)}, bf16[64,1152]{1,0:T(8,128)(2,1)S(1)}, u32[]{:S(2)}, u32[]{:S(2)}) collective-permute-start(bf16[64,1152]{1,0:T(8,128)(2,1)S(1)} %tag_tokens.1.refs_0_), channel_id=1, source_target_pairs={{0,2},{1,3},{2,0},{3,1},{4,6},{5,7},{6,4},{7,5},{8,10},{9,11},{10,... | collective-permute-start | bytes 442376 | tf_op jit(solution)/shard_map/ppermute | solution.py:108
  5.8 9.1 %collective-permute-start.5 = (bf16[64,1152]{1,0:T(8,128)(2,1)S(1)}, bf16[64,1152]{1,0:T(8,128)(2,1)S(1)}, u32[]{:S(2)}, u32[]{:S(2)}) collective-permute-start(bf16[64,1152]{1,0:T(8,128)(2,1)S(1)} %tag_tokens.1.refs_0_), channel_id=1, source_target_pairs={{0,8},{1,9},{2,10},{3,11},{4,12},{5,13},{6,14},{7,15},{8,0},{9,1},... | collective-permute-start | bytes 442376 | tf_op jit(solution)/shard_map/ppermute | solution.py:108
  8.4 6.7 %collective-permute-start.4 = (bf16[64,1152]{1,0:T(8,128)(2,1)S(1)}, bf16[64,1152]{1,0:T(8,128)(2,1)S(1)}, u32[]{:S(2)}, u32[]{:S(2)}) collective-permute-start(bf16[64,1152]{1,0:T(8,128)(2,1)S(1)} %collective-permute-done.3.refs_1_), channel_id=1, source_target_pairs={{0,2},{1,3},{2,0},{3,1},{4,6},{5,7},{6,4},{7,5},{8,10},{9,11},{10,... | collective-permute-start | bytes 442376 | tf_op jit(solution)/shard_map/ppermute | solution.py:108
  12.0 5.2 %collective-permute-start.7 = (bf16[64,1152]{1,0:T(8,128)(2,1)S(1)}, bf16[64,1152]{1,0:T(8,128)(2,1)S(1)}, u32[]{:S(2)}, u32[]{:S(2)}) collective-permute-start(bf16[64,1152]{1,0:T(8,128)(2,1)S(1)} %collective-permute-done.3.refs_1_), channel_id=1, source_target_pairs={{0,1},{1,0},{2,3},{3,2},{4,5},{5,4},{6,7},{7,6},{8,9},{9,8},{10,11... | collective-permute-start | bytes 442376 | tf_op jit(solution)/shard_map/ppermute | solution.py:108
  12.0 5.2 %collective-permute-start.6 = (bf16[64,1152]{1,0:T(8,128)(2,1)S(1)}, bf16[64,1152]{1,0:T(8,128)(2,1)S(1)}, u32[]{:S(2)}, u32[]{:S(2)}) collective-permute-start(bf16[64,1152]{1,0:T(8,128)(2,1)S(1)} %collective-permute-done.2.refs_0_), channel_id=1, source_target_pairs={{0,1},{1,0},{2,3},{3,2},{4,5},{5,4},{6,7},{7,6},{8,9},{9,8},{10,11... | collective-permute-start | bytes 442376 | tf_op jit(solution)/shard_map/ppermute | solution.py:108
  15.1 2.0 %collective-permute-start.8 = (bf16[64,1152]{1,0:T(8,128)(2,1)S(1)}, bf16[64,1152]{1,0:T(8,128)(2,1)S(1)}, u32[]{:S(2)}, u32[]{:S(2)}) collective-permute-start(bf16[64,1152]{1,0:T(8,128)(2,1)S(1)} %collective-permute-done.4.refs_2_), channel_id=1, source_target_pairs={{0,1},{1,0},{2,3},{3,2},{4,5},{5,4},{6,7},{7,6},{8,9},{9,8},{10,11... | collective-permute-start | bytes 442376 | tf_op jit(solution)/shard_map/ppermute | solution.py:108
  15.1 7.2 %collective-permute-start.12 = (bf16[64,1152]{1,0:T(8,128)(2,1)S(1)}, bf16[64,1152]{1,0:T(8,128)(2,1)S(1)}, u32[]{:S(2)}, u32[]{:S(2)}) collective-permute-start(bf16[64,1152]{1,0:T(8,128)(2,1)S(1)} %collective-permute-done.5.refs_0_), channel_id=1, source_target_pairs={{0,2},{1,3},{2,0},{3,1},{4,6},{5,7},{6,4},{7,5},{8,10},{9,11},{10,... | collective-permute-start | bytes 442376 | tf_op jit(solution)/shard_map/ppermute | solution.py:108
  17.1 6.0 %collective-permute-start.13 = (bf16[64,1152]{1,0:T(8,128)(2,1)S(1)}, bf16[64,1152]{1,0:T(8,128)(2,1)S(1)}, u32[]{:S(2)}, u32[]{:S(2)}) collective-permute-start(bf16[64,1152]{1,0:T(8,128)(2,1)S(1)} %collective-permute-done.5.refs_0_), channel_id=1, source_target_pairs={{0,4},{1,5},{2,6},{3,7},{4,0},{5,1},{6,2},{7,3},{8,12},{9,13},{10,... | collective-permute-start | bytes 442376 | tf_op jit(solution)/shard_map/ppermute | solution.py:108
  21.6 8.1 %collective-permute-start.9 = (bf16[192,512]{1,0:T(8,128)(2,1)S(1)}, bf16[192,512]{1,0:T(8,128)(2,1)S(1)}, u32[]{:S(2)}, u32[]{:S(2)}) collective-permute-start(bf16[192,512]{1,0:T(8,128)(2,1)S(1)} %get-tuple-element.20), channel_id=1, source_target_pairs={{0,1},{1,0},{2,3},{3,2},{4,5},{5,4},{6,7},{7,6},{8,9},{9,8},{10,11... | collective-permute-start | bytes 589832 | tf_op jit(solution)/shard_map/ppermute | solution.py:108
  21.8 2.1 %collective-permute-start = (bf16[64,1152]{1,0:T(8,128)(2,1)S(1)}, bf16[64,1152]{1,0:T(8,128)(2,1)S(1)}, u32[]{:S(2)}, u32[]{:S(2)}) collective-permute-start(bf16[64,1152]{1,0:T(8,128)(2,1)S(1)} %tag_tokens.1.refs_0_), channel_id=1, source_target_pairs={{0,1},{1,0},{2,3},{3,2},{4,5},{5,4},{6,7},{7,6},{8,9},{9,8},{10,11... | collective-permute-start | bytes 442376 | tf_op jit(solution)/shard_map/ppermute | solution.py:108
  22.1 3.5 %collective-permute-start.14 = (bf16[64,1152]{1,0:T(8,128)(2,1)S(1)}, bf16[64,1152]{1,0:T(8,128)(2,1)S(1)}, u32[]{:S(2)}, u32[]{:S(2)}) collective-permute-start(bf16[64,1152]{1,0:T(8,128)(2,1)S(1)} %collective-permute-done.5.refs_0_), channel_id=1, source_target_pairs={{0,1},{1,0},{2,3},{3,2},{4,5},{5,4},{6,7},{7,6},{8,9},{9,8},{10,11... | collective-permute-start | bytes 442376 | tf_op jit(solution)/shard_map/ppermute | solution.py:108
  23.1 3.0 %collective-permute-start.15 = (bf16[64,1152]{1,0:T(8,128)(2,1)S(1)}, bf16[64,1152]{1,0:T(8,128)(2,1)S(1)}, u32[]{:S(2)}, u32[]{:S(2)}) collective-permute-start(bf16[64,1152]{1,0:T(8,128)(2,1)S(1)} %collective-permute-done.12.refs_1_), channel_id=1, source_target_pairs={{0,1},{1,0},{2,3},{3,2},{4,5},{5,4},{6,7},{7,6},{8,9},{9,8},{10,11... | collective-permute-start | bytes 442376 | tf_op jit(solution)/shard_map/ppermute | solution.py:108
  23.1 6.3 %collective-permute-start.19 = (bf16[64,1152]{1,0:T(8,128)(2,1)S(1)}, bf16[64,1152]{1,0:T(8,128)(2,1)S(1)}, u32[]{:S(2)}, u32[]{:S(2)}) collective-permute-start(bf16[64,1152]{1,0:T(8,128)(2,1)S(1)} %collective-permute-done.13.refs_0_), channel_id=1, source_target_pairs={{0,2},{1,3},{2,0},{3,1},{4,6},{5,7},{6,4},{7,5},{8,10},{9,11},{10,... | collective-permute-start | bytes 442376 | tf_op jit(solution)/shard_map/ppermute | solution.py:108
  25.6 19.6 %collective-permute-start.1 = (bf16[64,512]{1,0:T(8,128)(2,1)S(1)}, bf16[64,512]{1,0:T(8,128)(2,1)S(1)}, u32[]{:S(2)}, u32[]{:S(2)}) collective-permute-start(bf16[64,512]{1,0:T(8,128)(2,1)S(1)} %get-tuple-element.17), channel_id=1, source_target_pairs={{0,1},{1,0},{2,3},{3,2},{4,5},{5,4},{6,7},{7,6},{8,9},{9,8},{10,11... | collective-permute-start | bytes 196616 | tf_op jit(solution)/shard_map/ppermute | solution.py:108
  25.7 6.3 %collective-permute-start.20 = (bf16[64,1152]{1,0:T(8,128)(2,1)S(1)}, bf16[64,1152]{1,0:T(8,128)(2,1)S(1)}, u32[]{:S(2)}, u32[]{:S(2)}) collective-permute-start(bf16[64,1152]{1,0:T(8,128)(2,1)S(1)} %collective-permute-done.13.refs_0_), channel_id=1, source_target_pairs={{0,1},{1,0},{2,3},{3,2},{4,5},{5,4},{6,7},{7,6},{8,9},{9,8},{10,11... | collective-permute-start | bytes 442376 | tf_op jit(solution)/shard_map/ppermute | solution.py:108
  29.4 2.6 %collective-permute-start.21 = (bf16[64,1152]{1,0:T(8,128)(2,1)S(1)}, bf16[64,1152]{1,0:T(8,128)(2,1)S(1)}, u32[]{:S(2)}, u32[]{:S(2)}) collective-permute-start(bf16[64,1152]{1,0:T(8,128)(2,1)S(1)} %collective-permute-done.19.refs_1_), channel_id=1, source_target_pairs={{0,1},{1,0},{2,3},{3,2},{4,5},{5,4},{6,7},{7,6},{8,9},{9,8},{10,11... | collective-permute-start | bytes 442376 | tf_op jit(solution)/shard_map/ppermute | solution.py:108
  29.8 6.4 %collective-permute-start.10 = (bf16[128,512]{1,0:T(8,128)(2,1)S(1)}, bf16[128,512]{1,0:T(8,128)(2,1)S(1)}, u32[]{:S(2)}, u32[]{:S(2)}) collective-permute-start(bf16[128,512]{1,0:T(8,128)(2,1)S(1)} %pad_maximum_fusion), channel_id=1, source_target_pairs={{0,2},{1,3},{2,0},{3,1},{4,6},{5,7},{6,4},{7,5},{8,10},{9,11},{10,... | collective-permute-start | bytes 393224 | tf_op jit(solution)/shard_map/ppermute | solution.py:108
  31.1 7.9 %collective-permute-start.17 = (bf16[64,512]{1,0:T(8,128)(2,1)S(1)}, bf16[64,512]{1,0:T(8,128)(2,1)S(1)}, u32[]{:S(2)}, u32[]{:S(2)}) collective-permute-start(bf16[64,512]{1,0:T(8,128)(2,1)S(1)} %slice.71), channel_id=1, source_target_pairs={{0,2},{1,3},{2,0},{3,1},{4,6},{5,7},{6,4},{7,5},{8,10},{9,11},{10,... | collective-permute-start | bytes 196616 | tf_op jit(solution)/shard_map/ppermute | solution.py:108
  35.0 2.7 %collective-permute-start.22 = (bf16[128,512]{1,0:T(8,128)(2,1)S(1)}, bf16[128,512]{1,0:T(8,128)(2,1)S(1)}, u32[]{:S(2)}, u32[]{:S(2)}) collective-permute-start(bf16[128,512]{1,0:T(8,128)(2,1)S(1)} %get-tuple-element.26), channel_id=1, source_target_pairs={{0,1},{1,0},{2,3},{3,2},{4,5},{5,4},{6,7},{7,6},{8,9},{9,8},{10,11... | collective-permute-start | bytes 393224 | tf_op jit(solution)/shard_map/ppermute | solution.py:108
  36.2 9.0 %collective-permute-start.11 = (bf16[64,512]{1,0:T(8,128)(2,1)S(1)}, bf16[64,512]{1,0:T(8,128)(2,1)S(1)}, u32[]{:S(2)}, u32[]{:S(2)}) collective-permute-start(bf16[64,512]{1,0:T(8,128)(2,1)S(1)} %fusion.2), channel_id=1, source_target_pairs={{0,4},{1,5},{2,6},{3,7},{4,0},{5,1},{6,2},{7,3},{8,12},{9,13},{10,... | collective-permute-start | bytes 196616 | tf_op jit(solution)/shard_map/ppermute | solution.py:108
  37.7 4.3 %collective-permute-start.23 = (bf16[64,512]{1,0:T(8,128)(2,1)S(1)}, bf16[64,512]{1,0:T(8,128)(2,1)S(1)}, u32[]{:S(2)}, u32[]{:S(2)}) collective-permute-start(bf16[64,512]{1,0:T(8,128)(2,1)S(1)} %slice.70), channel_id=1, source_target_pairs={{0,2},{1,3},{2,0},{3,1},{4,6},{5,7},{6,4},{7,5},{8,10},{9,11},{10,... | collective-permute-start | bytes 196616 | tf_op jit(solution)/shard_map/ppermute | solution.py:108
  39.0 7.1 %collective-permute-start.18 = (bf16[64,512]{1,0:T(8,128)(2,1)S(1)}, bf16[64,512]{1,0:T(8,128)(2,1)S(1)}, u32[]{:S(2)}, u32[]{:S(2)}) collective-permute-start(bf16[64,512]{1,0:T(8,128)(2,1)S(1)} %fusion.1), channel_id=1, source_target_pairs={{0,8},{1,9},{2,10},{3,11},{4,12},{5,13},{6,14},{7,15},{8,0},{9,1},... | collective-permute-start | bytes 196616 | tf_op jit(solution)/shard_map/ppermute | solution.py:108
  42.0 6.1 %collective-permute-start.24 = (bf16[64,512]{1,0:T(8,128)(2,1)S(1)}, bf16[64,512]{1,0:T(8,128)(2,1)S(1)}, u32[]{:S(2)}, u32[]{:S(2)}) collective-permute-start(bf16[64,512]{1,0:T(8,128)(2,1)S(1)} %fusion), channel_id=1, source_target_pairs={{0,12},{1,13},{2,14},{3,15},{4,8},{5,9},{6,10},{7,11},{8,4},{9,5},... | collective-permute-start | bytes 196616 | tf_op jit(solution)/shard_map/ppermute | solution.py:108
  (4 other events, 53.5 us)

commit v6 on v5

--- a/solution.py
+++ b/solution.py
@@ -126,6 +126,7 @@
     across, beside, beyond = exchange(own, 2), exchange(own, 4), exchange(own, 8)
     near, far = partial_sums((own,))
     start = paired(near, far)
+    (across,) = after(near, across)
     gathered = {2: beyond, 3: exchange(beyond, 4)}
     for j in range(4, size // 4):
         low = j & -j

time: 49 us -> 47.6 us (0.971)
  starting transfers between devices: 26.4 us -> 23.1 us
  waiting for transfers between devices: 8.31 us -> 10.2 us
    ppermute x25, starting transfers between devices: 26.4 us -> 23.1 us  [exchange(): return lax.ppermute(array, 'expert', [(i, i ^ mask) for i in range(size)])]
    ppermute x25, waiting for transfers between devices: 8.31 us -> 10.2 us  [exchange(): return lax.ppermute(array, 'expert', [(i, i ^ mask) for i in range(size)])]
  transfers between devices with their start and end apart: 25 -> 25, of which waited for: 8 -> 8; matrix products, arithmetic and copies ran while one was open for 0% -> 0% of each run, Pallas kernels for 24% -> 25%
where the time goes in v6:
time: 47.6 us; the launch traced here: 47.4 us
  starting transfers between devices  23.1 us (49%)
  Pallas kernels  13 us (27%)
  waiting for transfers between devices  10.2 us (21%)
  other arithmetic  0.87 us (2%)
    ppermute x25, starting transfers between devices, exchange(): return lax.ppermute(array, 'expert', [(i, i ^ mask) for i in range(size)])  23.1 us
    pallas_call x4, Pallas kernels, apply_experts(): pl.pallas_call(functools.partial(expert_kernel, len(blocks)), out_shape=(...  11.8 us
    ppermute x25, waiting for transfers between devices, exchange(): return lax.ppermute(array, 'expert', [(i, i ^ mask) for i in range(size)])  10.2 us
    pallas_call x1, Pallas kernels, tag_tokens(): pl.pallas_call(functools.partial(tag_kernel, local_experts), out_shape=ja...  1.17 us
  transfers between devices with their start and end apart: 25, of which 8 were waited for; matrix products, arithmetic and copies ran while one was open for 0% of the time, Pallas kernels for 25%

profile of v6, /device:TPU:0, one launch (start us, length us, event | category | flops | bytes accessed | tf_op | source)
XLA Modules:
  0.0 47.4 jit_solution(13229891961999454896)
XLA Ops:
  0.0 1.2 %tag_tokens.1.refs_0_ = bf16[64,1152]{1,0:T(8,128)(2,1)S(1)} custom-call(bf16[64,1024]{1,0:T(8,128)(2,1)} %codes_ref.1, s32[8,64]{1,0:T(8,128)} %bitcast.3, s32[8,64]{1,0:T(8,128)} %bitcast.4, bf16[8,64]{1,0:T(8,128)(2,1)} %bitcast.5), custom_call_target="tpu_custom_call" | custom-call | flops 8000000000 | bytes 16000000 | tf_op jit(solution)/shard_map/tag_tokens/pallas_call | solution.py:35
  1.2 3.1 %collective-permute-start.3 = (bf16[64,1152]{1,0:T(8,128)(2,1)S(1)}, bf16[64,1152]{1,0:T(8,128)(2,1)S(1)}, u32[]{:S(2)}, u32[]{:S(2)}) collective-permute-start(bf16[64,1152]{1,0:T(8,128)(2,1)S(1)} %tag_tokens.1.refs_0_), channel_id=1, source_target_pairs={{0,4},{1,5},{2,6},{3,7},{4,0},{5,1},{6,2},{7,3},{8,12},{9,13},{10,... | collective-permute-start | bytes 442376 | tf_op jit(solution)/shard_map/ppermute | solution.py:108
  4.3 1.5 %collective-permute-start.2 = (bf16[64,1152]{1,0:T(8,128)(2,1)S(1)}, bf16[64,1152]{1,0:T(8,128)(2,1)S(1)}, u32[]{:S(2)}, u32[]{:S(2)}) collective-permute-start(bf16[64,1152]{1,0:T(8,128)(2,1)S(1)} %tag_tokens.1.refs_0_), channel_id=1, source_target_pairs={{0,2},{1,3},{2,0},{3,1},{4,6},{5,7},{6,4},{7,5},{8,10},{9,11},{10,... | collective-permute-start | bytes 442376 | tf_op jit(solution)/shard_map/ppermute | solution.py:108
  5.8 2.6 %collective-permute-start.5 = (bf16[64,1152]{1,0:T(8,128)(2,1)S(1)}, bf16[64,1152]{1,0:T(8,128)(2,1)S(1)}, u32[]{:S(2)}, u32[]{:S(2)}) collective-permute-start(bf16[64,1152]{1,0:T(8,128)(2,1)S(1)} %tag_tokens.1.refs_0_), channel_id=1, source_target_pairs={{0,8},{1,9},{2,10},{3,11},{4,12},{5,13},{6,14},{7,15},{8,0},{9,1},... | collective-permute-start | bytes 442376 | tf_op jit(solution)/shard_map/ppermute | solution.py:108
  8.4 1.4 %collective-permute-start.4 = (bf16[64,1152]{1,0:T(8,128)(2,1)S(1)}, bf16[64,1152]{1,0:T(8,128)(2,1)S(1)}, u32[]{:S(2)}, u32[]{:S(2)}) collective-permute-start(bf16[64,1152]{1,0:T(8,128)(2,1)S(1)} %collective-permute-done.3.refs_1_), channel_id=1, source_target_pairs={{0,2},{1,3},{2,0},{3,1},{4,6},{5,7},{6,4},{7,5},{8,10},{9,11},{10,... | collective-permute-start | bytes 442376 | tf_op jit(solution)/shard_map/ppermute | solution.py:108
  9.8 1.6 %apply_experts.4 = (bf16[64,512]{1,0:T(8,128)(2,1)S(1)}, bf16[64,512]{1,0:T(8,128)(2,1)S(1)}) custom-call(bf16[64,1152]{1,0:T(8,128)(2,1)S(1)} %tag_tokens.1.refs_0_, bf16[64,1152]{1,0:T(8,128)(2,1)S(1)} %collective-permute-done.refs_1_, bf16[2,1024,1024]{2,1,0:T(8,128)(2,1)S(1)} %copy-done, bf16[2,1024,1024]{2,1,0:T(8,128)(2,1)S(1)} %copy-done.1, ...), custom_call_target="tpu_custom_call" | custom-call | flops 67108864 | bytes 1024 | tf_op jit(solution)/shard_map/apply_experts/pallas_call | solution.py:83
  12.0 3.8 %collective-permute-done.5.refs_0_ = bf16[64,1152]{1,0:T(8,128)(2,1)S(1)} collective-permute-done((bf16[64,1152]{1,0:T(8,128)(2,1)S(1)}, bf16[64,1152]{1,0:T(8,128)(2,1)S(1)}, u32[]{:S(2)}, u32[]{:S(2)}) %collective-permute-start.5) | collective-permute-done | bytes 147488 | tf_op jit(solution)/shard_map/ppermute | solution.py:108
  16.5 0.6 %collective-permute-done.8.refs_5_ = bf16[64,1152]{1,0:T(8,128)(2,1)S(1)} collective-permute-done((bf16[64,1152]{1,0:T(8,128)(2,1)S(1)}, bf16[64,1152]{1,0:T(8,128)(2,1)S(1)}, u32[]{:S(2)}, u32[]{:S(2)}) %collective-permute-start.8) | collective-permute-done | bytes 147488 | tf_op jit(solution)/shard_map/ppermute | solution.py:108
  17.2 4.3 %apply_experts.5 = (bf16[192,512]{1,0:T(8,128)(2,1)S(1)}, bf16[192,512]{1,0:T(8,128)(2,1)S(1)}) custom-call(bf16[64,1152]{1,0:T(8,128)(2,1)S(1)} %collective-permute-done.2.refs_0_, bf16[64,1152]{1,0:T(8,128)(2,1)S(1)} %collective-permute-done.3.refs_1_, bf16[64,1152]{1,0:T(8,128)(2,1)S(1)} %collective-permute-done.4.refs_2_, ...), custom_call_target="tpu_custom_call" | custom-call | flops 201326592 | bytes 1024 | tf_op jit(solution)/shard_map/apply_experts/pallas_call | solution.py:83
  22.3 1.5 %collective-permute-start.19 = (bf16[64,1152]{1,0:T(8,128)(2,1)S(1)}, bf16[64,1152]{1,0:T(8,128)(2,1)S(1)}, u32[]{:S(2)}, u32[]{:S(2)}) collective-permute-start(bf16[64,1152]{1,0:T(8,128)(2,1)S(1)} %collective-permute-done.13.refs_0_), channel_id=1, source_target_pairs={{0,2},{1,3},{2,0},{3,1},{4,6},{5,7},{6,4},{7,5},{8,10},{9,11},{10,... | collective-permute-start | bytes 442376 | tf_op jit(solution)/shard_map/ppermute | solution.py:108
  24.3 2.9 %apply_experts.6 = (bf16[128,512]{1,0:T(8,128)(2,1)S(1)}, bf16[128,512]{1,0:T(8,128)(2,1)S(1)}) custom-call(bf16[64,1152]{1,0:T(8,128)(2,1)S(1)} %collective-permute-done.5.refs_0_, bf16[64,1152]{1,0:T(8,128)(2,1)S(1)} %collective-permute-done.12.refs_1_, bf16[64,1152]{1,0:T(8,128)(2,1)S(1)} %collective-permute-done.14.refs_2_, ...), custom_call_target="tpu_custom_call" | custom-call | flops 134217728 | bytes 1024 | tf_op jit(solution)/shard_map/apply_experts/pallas_call | solution.py:83
  27.6 1.0 %collective-permute-done.19.refs_1_ = bf16[64,1152]{1,0:T(8,128)(2,1)S(1)} collective-permute-done((bf16[64,1152]{1,0:T(8,128)(2,1)S(1)}, bf16[64,1152]{1,0:T(8,128)(2,1)S(1)}, u32[]{:S(2)}, u32[]{:S(2)}) %collective-permute-start.19) | collective-permute-done | bytes 147488 | tf_op jit(solution)/shard_map/ppermute | solution.py:108
  28.7 1.5 %collective-permute-start.10 = (bf16[128,512]{1,0:T(8,128)(2,1)S(1)}, bf16[128,512]{1,0:T(8,128)(2,1)S(1)}, u32[]{:S(2)}, u32[]{:S(2)}) collective-permute-start(bf16[128,512]{1,0:T(8,128)(2,1)S(1)} %pad_maximum_fusion), channel_id=1, source_target_pairs={{0,2},{1,3},{2,0},{3,1},{4,6},{5,7},{6,4},{7,5},{8,10},{9,11},{10,... | collective-permute-start | bytes 393224 | tf_op jit(solution)/shard_map/ppermute | solution.py:108
  30.3 0.6 %collective-permute-start.17 = (bf16[64,512]{1,0:T(8,128)(2,1)S(1)}, bf16[64,512]{1,0:T(8,128)(2,1)S(1)}, u32[]{:S(2)}, u32[]{:S(2)}) collective-permute-start(bf16[64,512]{1,0:T(8,128)(2,1)S(1)} %slice.71), channel_id=1, source_target_pairs={{0,2},{1,3},{2,0},{3,1},{4,6},{5,7},{6,4},{7,5},{8,10},{9,11},{10,... | collective-permute-start | bytes 196616 | tf_op jit(solution)/shard_map/ppermute | solution.py:108
  30.9 2.9 %apply_experts.7 = (bf16[128,512]{1,0:T(8,128)(2,1)S(1)}, bf16[128,512]{1,0:T(8,128)(2,1)S(1)}) custom-call(bf16[64,1152]{1,0:T(8,128)(2,1)S(1)} %collective-permute-done.13.refs_0_, bf16[64,1152]{1,0:T(8,128)(2,1)S(1)} %collective-permute-done.19.refs_1_, bf16[64,1152]{1,0:T(8,128)(2,1)S(1)} %collective-permute-done.20.refs_2_, ...), custom_call_target="tpu_custom_call" | custom-call | flops 134217728 | bytes 1024 | tf_op jit(solution)/shard_map/apply_experts/pallas_call | solution.py:83
  34.0 1.1 %collective-permute-done.10 = bf16[128,512]{1,0:T(8,128)(2,1)S(1)} collective-permute-done((bf16[128,512]{1,0:T(8,128)(2,1)S(1)}, bf16[128,512]{1,0:T(8,128)(2,1)S(1)}, u32[]{:S(2)}, u32[]{:S(2)}) %collective-permute-start.10) | collective-permute-done | bytes 131104 | tf_op jit(solution)/shard_map/ppermute | solution.py:108
  35.1 1.1 %collective-permute-start.11 = (bf16[64,512]{1,0:T(8,128)(2,1)S(1)}, bf16[64,512]{1,0:T(8,128)(2,1)S(1)}, u32[]{:S(2)}, u32[]{:S(2)}) collective-permute-start(bf16[64,512]{1,0:T(8,128)(2,1)S(1)} %fusion.2), channel_id=1, source_target_pairs={{0,4},{1,5},{2,6},{3,7},{4,0},{5,1},{6,2},{7,3},{8,12},{9,13},{10,... | collective-permute-start | bytes 196616 | tf_op jit(solution)/shard_map/ppermute | solution.py:108
  36.3 1.5 %collective-permute-start.23 = (bf16[64,512]{1,0:T(8,128)(2,1)S(1)}, bf16[64,512]{1,0:T(8,128)(2,1)S(1)}, u32[]{:S(2)}, u32[]{:S(2)}) collective-permute-start(bf16[64,512]{1,0:T(8,128)(2,1)S(1)} %slice.70), channel_id=1, source_target_pairs={{0,2},{1,3},{2,0},{3,1},{4,6},{5,7},{6,4},{7,5},{8,10},{9,11},{10,... | collective-permute-start | bytes 196616 | tf_op jit(solution)/shard_map/ppermute | solution.py:108
  37.8 2.1 %collective-permute-start.18 = (bf16[64,512]{1,0:T(8,128)(2,1)S(1)}, bf16[64,512]{1,0:T(8,128)(2,1)S(1)}, u32[]{:S(2)}, u32[]{:S(2)}) collective-permute-start(bf16[64,512]{1,0:T(8,128)(2,1)S(1)} %fusion.1), channel_id=1, source_target_pairs={{0,8},{1,9},{2,10},{3,11},{4,12},{5,13},{6,14},{7,15},{8,0},{9,1},... | collective-permute-start | bytes 196616 | tf_op jit(solution)/shard_map/ppermute | solution.py:108
  40.0 0.6 %collective-permute-done.23 = bf16[64,512]{1,0:T(8,128)(2,1)S(1)} collective-permute-done((bf16[64,512]{1,0:T(8,128)(2,1)S(1)}, bf16[64,512]{1,0:T(8,128)(2,1)S(1)}, u32[]{:S(2)}, u32[]{:S(2)}) %collective-permute-start.23) | collective-permute-done | bytes 65568 | tf_op jit(solution)/shard_map/ppermute | solution.py:108
  40.6 3.3 %collective-permute-start.24 = (bf16[64,512]{1,0:T(8,128)(2,1)S(1)}, bf16[64,512]{1,0:T(8,128)(2,1)S(1)}, u32[]{:S(2)}, u32[]{:S(2)}) collective-permute-start(bf16[64,512]{1,0:T(8,128)(2,1)S(1)} %fusion), channel_id=1, source_target_pairs={{0,12},{1,13},{2,14},{3,15},{4,8},{5,9},{6,10},{7,11},{8,4},{9,5},... | collective-permute-start | bytes 196616 | tf_op jit(solution)/shard_map/ppermute | solution.py:108
  43.9 0.9 %collective-permute-done.18 = bf16[64,512]{1,0:T(8,128)(2,1)S(1)} collective-permute-done((bf16[64,512]{1,0:T(8,128)(2,1)S(1)}, bf16[64,512]{1,0:T(8,128)(2,1)S(1)}, u32[]{:S(2)}, u32[]{:S(2)}) %collective-permute-start.18) | collective-permute-done | bytes 65568 | tf_op jit(solution)/shard_map/ppermute | solution.py:108
  44.8 1.9 %collective-permute-done.24 = bf16[64,512]{1,0:T(8,128)(2,1)S(1)} collective-permute-done((bf16[64,512]{1,0:T(8,128)(2,1)S(1)}, bf16[64,512]{1,0:T(8,128)(2,1)S(1)}, u32[]{:S(2)}, u32[]{:S(2)}) %collective-permute-start.24) | collective-permute-done | bytes 65568 | tf_op jit(solution)/shard_map/ppermute | solution.py:108
  46.7 0.7 %fusion.6 = bf16[64,512]{1,0:T(8,128)(2,1)} fusion(f32[128,512]{1,0:T(8,128)S(1)} %convert_element_type.61, bf16[64,512]{1,0:T(8,128)(2,1)S(1)} %collective-permute-done.24, bf16[64,512]{1,0:T(8,128)(2,1)S(1)} %collective-permute-done.18, bf16[64,512]{1,0:T(8,128)(2,1)S(1)} %collective-permute-done.11, bf16[64,512]{1,0:T(8,128)(2,1)S(1)} %collective-permute-done.1, ...), kind=kLoop, calls=%fused_computation.15 | loop fusion | flops 360448 | bytes 524288 | tf_op jit(solution)/shard_map/convert_element_type | solution.py:151
  (49 shorter events, 3.3 us)
Async XLA Ops:
  1.2 7.2 %collective-permute-start.3 = (bf16[64,1152]{1,0:T(8,128)(2,1)S(1)}, bf16[64,1152]{1,0:T(8,128)(2,1)S(1)}, u32[]{:S(2)}, u32[]{:S(2)}) collective-permute-start(bf16[64,1152]{1,0:T(8,128)(2,1)S(1)} %tag_tokens.1.refs_0_), channel_id=1, source_target_pairs={{0,4},{1,5},{2,6},{3,7},{4,0},{5,1},{6,2},{7,3},{8,12},{9,13},{10,... | collective-permute-start | bytes 442376 | tf_op jit(solution)/shard_map/ppermute | solution.py:108
  4.3 5.5 %collective-permute-start = (bf16[64,1152]{1,0:T(8,128)(2,1)S(1)}, bf16[64,1152]{1,0:T(8,128)(2,1)S(1)}, u32[]{:S(2)}, u32[]{:S(2)}) collective-permute-start(bf16[64,1152]{1,0:T(8,128)(2,1)S(1)} %tag_tokens.1.refs_0_), channel_id=1, source_target_pairs={{0,1},{1,0},{2,3},{3,2},{4,5},{5,4},{6,7},{7,6},{8,9},{9,8},{10,11... | collective-permute-start | bytes 442376 | tf_op jit(solution)/shard_map/ppermute | solution.py:108
  4.3 7.2 %collective-permute-start.2 = (bf16[64,1152]{1,0:T(8,128)(2,1)S(1)}, bf16[64,1152]{1,0:T(8,128)(2,1)S(1)}, u32[]{:S(2)}, u32[]{:S(2)}) collective-permute-start(bf16[64,1152]{1,0:T(8,128)(2,1)S(1)} %tag_tokens.1.refs_0_), channel_id=1, source_target_pairs={{0,2},{1,3},{2,0},{3,1},{4,6},{5,7},{6,4},{7,5},{8,10},{9,11},{10,... | collective-permute-start | bytes 442376 | tf_op jit(solution)/shard_map/ppermute | solution.py:108
  5.8 10.0 %collective-permute-start.5 = (bf16[64,1152]{1,0:T(8,128)(2,1)S(1)}, bf16[64,1152]{1,0:T(8,128)(2,1)S(1)}, u32[]{:S(2)}, u32[]{:S(2)}) collective-permute-start(bf16[64,1152]{1,0:T(8,128)(2,1)S(1)} %tag_tokens.1.refs_0_), channel_id=1, source_target_pairs={{0,8},{1,9},{2,10},{3,11},{4,12},{5,13},{6,14},{7,15},{8,0},{9,1},... | collective-permute-start | bytes 442376 | tf_op jit(solution)/shard_map/ppermute | solution.py:108
  8.4 7.4 %collective-permute-start.4 = (bf16[64,1152]{1,0:T(8,128)(2,1)S(1)}, bf16[64,1152]{1,0:T(8,128)(2,1)S(1)}, u32[]{:S(2)}, u32[]{:S(2)}) collective-permute-start(bf16[64,1152]{1,0:T(8,128)(2,1)S(1)} %collective-permute-done.3.refs_1_), channel_id=1, source_target_pairs={{0,2},{1,3},{2,0},{3,1},{4,6},{5,7},{6,4},{7,5},{8,10},{9,11},{10,... | collective-permute-start | bytes 442376 | tf_op jit(solution)/shard_map/ppermute | solution.py:108
  11.4 5.1 %collective-permute-start.6 = (bf16[64,1152]{1,0:T(8,128)(2,1)S(1)}, bf16[64,1152]{1,0:T(8,128)(2,1)S(1)}, u32[]{:S(2)}, u32[]{:S(2)}) collective-permute-start(bf16[64,1152]{1,0:T(8,128)(2,1)S(1)} %collective-permute-done.2.refs_0_), channel_id=1, source_target_pairs={{0,1},{1,0},{2,3},{3,2},{4,5},{5,4},{6,7},{7,6},{8,9},{9,8},{10,11... | collective-permute-start | bytes 442376 | tf_op jit(solution)/shard_map/ppermute | solution.py:108
  11.5 5.0 %collective-permute-start.7 = (bf16[64,1152]{1,0:T(8,128)(2,1)S(1)}, bf16[64,1152]{1,0:T(8,128)(2,1)S(1)}, u32[]{:S(2)}, u32[]{:S(2)}) collective-permute-start(bf16[64,1152]{1,0:T(8,128)(2,1)S(1)} %collective-permute-done.3.refs_1_), channel_id=1, source_target_pairs={{0,1},{1,0},{2,3},{3,2},{4,5},{5,4},{6,7},{7,6},{8,9},{9,8},{10,11... | collective-permute-start | bytes 442376 | tf_op jit(solution)/shard_map/ppermute | solution.py:108
  15.8 6.3 %collective-permute-start.12 = (bf16[64,1152]{1,0:T(8,128)(2,1)S(1)}, bf16[64,1152]{1,0:T(8,128)(2,1)S(1)}, u32[]{:S(2)}, u32[]{:S(2)}) collective-permute-start(bf16[64,1152]{1,0:T(8,128)(2,1)S(1)} %collective-permute-done.5.refs_0_), channel_id=1, source_target_pairs={{0,2},{1,3},{2,0},{3,1},{4,6},{5,7},{6,4},{7,5},{8,10},{9,11},{10,... | collective-permute-start | bytes 442376 | tf_op jit(solution)/shard_map/ppermute | solution.py:108
  16.4 6.0 %collective-permute-start.13 = (bf16[64,1152]{1,0:T(8,128)(2,1)S(1)}, bf16[64,1152]{1,0:T(8,128)(2,1)S(1)}, u32[]{:S(2)}, u32[]{:S(2)}) collective-permute-start(bf16[64,1152]{1,0:T(8,128)(2,1)S(1)} %collective-permute-done.5.refs_0_), channel_id=1, source_target_pairs={{0,4},{1,5},{2,6},{3,7},{4,0},{5,1},{6,2},{7,3},{8,12},{9,13},{10,... | collective-permute-start | bytes 442376 | tf_op jit(solution)/shard_map/ppermute | solution.py:108
  21.5 7.1 %collective-permute-start.9 = (bf16[192,512]{1,0:T(8,128)(2,1)S(1)}, bf16[192,512]{1,0:T(8,128)(2,1)S(1)}, u32[]{:S(2)}, u32[]{:S(2)}) collective-permute-start(bf16[192,512]{1,0:T(8,128)(2,1)S(1)} %get-tuple-element.22), channel_id=1, source_target_pairs={{0,1},{1,0},{2,3},{3,2},{4,5},{5,4},{6,7},{7,6},{8,9},{9,8},{10,11... | collective-permute-start | bytes 589832 | tf_op jit(solution)/shard_map/ppermute | solution.py:108
  21.7 2.3 %collective-permute-start.14 = (bf16[64,1152]{1,0:T(8,128)(2,1)S(1)}, bf16[64,1152]{1,0:T(8,128)(2,1)S(1)}, u32[]{:S(2)}, u32[]{:S(2)}) collective-permute-start(bf16[64,1152]{1,0:T(8,128)(2,1)S(1)} %collective-permute-done.5.refs_0_), channel_id=1, source_target_pairs={{0,1},{1,0},{2,3},{3,2},{4,5},{5,4},{6,7},{7,6},{8,9},{9,8},{10,11... | collective-permute-start | bytes 442376 | tf_op jit(solution)/shard_map/ppermute | solution.py:108
  22.3 2.0 %collective-permute-start.15 = (bf16[64,1152]{1,0:T(8,128)(2,1)S(1)}, bf16[64,1152]{1,0:T(8,128)(2,1)S(1)}, u32[]{:S(2)}, u32[]{:S(2)}) collective-permute-start(bf16[64,1152]{1,0:T(8,128)(2,1)S(1)} %collective-permute-done.12.refs_1_), channel_id=1, source_target_pairs={{0,1},{1,0},{2,3},{3,2},{4,5},{5,4},{6,7},{7,6},{8,9},{9,8},{10,11... | collective-permute-start | bytes 442376 | tf_op jit(solution)/shard_map/ppermute | solution.py:108
  22.3 6.3 %collective-permute-start.19 = (bf16[64,1152]{1,0:T(8,128)(2,1)S(1)}, bf16[64,1152]{1,0:T(8,128)(2,1)S(1)}, u32[]{:S(2)}, u32[]{:S(2)}) collective-permute-start(bf16[64,1152]{1,0:T(8,128)(2,1)S(1)} %collective-permute-done.13.refs_0_), channel_id=1, source_target_pairs={{0,2},{1,3},{2,0},{3,1},{4,6},{5,7},{6,4},{7,5},{8,10},{9,11},{10,... | collective-permute-start | bytes 442376 | tf_op jit(solution)/shard_map/ppermute | solution.py:108
  23.8 20.1 %collective-permute-start.1 = (bf16[64,512]{1,0:T(8,128)(2,1)S(1)}, bf16[64,512]{1,0:T(8,128)(2,1)S(1)}, u32[]{:S(2)}, u32[]{:S(2)}) collective-permute-start(bf16[64,512]{1,0:T(8,128)(2,1)S(1)} %get-tuple-element.18), channel_id=1, source_target_pairs={{0,1},{1,0},{2,3},{3,2},{4,5},{5,4},{6,7},{7,6},{8,9},{9,8},{10,11... | collective-permute-start | bytes 196616 | tf_op jit(solution)/shard_map/ppermute | solution.py:108
  24.0 6.9 %collective-permute-start.20 = (bf16[64,1152]{1,0:T(8,128)(2,1)S(1)}, bf16[64,1152]{1,0:T(8,128)(2,1)S(1)}, u32[]{:S(2)}, u32[]{:S(2)}) collective-permute-start(bf16[64,1152]{1,0:T(8,128)(2,1)S(1)} %collective-permute-done.13.refs_0_), channel_id=1, source_target_pairs={{0,1},{1,0},{2,3},{3,2},{4,5},{5,4},{6,7},{7,6},{8,9},{9,8},{10,11... | collective-permute-start | bytes 442376 | tf_op jit(solution)/shard_map/ppermute | solution.py:108
  27.3 3.0 %collective-permute-start.16 = (bf16[128,512]{1,0:T(8,128)(2,1)S(1)}, bf16[128,512]{1,0:T(8,128)(2,1)S(1)}, u32[]{:S(2)}, u32[]{:S(2)}) collective-permute-start(bf16[128,512]{1,0:T(8,128)(2,1)S(1)} %get-tuple-element.25), channel_id=1, source_target_pairs={{0,1},{1,0},{2,3},{3,2},{4,5},{5,4},{6,7},{7,6},{8,9},{9,8},{10,11... | collective-permute-start | bytes 393224 | tf_op jit(solution)/shard_map/ppermute | solution.py:108
  28.6 2.3 %collective-permute-start.21 = (bf16[64,1152]{1,0:T(8,128)(2,1)S(1)}, bf16[64,1152]{1,0:T(8,128)(2,1)S(1)}, u32[]{:S(2)}, u32[]{:S(2)}) collective-permute-start(bf16[64,1152]{1,0:T(8,128)(2,1)S(1)} %collective-permute-done.19.refs_1_), channel_id=1, source_target_pairs={{0,1},{1,0},{2,3},{3,2},{4,5},{5,4},{6,7},{7,6},{8,9},{9,8},{10,11... | collective-permute-start | bytes 442376 | tf_op jit(solution)/shard_map/ppermute | solution.py:108
  28.7 6.4 %collective-permute-start.10 = (bf16[128,512]{1,0:T(8,128)(2,1)S(1)}, bf16[128,512]{1,0:T(8,128)(2,1)S(1)}, u32[]{:S(2)}, u32[]{:S(2)}) collective-permute-start(bf16[128,512]{1,0:T(8,128)(2,1)S(1)} %pad_maximum_fusion), channel_id=1, source_target_pairs={{0,2},{1,3},{2,0},{3,1},{4,6},{5,7},{6,4},{7,5},{8,10},{9,11},{10,... | collective-permute-start | bytes 393224 | tf_op jit(solution)/shard_map/ppermute | solution.py:108
  30.3 7.5 %collective-permute-start.17 = (bf16[64,512]{1,0:T(8,128)(2,1)S(1)}, bf16[64,512]{1,0:T(8,128)(2,1)S(1)}, u32[]{:S(2)}, u32[]{:S(2)}) collective-permute-start(bf16[64,512]{1,0:T(8,128)(2,1)S(1)} %slice.71), channel_id=1, source_target_pairs={{0,2},{1,3},{2,0},{3,1},{4,6},{5,7},{6,4},{7,5},{8,10},{9,11},{10,... | collective-permute-start | bytes 196616 | tf_op jit(solution)/shard_map/ppermute | solution.py:108
  33.9 2.3 %collective-permute-start.22 = (bf16[128,512]{1,0:T(8,128)(2,1)S(1)}, bf16[128,512]{1,0:T(8,128)(2,1)S(1)}, u32[]{:S(2)}, u32[]{:S(2)}) collective-permute-start(bf16[128,512]{1,0:T(8,128)(2,1)S(1)} %get-tuple-element.28), channel_id=1, source_target_pairs={{0,1},{1,0},{2,3},{3,2},{4,5},{5,4},{6,7},{7,6},{8,9},{9,8},{10,11... | collective-permute-start | bytes 393224 | tf_op jit(solution)/shard_map/ppermute | solution.py:108
  35.1 8.8 %collective-permute-start.11 = (bf16[64,512]{1,0:T(8,128)(2,1)S(1)}, bf16[64,512]{1,0:T(8,128)(2,1)S(1)}, u32[]{:S(2)}, u32[]{:S(2)}) collective-permute-start(bf16[64,512]{1,0:T(8,128)(2,1)S(1)} %fusion.2), channel_id=1, source_target_pairs={{0,4},{1,5},{2,6},{3,7},{4,0},{5,1},{6,2},{7,3},{8,12},{9,13},{10,... | collective-permute-start | bytes 196616 | tf_op jit(solution)/shard_map/ppermute | solution.py:108
  36.3 4.3 %collective-permute-start.23 = (bf16[64,512]{1,0:T(8,128)(2,1)S(1)}, bf16[64,512]{1,0:T(8,128)(2,1)S(1)}, u32[]{:S(2)}, u32[]{:S(2)}) collective-permute-start(bf16[64,512]{1,0:T(8,128)(2,1)S(1)} %slice.70), channel_id=1, source_target_pairs={{0,2},{1,3},{2,0},{3,1},{4,6},{5,7},{6,4},{7,5},{8,10},{9,11},{10,... | collective-permute-start | bytes 196616 | tf_op jit(solution)/shard_map/ppermute | solution.py:108
  37.8 7.0 %collective-permute-start.18 = (bf16[64,512]{1,0:T(8,128)(2,1)S(1)}, bf16[64,512]{1,0:T(8,128)(2,1)S(1)}, u32[]{:S(2)}, u32[]{:S(2)}) collective-permute-start(bf16[64,512]{1,0:T(8,128)(2,1)S(1)} %fusion.1), channel_id=1, source_target_pairs={{0,8},{1,9},{2,10},{3,11},{4,12},{5,13},{6,14},{7,15},{8,0},{9,1},... | collective-permute-start | bytes 196616 | tf_op jit(solution)/shard_map/ppermute | solution.py:108
  40.6 6.1 %collective-permute-start.24 = (bf16[64,512]{1,0:T(8,128)(2,1)S(1)}, bf16[64,512]{1,0:T(8,128)(2,1)S(1)}, u32[]{:S(2)}, u32[]{:S(2)}) collective-permute-start(bf16[64,512]{1,0:T(8,128)(2,1)S(1)} %fusion), channel_id=1, source_target_pairs={{0,12},{1,13},{2,14},{3,15},{4,8},{5,9},{6,10},{7,11},{8,4},{9,5},... | collective-permute-start | bytes 196616 | tf_op jit(solution)/shard_map/ppermute | solution.py:108
  (4 other events, 30.8 us)

commit v7 on v6

--- a/solution.py
+++ b/solution.py
@@ -12,29 +12,36 @@
 VMEM_SPEC = pl.BlockSpec(memory_space=pltpu.VMEM)
 
 
-def tag_kernel(local_experts, codes_ref, devices_ref, members_ref, scores_ref, out_ref):
+def tag_kernel(local_experts, experts, codes_ref, devices_ref, members_ref, scores_ref, out_ref):
     rows, rank_in = codes_ref.shape
-    lanes = out_ref.shape[1] - rank_in
+    fold = LANES // experts
+    part = rows // fold
     ids = devices_ref[...] * local_experts + members_ref[...]
     scores = scores_ref[...].astype(jnp.float32)
-    expert = lax.broadcasted_iota(jnp.int32, (lanes, rows), 0)
-    spread = jnp.zeros((lanes, rows), jnp.float32)
-    for k in range(ids.shape[0]):
-        spread = jnp.where(expert == ids[k : k + 1, :], scores[k : k + 1, :], spread)
-    out_ref[:, :rank_in] = codes_ref[...]
-    out_ref[:, rank_in:] = spread.T.astype(jnp.bfloat16)
+    expert = lax.broadcasted_iota(jnp.int32, (experts, part), 0)
+    pieces = []
+    for q in range(fold):
+        tokens = slice(q * part, (q + 1) * part)
+        spread = jnp.zeros((experts, part), jnp.float32)
+        for k in range(ids.shape[0]):
+            spread = jnp.where(expert == ids[k : k + 1, tokens], scores[k : k + 1, tokens], spread)
+        pieces.append(spread)
+    for c in range(rank_in // LANES):
+        out_ref[c * rows : (c + 1) * rows, :] = codes_ref[:, c * LANES : (c + 1) * LANES]
+    packed = jnp.concatenate(pieces, axis=0).T
+    out_ref[rank_in // LANES * rows :, :] = packed.astype(jnp.bfloat16)
 
 
 def tag_tokens(codes, devices, members, scores, local_experts, experts):
-    lanes = -(-experts // LANES) * LANES
     rows, rank_in = codes.shape
     operands = [
         pltpu.with_memory_space_constraint(operand, pltpu.HBM)
         for operand in (codes, devices.T, members.T, scores.T)
     ]
+    height = rank_in // LANES * rows + rows * experts // LANES
     return pl.pallas_call(
-        functools.partial(tag_kernel, local_experts),
-        out_shape=jax.ShapeDtypeStruct((rows, rank_in + lanes), jnp.bfloat16),
+        functools.partial(tag_kernel, local_experts, experts),
+        out_shape=jax.ShapeDtypeStruct((height, LANES), jnp.bfloat16),
         out_specs=VMEM_SPEC,
         compiler_params=pltpu.CompilerParams(vmem_limit_bytes=8 * MIB),
         cost_estimate=pl.CostEstimate(
@@ -44,22 +51,36 @@
     )(*operands)
 
 
-def expert_kernel(count, *refs):
+def expert_kernel(count, experts, *refs):
     blocks, (gate_ref, up_ref, down_ref, near_ref, far_ref, rows_ref) = refs[:count], refs[count:]
     local_experts, rank_in, hidden_units = gate_ref.shape
-    at = 0
-    for block in blocks:
-        rows_ref[at : at + block.shape[0], :] = block[...]
-        at += block.shape[0]
-    scores = rows_ref[:, rank_in:].astype(jnp.float32)
-    total = jnp.sum(scores, axis=1, keepdims=True)
-    lane = lax.broadcasted_iota(jnp.int32, scores.shape, 1)
+    size = rows_ref.shape[0] // count
+    fold = LANES // experts
+    part = size // fold
+    for i, block in enumerate(blocks):
+        for c in range(rank_in // LANES):
+            rows_ref[i * size : (i + 1) * size, c * LANES : (c + 1) * LANES] = block[
+                c * size : (c + 1) * size, :
+            ]
+    packed = [block[rank_in // LANES * size :, :].astype(jnp.float32) for block in blocks]
+    packed = jnp.concatenate(packed, axis=0)
+    lane = lax.broadcasted_iota(jnp.int32, packed.shape, 1)
     first = lax.axis_index("expert") * local_experts
-    codes = rows_ref[:, :rank_in]
+
+    def per_row(select):
+        sums = [
+            jnp.sum(jnp.where(select(q), packed, 0.0), axis=1, keepdims=True) for q in range(fold)
+        ]
+        return jnp.concatenate(
+            [sums[q][i * part : (i + 1) * part] for i in range(count) for q in range(fold)], axis=0
+        )
+
+    total = per_row(lambda q: (lane >= q * experts) & (lane < (q + 1) * experts))
+    codes = rows_ref[...]
     out = jnp.zeros((codes.shape[0], down_ref.shape[2]), jnp.float32)
     own = jnp.zeros_like(total)
     for e in range(local_experts):
-        score = jnp.sum(jnp.where(lane == first + e, scores, 0.0), axis=1, keepdims=True)
+        score = per_row(lambda q: lane == q * experts + first + e)
         own = own + score
         gate = jnp.dot(codes, gate_ref[e], preferred_element_type=jnp.float32)
         up = jnp.dot(codes, up_ref[e], preferred_element_type=jnp.float32)
@@ -73,19 +94,18 @@
     far_ref[...] = out[half:]
 
 
-def apply_experts(blocks, weights):
-    width = blocks[0].shape[1]
-    rows = sum(block.shape[0] for block in blocks)
+def apply_experts(blocks, weights, size, experts):
     local_experts, rank_in, hidden_units = weights[0].shape
+    rows = size * len(blocks)
     rank_out = weights[2].shape[2]
     half = jax.ShapeDtypeStruct((rows // 2, rank_out), jnp.bfloat16)
     flops = 2 * rows * local_experts * hidden_units * (2 * rank_in + rank_out)
     return pl.pallas_call(
-        functools.partial(expert_kernel, len(blocks)),
+        functools.partial(expert_kernel, len(blocks), experts),
         out_shape=(half, half),
         in_specs=[VMEM_SPEC] * (len(blocks) + 3),
         out_specs=(VMEM_SPEC, VMEM_SPEC),
-        scratch_shapes=[pltpu.VMEM((rows, width), jnp.bfloat16)],
+        scratch_shapes=[pltpu.VMEM((rows, rank_in), jnp.bfloat16)],
         compiler_params=pltpu.CompilerParams(vmem_limit_bytes=24 * MIB),
         cost_estimate=pl.CostEstimate(
             flops=flops // 20, bytes_accessed=1024, transcendentals=0
@@ -112,7 +132,7 @@
     )
     def partial_sums(blocks):
         blocks = blocks + tuple(exchange(block, 1) for block in blocks)
-        return apply_experts(blocks, weights)
+        return apply_experts(blocks, weights, rows, local_experts * size)
 
     def paired(near, far):
         return wide(near) + wide(exchange(far, 1))

time: 47.6 us -> 47 us (0.987)
  waiting for transfers between devices: 10.2 us -> 9.22 us
  Pallas kernels: 13 us -> 13.6 us
    ppermute x25, waiting for transfers between devices: 10.2 us -> 9.22 us  [exchange(): return lax.ppermute(array, 'expert', [(i, i ^ mask) for i in range(size)])]
    pallas_call x5, Pallas kernels: 13 us -> 13.6 us  [the longest x4 12.4 us: apply_experts(): pl.pallas_call(functools.partial(expert_kernel, len(blocks), experts), ou...]
  transfers between devices with their start and end apart: 25 -> 25, of which waited for: 8 -> 7; matrix products, arithmetic and copies ran while one was open for 0% -> 1% of each run, Pallas kernels for 25% -> 27%
where the time goes in v7:
time: 47 us; the launch traced here: 46.8 us
  starting transfers between devices  22.9 us (49%)
  Pallas kernels  13.6 us (29%)
  waiting for transfers between devices  9.22 us (20%)
  other arithmetic  0.89 us (2%)
    ppermute x25, starting transfers between devices, exchange(): return lax.ppermute(array, 'expert', [(i, i ^ mask) for i in range(size)])  22.9 us
    pallas_call x4, Pallas kernels, apply_experts(): pl.pallas_call(functools.partial(expert_kernel, len(blocks), experts), ou...  12.4 us
    ppermute x25, waiting for transfers between devices, exchange(): return lax.ppermute(array, 'expert', [(i, i ^ mask) for i in range(size)])  9.22 us
    pallas_call x1, Pallas kernels, tag_tokens(): pl.pallas_call(functools.partial(tag_kernel, local_experts, experts), out...  1.21 us
  transfers between devices with their start and end apart: 25, of which 7 were waited for; matrix products, arithmetic and copies ran while one was open for 1% of the time, Pallas kernels for 27%

profile of v7, /device:TPU:0, one launch (start us, length us, event | category | flops | bytes accessed | tf_op | source)
XLA Modules:
  0.0 46.8 jit_solution(7539530110224471716)
XLA Ops:
  0.0 1.2 %tag_tokens.1.refs_0_ = bf16[528,128]{1,0:T(8,128)(2,1)S(1)} custom-call(bf16[64,1024]{1,0:T(8,128)(2,1)} %codes_ref.1, s32[8,64]{1,0:T(8,128)} %bitcast.3, s32[8,64]{1,0:T(8,128)} %bitcast.4, bf16[8,64]{1,0:T(8,128)(2,1)} %bitcast.5), custom_call_target="tpu_custom_call" | custom-call | flops 8000000000 | bytes 16000000 | tf_op jit(solution)/shard_map/tag_tokens/pallas_call | solution.py:42
  1.2 3.1 %collective-permute-start.3 = (bf16[528,128]{1,0:T(8,128)(2,1)S(1)}, bf16[528,128]{1,0:T(8,128)(2,1)S(1)}, u32[]{:S(2)}, u32[]{:S(2)}) collective-permute-start(bf16[528,128]{1,0:T(8,128)(2,1)S(1)} %tag_tokens.1.refs_0_), channel_id=1, source_target_pairs={{0,4},{1,5},{2,6},{3,7},{4,0},{5,1},{6,2},{7,3},{8,12},{9,13},{10,... | collective-permute-start | bytes 405512 | tf_op jit(solution)/shard_map/ppermute | solution.py:128
  4.3 1.5 %collective-permute-start.2 = (bf16[528,128]{1,0:T(8,128)(2,1)S(1)}, bf16[528,128]{1,0:T(8,128)(2,1)S(1)}, u32[]{:S(2)}, u32[]{:S(2)}) collective-permute-start(bf16[528,128]{1,0:T(8,128)(2,1)S(1)} %tag_tokens.1.refs_0_), channel_id=1, source_target_pairs={{0,2},{1,3},{2,0},{3,1},{4,6},{5,7},{6,4},{7,5},{8,10},{9,11},{10,... | collective-permute-start | bytes 405512 | tf_op jit(solution)/shard_map/ppermute | solution.py:128
  5.8 2.6 %collective-permute-start.5 = (bf16[528,128]{1,0:T(8,128)(2,1)S(1)}, bf16[528,128]{1,0:T(8,128)(2,1)S(1)}, u32[]{:S(2)}, u32[]{:S(2)}) collective-permute-start(bf16[528,128]{1,0:T(8,128)(2,1)S(1)} %tag_tokens.1.refs_0_), channel_id=1, source_target_pairs={{0,8},{1,9},{2,10},{3,11},{4,12},{5,13},{6,14},{7,15},{8,0},{9,1},... | collective-permute-start | bytes 405512 | tf_op jit(solution)/shard_map/ppermute | solution.py:128
  8.4 1.2 %collective-permute-start.4 = (bf16[528,128]{1,0:T(8,128)(2,1)S(1)}, bf16[528,128]{1,0:T(8,128)(2,1)S(1)}, u32[]{:S(2)}, u32[]{:S(2)}) collective-permute-start(bf16[528,128]{1,0:T(8,128)(2,1)S(1)} %collective-permute-done.3.refs_1_), channel_id=1, source_target_pairs={{0,2},{1,3},{2,0},{3,1},{4,6},{5,7},{6,4},{7,5},{8,10},{9,11},{10,... | collective-permute-start | bytes 405512 | tf_op jit(solution)/shard_map/ppermute | solution.py:128
  9.6 1.7 %apply_experts.4 = (bf16[64,512]{1,0:T(8,128)(2,1)S(1)}, bf16[64,512]{1,0:T(8,128)(2,1)S(1)}) custom-call(bf16[528,128]{1,0:T(8,128)(2,1)S(1)} %tag_tokens.1.refs_0_, bf16[528,128]{1,0:T(8,128)(2,1)S(1)} %collective-permute-done.refs_1_, bf16[2,1024,1024]{2,1,0:T(8,128)(2,1)S(1)} %copy-done, bf16[2,1024,1024]{2,1,0:T(8,128)(2,1)S(1)} %copy-done.1, ...), custom_call_target="tpu_custom_call" | custom-call | flops 67108864 | bytes 1024 | tf_op jit(solution)/shard_map/apply_experts/pallas_call | solution.py:103
  11.9 3.4 %collective-permute-done.5.refs_0_ = bf16[528,128]{1,0:T(8,128)(2,1)S(1)} collective-permute-done((bf16[528,128]{1,0:T(8,128)(2,1)S(1)}, bf16[528,128]{1,0:T(8,128)(2,1)S(1)}, u32[]{:S(2)}, u32[]{:S(2)}) %collective-permute-start.5) | collective-permute-done | bytes 135200 | tf_op jit(solution)/shard_map/ppermute | solution.py:128
  15.3 0.6 %collective-permute-start.12 = (bf16[528,128]{1,0:T(8,128)(2,1)S(1)}, bf16[528,128]{1,0:T(8,128)(2,1)S(1)}, u32[]{:S(2)}, u32[]{:S(2)}) collective-permute-start(bf16[528,128]{1,0:T(8,128)(2,1)S(1)} %collective-permute-done.5.refs_0_), channel_id=1, source_target_pairs={{0,2},{1,3},{2,0},{3,1},{4,6},{5,7},{6,4},{7,5},{8,10},{9,11},{10,... | collective-permute-start | bytes 405512 | tf_op jit(solution)/shard_map/ppermute | solution.py:128
  16.6 4.5 %apply_experts.5 = (bf16[192,512]{1,0:T(8,128)(2,1)S(1)}, bf16[192,512]{1,0:T(8,128)(2,1)S(1)}) custom-call(bf16[528,128]{1,0:T(8,128)(2,1)S(1)} %collective-permute-done.2.refs_0_, bf16[528,128]{1,0:T(8,128)(2,1)S(1)} %collective-permute-done.3.refs_1_, bf16[528,128]{1,0:T(8,128)(2,1)S(1)} %collective-permute-done.4.refs_2_, ...), custom_call_target="tpu_custom_call" | custom-call | flops 201326592 | bytes 1024 | tf_op jit(solution)/shard_map/apply_experts/pallas_call | solution.py:103
  21.9 1.1 %collective-permute-start.19 = (bf16[528,128]{1,0:T(8,128)(2,1)S(1)}, bf16[528,128]{1,0:T(8,128)(2,1)S(1)}, u32[]{:S(2)}, u32[]{:S(2)}) collective-permute-start(bf16[528,128]{1,0:T(8,128)(2,1)S(1)} %collective-permute-done.13.refs_0_), channel_id=1, source_target_pairs={{0,2},{1,3},{2,0},{3,1},{4,6},{5,7},{6,4},{7,5},{8,10},{9,11},{10,... | collective-permute-start | bytes 405512 | tf_op jit(solution)/shard_map/ppermute | solution.py:128
  23.6 3.1 %apply_experts.6 = (bf16[128,512]{1,0:T(8,128)(2,1)S(1)}, bf16[128,512]{1,0:T(8,128)(2,1)S(1)}) custom-call(bf16[528,128]{1,0:T(8,128)(2,1)S(1)} %collective-permute-done.5.refs_0_, bf16[528,128]{1,0:T(8,128)(2,1)S(1)} %collective-permute-done.12.refs_1_, bf16[528,128]{1,0:T(8,128)(2,1)S(1)} %collective-permute-done.14.refs_2_, ...), custom_call_target="tpu_custom_call" | custom-call | flops 134217728 | bytes 1024 | tf_op jit(solution)/shard_map/apply_experts/pallas_call | solution.py:103
  27.0 0.8 %collective-permute-done.19.refs_1_ = bf16[528,128]{1,0:T(8,128)(2,1)S(1)} collective-permute-done((bf16[528,128]{1,0:T(8,128)(2,1)S(1)}, bf16[528,128]{1,0:T(8,128)(2,1)S(1)}, u32[]{:S(2)}, u32[]{:S(2)}) %collective-permute-start.19) | collective-permute-done | bytes 135200 | tf_op jit(solution)/shard_map/ppermute | solution.py:128
  27.9 1.4 %collective-permute-start.10 = (bf16[128,512]{1,0:T(8,128)(2,1)S(1)}, bf16[128,512]{1,0:T(8,128)(2,1)S(1)}, u32[]{:S(2)}, u32[]{:S(2)}) collective-permute-start(bf16[128,512]{1,0:T(8,128)(2,1)S(1)} %pad_maximum_fusion), channel_id=1, source_target_pairs={{0,2},{1,3},{2,0},{3,1},{4,6},{5,7},{6,4},{7,5},{8,10},{9,11},{10,... | collective-permute-start | bytes 393224 | tf_op jit(solution)/shard_map/ppermute | solution.py:128
  29.3 0.8 %collective-permute-start.17 = (bf16[64,512]{1,0:T(8,128)(2,1)S(1)}, bf16[64,512]{1,0:T(8,128)(2,1)S(1)}, u32[]{:S(2)}, u32[]{:S(2)}) collective-permute-start(bf16[64,512]{1,0:T(8,128)(2,1)S(1)} %slice.71), channel_id=1, source_target_pairs={{0,2},{1,3},{2,0},{3,1},{4,6},{5,7},{6,4},{7,5},{8,10},{9,11},{10,... | collective-permute-start | bytes 196616 | tf_op jit(solution)/shard_map/ppermute | solution.py:128
  30.1 3.1 %apply_experts.7 = (bf16[128,512]{1,0:T(8,128)(2,1)S(1)}, bf16[128,512]{1,0:T(8,128)(2,1)S(1)}) custom-call(bf16[528,128]{1,0:T(8,128)(2,1)S(1)} %collective-permute-done.13.refs_0_, bf16[528,128]{1,0:T(8,128)(2,1)S(1)} %collective-permute-done.19.refs_1_, bf16[528,128]{1,0:T(8,128)(2,1)S(1)} %collective-permute-done.20.refs_2_, ...), custom_call_target="tpu_custom_call" | custom-call | flops 134217728 | bytes 1024 | tf_op jit(solution)/shard_map/apply_experts/pallas_call | solution.py:103
  33.3 0.9 %collective-permute-done.10 = bf16[128,512]{1,0:T(8,128)(2,1)S(1)} collective-permute-done((bf16[128,512]{1,0:T(8,128)(2,1)S(1)}, bf16[128,512]{1,0:T(8,128)(2,1)S(1)}, u32[]{:S(2)}, u32[]{:S(2)}) %collective-permute-start.10) | collective-permute-done | bytes 131104 | tf_op jit(solution)/shard_map/ppermute | solution.py:128
  34.3 1.3 %collective-permute-start.11 = (bf16[64,512]{1,0:T(8,128)(2,1)S(1)}, bf16[64,512]{1,0:T(8,128)(2,1)S(1)}, u32[]{:S(2)}, u32[]{:S(2)}) collective-permute-start(bf16[64,512]{1,0:T(8,128)(2,1)S(1)} %fusion.2), channel_id=1, source_target_pairs={{0,4},{1,5},{2,6},{3,7},{4,0},{5,1},{6,2},{7,3},{8,12},{9,13},{10,... | collective-permute-start | bytes 196616 | tf_op jit(solution)/shard_map/ppermute | solution.py:128
  35.6 1.5 %collective-permute-start.23 = (bf16[64,512]{1,0:T(8,128)(2,1)S(1)}, bf16[64,512]{1,0:T(8,128)(2,1)S(1)}, u32[]{:S(2)}, u32[]{:S(2)}) collective-permute-start(bf16[64,512]{1,0:T(8,128)(2,1)S(1)} %slice.70), channel_id=1, source_target_pairs={{0,2},{1,3},{2,0},{3,1},{4,6},{5,7},{6,4},{7,5},{8,10},{9,11},{10,... | collective-permute-start | bytes 196616 | tf_op jit(solution)/shard_map/ppermute | solution.py:128
  37.2 1.9 %collective-permute-start.18 = (bf16[64,512]{1,0:T(8,128)(2,1)S(1)}, bf16[64,512]{1,0:T(8,128)(2,1)S(1)}, u32[]{:S(2)}, u32[]{:S(2)}) collective-permute-start(bf16[64,512]{1,0:T(8,128)(2,1)S(1)} %fusion.1), channel_id=1, source_target_pairs={{0,8},{1,9},{2,10},{3,11},{4,12},{5,13},{6,14},{7,15},{8,0},{9,1},... | collective-permute-start | bytes 196616 | tf_op jit(solution)/shard_map/ppermute | solution.py:128
  39.1 0.9 %collective-permute-done.23 = bf16[64,512]{1,0:T(8,128)(2,1)S(1)} collective-permute-done((bf16[64,512]{1,0:T(8,128)(2,1)S(1)}, bf16[64,512]{1,0:T(8,128)(2,1)S(1)}, u32[]{:S(2)}, u32[]{:S(2)}) %collective-permute-start.23) | collective-permute-done | bytes 65568 | tf_op jit(solution)/shard_map/ppermute | solution.py:128
  40.0 3.5 %collective-permute-start.24 = (bf16[64,512]{1,0:T(8,128)(2,1)S(1)}, bf16[64,512]{1,0:T(8,128)(2,1)S(1)}, u32[]{:S(2)}, u32[]{:S(2)}) collective-permute-start(bf16[64,512]{1,0:T(8,128)(2,1)S(1)} %fusion), channel_id=1, source_target_pairs={{0,12},{1,13},{2,14},{3,15},{4,8},{5,9},{6,10},{7,11},{8,4},{9,5},... | collective-permute-start | bytes 196616 | tf_op jit(solution)/shard_map/ppermute | solution.py:128
  43.5 1.0 %collective-permute-done.18 = bf16[64,512]{1,0:T(8,128)(2,1)S(1)} collective-permute-done((bf16[64,512]{1,0:T(8,128)(2,1)S(1)}, bf16[64,512]{1,0:T(8,128)(2,1)S(1)}, u32[]{:S(2)}, u32[]{:S(2)}) %collective-permute-start.18) | collective-permute-done | bytes 65568 | tf_op jit(solution)/shard_map/ppermute | solution.py:128
  44.5 1.6 %collective-permute-done.24 = bf16[64,512]{1,0:T(8,128)(2,1)S(1)} collective-permute-done((bf16[64,512]{1,0:T(8,128)(2,1)S(1)}, bf16[64,512]{1,0:T(8,128)(2,1)S(1)}, u32[]{:S(2)}, u32[]{:S(2)}) %collective-permute-start.24) | collective-permute-done | bytes 65568 | tf_op jit(solution)/shard_map/ppermute | solution.py:128
  46.1 0.7 %fusion.6 = bf16[64,512]{1,0:T(8,128)(2,1)} fusion(f32[128,512]{1,0:T(8,128)S(1)} %convert_element_type.61, bf16[64,512]{1,0:T(8,128)(2,1)S(1)} %collective-permute-done.24, bf16[64,512]{1,0:T(8,128)(2,1)S(1)} %collective-permute-done.18, bf16[64,512]{1,0:T(8,128)(2,1)S(1)} %collective-permute-done.11, bf16[64,512]{1,0:T(8,128)(2,1)S(1)} %collective-permute-done.1, ...), kind=kLoop, calls=%fused_computation.15 | loop fusion | flops 360448 | bytes 524288 | tf_op jit(solution)/shard_map/convert_element_type | solution.py:171
  (49 shorter events, 3.3 us)
Async XLA Ops:
  1.2 7.2 %collective-permute-start.3 = (bf16[528,128]{1,0:T(8,128)(2,1)S(1)}, bf16[528,128]{1,0:T(8,128)(2,1)S(1)}, u32[]{:S(2)}, u32[]{:S(2)}) collective-permute-start(bf16[528,128]{1,0:T(8,128)(2,1)S(1)} %tag_tokens.1.refs_0_), channel_id=1, source_target_pairs={{0,4},{1,5},{2,6},{3,7},{4,0},{5,1},{6,2},{7,3},{8,12},{9,13},{10,... | collective-permute-start | bytes 405512 | tf_op jit(solution)/shard_map/ppermute | solution.py:128
  4.3 5.3 %collective-permute-start = (bf16[528,128]{1,0:T(8,128)(2,1)S(1)}, bf16[528,128]{1,0:T(8,128)(2,1)S(1)}, u32[]{:S(2)}, u32[]{:S(2)}) collective-permute-start(bf16[528,128]{1,0:T(8,128)(2,1)S(1)} %tag_tokens.1.refs_0_), channel_id=1, source_target_pairs={{0,1},{1,0},{2,3},{3,2},{4,5},{5,4},{6,7},{7,6},{8,9},{9,8},{10,11... | collective-permute-start | bytes 405512 | tf_op jit(solution)/shard_map/ppermute | solution.py:128
  4.3 7.0 %collective-permute-start.2 = (bf16[528,128]{1,0:T(8,128)(2,1)S(1)}, bf16[528,128]{1,0:T(8,128)(2,1)S(1)}, u32[]{:S(2)}, u32[]{:S(2)}) collective-permute-start(bf16[528,128]{1,0:T(8,128)(2,1)S(1)} %tag_tokens.1.refs_0_), channel_id=1, source_target_pairs={{0,2},{1,3},{2,0},{3,1},{4,6},{5,7},{6,4},{7,5},{8,10},{9,11},{10,... | collective-permute-start | bytes 405512 | tf_op jit(solution)/shard_map/ppermute | solution.py:128
  5.8 9.5 %collective-permute-start.5 = (bf16[528,128]{1,0:T(8,128)(2,1)S(1)}, bf16[528,128]{1,0:T(8,128)(2,1)S(1)}, u32[]{:S(2)}, u32[]{:S(2)}) collective-permute-start(bf16[528,128]{1,0:T(8,128)(2,1)S(1)} %tag_tokens.1.refs_0_), channel_id=1, source_target_pairs={{0,8},{1,9},{2,10},{3,11},{4,12},{5,13},{6,14},{7,15},{8,0},{9,1},... | collective-permute-start | bytes 405512 | tf_op jit(solution)/shard_map/ppermute | solution.py:128
  8.4 6.9 %collective-permute-start.4 = (bf16[528,128]{1,0:T(8,128)(2,1)S(1)}, bf16[528,128]{1,0:T(8,128)(2,1)S(1)}, u32[]{:S(2)}, u32[]{:S(2)}) collective-permute-start(bf16[528,128]{1,0:T(8,128)(2,1)S(1)} %collective-permute-done.3.refs_1_), channel_id=1, source_target_pairs={{0,2},{1,3},{2,0},{3,1},{4,6},{5,7},{6,4},{7,5},{8,10},{9,11},{10,... | collective-permute-start | bytes 405512 | tf_op jit(solution)/shard_map/ppermute | solution.py:128
  11.3 4.9 %collective-permute-start.6 = (bf16[528,128]{1,0:T(8,128)(2,1)S(1)}, bf16[528,128]{1,0:T(8,128)(2,1)S(1)}, u32[]{:S(2)}, u32[]{:S(2)}) collective-permute-start(bf16[528,128]{1,0:T(8,128)(2,1)S(1)} %collective-permute-done.2.refs_0_), channel_id=1, source_target_pairs={{0,1},{1,0},{2,3},{3,2},{4,5},{5,4},{6,7},{7,6},{8,9},{9,8},{10,11... | collective-permute-start | bytes 405512 | tf_op jit(solution)/shard_map/ppermute | solution.py:128
  11.4 4.8 %collective-permute-start.7 = (bf16[528,128]{1,0:T(8,128)(2,1)S(1)}, bf16[528,128]{1,0:T(8,128)(2,1)S(1)}, u32[]{:S(2)}, u32[]{:S(2)}) collective-permute-start(bf16[528,128]{1,0:T(8,128)(2,1)S(1)} %collective-permute-done.3.refs_1_), channel_id=1, source_target_pairs={{0,1},{1,0},{2,3},{3,2},{4,5},{5,4},{6,7},{7,6},{8,9},{9,8},{10,11... | collective-permute-start | bytes 405512 | tf_op jit(solution)/shard_map/ppermute | solution.py:128
  15.3 6.4 %collective-permute-start.12 = (bf16[528,128]{1,0:T(8,128)(2,1)S(1)}, bf16[528,128]{1,0:T(8,128)(2,1)S(1)}, u32[]{:S(2)}, u32[]{:S(2)}) collective-permute-start(bf16[528,128]{1,0:T(8,128)(2,1)S(1)} %collective-permute-done.5.refs_0_), channel_id=1, source_target_pairs={{0,2},{1,3},{2,0},{3,1},{4,6},{5,7},{6,4},{7,5},{8,10},{9,11},{10,... | collective-permute-start | bytes 405512 | tf_op jit(solution)/shard_map/ppermute | solution.py:128
  15.8 5.9 %collective-permute-start.13 = (bf16[528,128]{1,0:T(8,128)(2,1)S(1)}, bf16[528,128]{1,0:T(8,128)(2,1)S(1)}, u32[]{:S(2)}, u32[]{:S(2)}) collective-permute-start(bf16[528,128]{1,0:T(8,128)(2,1)S(1)} %collective-permute-done.5.refs_0_), channel_id=1, source_target_pairs={{0,4},{1,5},{2,6},{3,7},{4,0},{5,1},{6,2},{7,3},{8,12},{9,13},{10,... | collective-permute-start | bytes 405512 | tf_op jit(solution)/shard_map/ppermute | solution.py:128
  21.2 6.6 %collective-permute-start.9 = (bf16[192,512]{1,0:T(8,128)(2,1)S(1)}, bf16[192,512]{1,0:T(8,128)(2,1)S(1)}, u32[]{:S(2)}, u32[]{:S(2)}) collective-permute-start(bf16[192,512]{1,0:T(8,128)(2,1)S(1)} %get-tuple-element.22), channel_id=1, source_target_pairs={{0,1},{1,0},{2,3},{3,2},{4,5},{5,4},{6,7},{7,6},{8,9},{9,8},{10,11... | collective-permute-start | bytes 589832 | tf_op jit(solution)/shard_map/ppermute | solution.py:128
  21.4 1.9 %collective-permute-start.14 = (bf16[528,128]{1,0:T(8,128)(2,1)S(1)}, bf16[528,128]{1,0:T(8,128)(2,1)S(1)}, u32[]{:S(2)}, u32[]{:S(2)}) collective-permute-start(bf16[528,128]{1,0:T(8,128)(2,1)S(1)} %collective-permute-done.5.refs_0_), channel_id=1, source_target_pairs={{0,1},{1,0},{2,3},{3,2},{4,5},{5,4},{6,7},{7,6},{8,9},{9,8},{10,11... | collective-permute-start | bytes 405512 | tf_op jit(solution)/shard_map/ppermute | solution.py:128
  21.7 1.8 %collective-permute-start.15 = (bf16[528,128]{1,0:T(8,128)(2,1)S(1)}, bf16[528,128]{1,0:T(8,128)(2,1)S(1)}, u32[]{:S(2)}, u32[]{:S(2)}) collective-permute-start(bf16[528,128]{1,0:T(8,128)(2,1)S(1)} %collective-permute-done.12.refs_1_), channel_id=1, source_target_pairs={{0,1},{1,0},{2,3},{3,2},{4,5},{5,4},{6,7},{7,6},{8,9},{9,8},{10,11... | collective-permute-start | bytes 405512 | tf_op jit(solution)/shard_map/ppermute | solution.py:128
  21.9 5.9 %collective-permute-start.19 = (bf16[528,128]{1,0:T(8,128)(2,1)S(1)}, bf16[528,128]{1,0:T(8,128)(2,1)S(1)}, u32[]{:S(2)}, u32[]{:S(2)}) collective-permute-start(bf16[528,128]{1,0:T(8,128)(2,1)S(1)} %collective-permute-done.13.refs_0_), channel_id=1, source_target_pairs={{0,2},{1,3},{2,0},{3,1},{4,6},{5,7},{6,4},{7,5},{8,10},{9,11},{10,... | collective-permute-start | bytes 405512 | tf_op jit(solution)/shard_map/ppermute | solution.py:128
  23.0 20.4 %collective-permute-start.1 = (bf16[64,512]{1,0:T(8,128)(2,1)S(1)}, bf16[64,512]{1,0:T(8,128)(2,1)S(1)}, u32[]{:S(2)}, u32[]{:S(2)}) collective-permute-start(bf16[64,512]{1,0:T(8,128)(2,1)S(1)} %get-tuple-element.18), channel_id=1, source_target_pairs={{0,1},{1,0},{2,3},{3,2},{4,5},{5,4},{6,7},{7,6},{8,9},{9,8},{10,11... | collective-permute-start | bytes 196616 | tf_op jit(solution)/shard_map/ppermute | solution.py:128
  23.3 6.8 %collective-permute-start.20 = (bf16[528,128]{1,0:T(8,128)(2,1)S(1)}, bf16[528,128]{1,0:T(8,128)(2,1)S(1)}, u32[]{:S(2)}, u32[]{:S(2)}) collective-permute-start(bf16[528,128]{1,0:T(8,128)(2,1)S(1)} %collective-permute-done.13.refs_0_), channel_id=1, source_target_pairs={{0,1},{1,0},{2,3},{3,2},{4,5},{5,4},{6,7},{7,6},{8,9},{9,8},{10,11... | collective-permute-start | bytes 405512 | tf_op jit(solution)/shard_map/ppermute | solution.py:128
  26.7 2.5 %collective-permute-start.16 = (bf16[128,512]{1,0:T(8,128)(2,1)S(1)}, bf16[128,512]{1,0:T(8,128)(2,1)S(1)}, u32[]{:S(2)}, u32[]{:S(2)}) collective-permute-start(bf16[128,512]{1,0:T(8,128)(2,1)S(1)} %get-tuple-element.25), channel_id=1, source_target_pairs={{0,1},{1,0},{2,3},{3,2},{4,5},{5,4},{6,7},{7,6},{8,9},{9,8},{10,11... | collective-permute-start | bytes 393224 | tf_op jit(solution)/shard_map/ppermute | solution.py:128
  27.7 2.3 %collective-permute-start.21 = (bf16[528,128]{1,0:T(8,128)(2,1)S(1)}, bf16[528,128]{1,0:T(8,128)(2,1)S(1)}, u32[]{:S(2)}, u32[]{:S(2)}) collective-permute-start(bf16[528,128]{1,0:T(8,128)(2,1)S(1)} %collective-permute-done.19.refs_1_), channel_id=1, source_target_pairs={{0,1},{1,0},{2,3},{3,2},{4,5},{5,4},{6,7},{7,6},{8,9},{9,8},{10,11... | collective-permute-start | bytes 405512 | tf_op jit(solution)/shard_map/ppermute | solution.py:128
  27.9 6.4 %collective-permute-start.10 = (bf16[128,512]{1,0:T(8,128)(2,1)S(1)}, bf16[128,512]{1,0:T(8,128)(2,1)S(1)}, u32[]{:S(2)}, u32[]{:S(2)}) collective-permute-start(bf16[128,512]{1,0:T(8,128)(2,1)S(1)} %pad_maximum_fusion), channel_id=1, source_target_pairs={{0,2},{1,3},{2,0},{3,1},{4,6},{5,7},{6,4},{7,5},{8,10},{9,11},{10,... | collective-permute-start | bytes 393224 | tf_op jit(solution)/shard_map/ppermute | solution.py:128
  29.3 7.9 %collective-permute-start.17 = (bf16[64,512]{1,0:T(8,128)(2,1)S(1)}, bf16[64,512]{1,0:T(8,128)(2,1)S(1)}, u32[]{:S(2)}, u32[]{:S(2)}) collective-permute-start(bf16[64,512]{1,0:T(8,128)(2,1)S(1)} %slice.71), channel_id=1, source_target_pairs={{0,2},{1,3},{2,0},{3,1},{4,6},{5,7},{6,4},{7,5},{8,10},{9,11},{10,... | collective-permute-start | bytes 196616 | tf_op jit(solution)/shard_map/ppermute | solution.py:128
  33.2 2.4 %collective-permute-start.22 = (bf16[128,512]{1,0:T(8,128)(2,1)S(1)}, bf16[128,512]{1,0:T(8,128)(2,1)S(1)}, u32[]{:S(2)}, u32[]{:S(2)}) collective-permute-start(bf16[128,512]{1,0:T(8,128)(2,1)S(1)} %get-tuple-element.28), channel_id=1, source_target_pairs={{0,1},{1,0},{2,3},{3,2},{4,5},{5,4},{6,7},{7,6},{8,9},{9,8},{10,11... | collective-permute-start | bytes 393224 | tf_op jit(solution)/shard_map/ppermute | solution.py:128
  34.3 9.2 %collective-permute-start.11 = (bf16[64,512]{1,0:T(8,128)(2,1)S(1)}, bf16[64,512]{1,0:T(8,128)(2,1)S(1)}, u32[]{:S(2)}, u32[]{:S(2)}) collective-permute-start(bf16[64,512]{1,0:T(8,128)(2,1)S(1)} %fusion.2), channel_id=1, source_target_pairs={{0,4},{1,5},{2,6},{3,7},{4,0},{5,1},{6,2},{7,3},{8,12},{9,13},{10,... | collective-permute-start | bytes 196616 | tf_op jit(solution)/shard_map/ppermute | solution.py:128
  35.6 4.3 %collective-permute-start.23 = (bf16[64,512]{1,0:T(8,128)(2,1)S(1)}, bf16[64,512]{1,0:T(8,128)(2,1)S(1)}, u32[]{:S(2)}, u32[]{:S(2)}) collective-permute-start(bf16[64,512]{1,0:T(8,128)(2,1)S(1)} %slice.70), channel_id=1, source_target_pairs={{0,2},{1,3},{2,0},{3,1},{4,6},{5,7},{6,4},{7,5},{8,10},{9,11},{10,... | collective-permute-start | bytes 196616 | tf_op jit(solution)/shard_map/ppermute | solution.py:128
  37.2 7.3 %collective-permute-start.18 = (bf16[64,512]{1,0:T(8,128)(2,1)S(1)}, bf16[64,512]{1,0:T(8,128)(2,1)S(1)}, u32[]{:S(2)}, u32[]{:S(2)}) collective-permute-start(bf16[64,512]{1,0:T(8,128)(2,1)S(1)} %fusion.1), channel_id=1, source_target_pairs={{0,8},{1,9},{2,10},{3,11},{4,12},{5,13},{6,14},{7,15},{8,0},{9,1},... | collective-permute-start | bytes 196616 | tf_op jit(solution)/shard_map/ppermute | solution.py:128
  40.0 6.1 %collective-permute-start.24 = (bf16[64,512]{1,0:T(8,128)(2,1)S(1)}, bf16[64,512]{1,0:T(8,128)(2,1)S(1)}, u32[]{:S(2)}, u32[]{:S(2)}) collective-permute-start(bf16[64,512]{1,0:T(8,128)(2,1)S(1)} %fusion), channel_id=1, source_target_pairs={{0,12},{1,13},{2,14},{3,15},{4,8},{5,9},{6,10},{7,11},{8,4},{9,5},... | collective-permute-start | bytes 196616 | tf_op jit(solution)/shard_map/ppermute | solution.py:128
  (4 other events, 30.1 us)

commit v8 on v7

--- a/solution.py
+++ b/solution.py
@@ -62,25 +62,34 @@
             rows_ref[i * size : (i + 1) * size, c * LANES : (c + 1) * LANES] = block[
                 c * size : (c + 1) * size, :
             ]
-    packed = [block[rank_in // LANES * size :, :].astype(jnp.float32) for block in blocks]
-    packed = jnp.concatenate(packed, axis=0)
-    lane = lax.broadcasted_iota(jnp.int32, packed.shape, 1)
+    packed = jnp.concatenate([block[rank_in // LANES * size :, :] for block in blocks], axis=0)
     first = lax.axis_index("expert") * local_experts
+    lane = lax.broadcasted_iota(jnp.int32, (LANES, LANES), 0)
+    column = lax.broadcasted_iota(jnp.int32, (LANES, LANES), 1)
+    shift = fold.bit_length() - 1
+    inside, kind = lane - (column & (fold - 1)) * experts, column >> shift
+    whole = (kind == 0) & (inside >= 0) & (inside < experts)
+    taken = whole | ((kind > 0) & (inside == first + kind - 1))
+    picked = jnp.dot(
+        packed, jnp.where(taken, 1.0, 0.0).astype(jnp.bfloat16), preferred_element_type=jnp.float32
+    )
 
-    def per_row(select):
-        sums = [
-            jnp.sum(jnp.where(select(q), packed, 0.0), axis=1, keepdims=True) for q in range(fold)
-        ]
+    def per_row(kind):
         return jnp.concatenate(
-            [sums[q][i * part : (i + 1) * part] for i in range(count) for q in range(fold)], axis=0
+            [
+                picked[i * part : (i + 1) * part, kind * fold + q : kind * fold + q + 1]
+                for i in range(count)
+                for q in range(fold)
+            ],
+            axis=0,
         )
 
-    total = per_row(lambda q: (lane >= q * experts) & (lane < (q + 1) * experts))
+    total = per_row(0)
     codes = rows_ref[...]
     out = jnp.zeros((codes.shape[0], down_ref.shape[2]), jnp.float32)
     own = jnp.zeros_like(total)
     for e in range(local_experts):
-        score = per_row(lambda q: lane == q * experts + first + e)
+        score = per_row(1 + e)
         own = own + score
         gate = jnp.dot(codes, gate_ref[e], preferred_element_type=jnp.float32)
         up = jnp.dot(codes, up_ref[e], preferred_element_type=jnp.float32)

time: 47 us -> 46.9 us (level)
  transfers between devices with their start and end apart: 25 -> 25, of which waited for: 7 -> 7; matrix products, arithmetic and copies ran while one was open for 1% -> 1% of each run, Pallas kernels for 27% -> 26%
where the time goes in v8:
time: 46.9 us; the launch traced here: 46.8 us
  starting transfers between devices  22.9 us (49%)
  Pallas kernels  13.5 us (29%)
  waiting for transfers between devices  9.38 us (20%)
  other arithmetic  0.89 us (2%)
    ppermute x25, starting transfers between devices, exchange(): return lax.ppermute(array, 'expert', [(i, i ^ mask) for i in range(size)])  22.9 us
    pallas_call x4, Pallas kernels, apply_experts(): pl.pallas_call(functools.partial(expert_kernel, len(blocks), experts), ou...  12.2 us
    ppermute x25, waiting for transfers between devices, exchange(): return lax.ppermute(array, 'expert', [(i, i ^ mask) for i in range(size)])  9.38 us
    pallas_call x1, Pallas kernels, tag_tokens(): pl.pallas_call(functools.partial(tag_kernel, local_experts, experts), out...  1.21 us
  transfers between devices with their start and end apart: 25, of which 7 were waited for; matrix products, arithmetic and copies ran while one was open for 1% of the time, Pallas kernels for 26%

profile of v8, /device:TPU:0, one launch (start us, length us, event | category | flops | bytes accessed | tf_op | source)
XLA Modules:
  0.0 46.8 jit_solution(7909976324229083849)
XLA Ops:
  0.0 1.2 %tag_tokens.1.refs_0_ = bf16[528,128]{1,0:T(8,128)(2,1)S(1)} custom-call(bf16[64,1024]{1,0:T(8,128)(2,1)} %codes_ref.1, s32[8,64]{1,0:T(8,128)} %bitcast.3, s32[8,64]{1,0:T(8,128)} %bitcast.4, bf16[8,64]{1,0:T(8,128)(2,1)} %bitcast.5), custom_call_target="tpu_custom_call" | custom-call | flops 8000000000 | bytes 16000000 | tf_op jit(solution)/shard_map/tag_tokens/pallas_call | solution.py:42
  1.2 3.1 %collective-permute-start.3 = (bf16[528,128]{1,0:T(8,128)(2,1)S(1)}, bf16[528,128]{1,0:T(8,128)(2,1)S(1)}, u32[]{:S(2)}, u32[]{:S(2)}) collective-permute-start(bf16[528,128]{1,0:T(8,128)(2,1)S(1)} %tag_tokens.1.refs_0_), channel_id=1, source_target_pairs={{0,4},{1,5},{2,6},{3,7},{4,0},{5,1},{6,2},{7,3},{8,12},{9,13},{10,... | collective-permute-start | bytes 405512 | tf_op jit(solution)/shard_map/ppermute | solution.py:137
  4.3 1.5 %collective-permute-start.2 = (bf16[528,128]{1,0:T(8,128)(2,1)S(1)}, bf16[528,128]{1,0:T(8,128)(2,1)S(1)}, u32[]{:S(2)}, u32[]{:S(2)}) collective-permute-start(bf16[528,128]{1,0:T(8,128)(2,1)S(1)} %tag_tokens.1.refs_0_), channel_id=1, source_target_pairs={{0,2},{1,3},{2,0},{3,1},{4,6},{5,7},{6,4},{7,5},{8,10},{9,11},{10,... | collective-permute-start | bytes 405512 | tf_op jit(solution)/shard_map/ppermute | solution.py:137
  5.8 2.6 %collective-permute-start.5 = (bf16[528,128]{1,0:T(8,128)(2,1)S(1)}, bf16[528,128]{1,0:T(8,128)(2,1)S(1)}, u32[]{:S(2)}, u32[]{:S(2)}) collective-permute-start(bf16[528,128]{1,0:T(8,128)(2,1)S(1)} %tag_tokens.1.refs_0_), channel_id=1, source_target_pairs={{0,8},{1,9},{2,10},{3,11},{4,12},{5,13},{6,14},{7,15},{8,0},{9,1},... | collective-permute-start | bytes 405512 | tf_op jit(solution)/shard_map/ppermute | solution.py:137
  8.4 1.2 %collective-permute-start.4 = (bf16[528,128]{1,0:T(8,128)(2,1)S(1)}, bf16[528,128]{1,0:T(8,128)(2,1)S(1)}, u32[]{:S(2)}, u32[]{:S(2)}) collective-permute-start(bf16[528,128]{1,0:T(8,128)(2,1)S(1)} %collective-permute-done.3.refs_1_), channel_id=1, source_target_pairs={{0,2},{1,3},{2,0},{3,1},{4,6},{5,7},{6,4},{7,5},{8,10},{9,11},{10,... | collective-permute-start | bytes 405512 | tf_op jit(solution)/shard_map/ppermute | solution.py:137
  9.6 1.6 %apply_experts.4 = (bf16[64,512]{1,0:T(8,128)(2,1)S(1)}, bf16[64,512]{1,0:T(8,128)(2,1)S(1)}) custom-call(bf16[528,128]{1,0:T(8,128)(2,1)S(1)} %tag_tokens.1.refs_0_, bf16[528,128]{1,0:T(8,128)(2,1)S(1)} %collective-permute-done.refs_1_, bf16[2,1024,1024]{2,1,0:T(8,128)(2,1)S(1)} %copy-done, bf16[2,1024,1024]{2,1,0:T(8,128)(2,1)S(1)} %copy-done.1, ...), custom_call_target="tpu_custom_call" | custom-call | flops 67108864 | bytes 1024 | tf_op jit(solution)/shard_map/apply_experts/pallas_call | solution.py:112
  11.8 3.5 %collective-permute-done.5.refs_0_ = bf16[528,128]{1,0:T(8,128)(2,1)S(1)} collective-permute-done((bf16[528,128]{1,0:T(8,128)(2,1)S(1)}, bf16[528,128]{1,0:T(8,128)(2,1)S(1)}, u32[]{:S(2)}, u32[]{:S(2)}) %collective-permute-start.5) | collective-permute-done | bytes 135200 | tf_op jit(solution)/shard_map/ppermute | solution.py:137
  15.3 0.6 %collective-permute-start.12 = (bf16[528,128]{1,0:T(8,128)(2,1)S(1)}, bf16[528,128]{1,0:T(8,128)(2,1)S(1)}, u32[]{:S(2)}, u32[]{:S(2)}) collective-permute-start(bf16[528,128]{1,0:T(8,128)(2,1)S(1)} %collective-permute-done.5.refs_0_), channel_id=1, source_target_pairs={{0,2},{1,3},{2,0},{3,1},{4,6},{5,7},{6,4},{7,5},{8,10},{9,11},{10,... | collective-permute-start | bytes 405512 | tf_op jit(solution)/shard_map/ppermute | solution.py:137
  16.6 4.5 %apply_experts.5 = (bf16[192,512]{1,0:T(8,128)(2,1)S(1)}, bf16[192,512]{1,0:T(8,128)(2,1)S(1)}) custom-call(bf16[528,128]{1,0:T(8,128)(2,1)S(1)} %collective-permute-done.2.refs_0_, bf16[528,128]{1,0:T(8,128)(2,1)S(1)} %collective-permute-done.3.refs_1_, bf16[528,128]{1,0:T(8,128)(2,1)S(1)} %collective-permute-done.4.refs_2_, ...), custom_call_target="tpu_custom_call" | custom-call | flops 201326592 | bytes 1024 | tf_op jit(solution)/shard_map/apply_experts/pallas_call | solution.py:112
  21.9 1.2 %collective-permute-start.19 = (bf16[528,128]{1,0:T(8,128)(2,1)S(1)}, bf16[528,128]{1,0:T(8,128)(2,1)S(1)}, u32[]{:S(2)}, u32[]{:S(2)}) collective-permute-start(bf16[528,128]{1,0:T(8,128)(2,1)S(1)} %collective-permute-done.13.refs_0_), channel_id=1, source_target_pairs={{0,2},{1,3},{2,0},{3,1},{4,6},{5,7},{6,4},{7,5},{8,10},{9,11},{10,... | collective-permute-start | bytes 405512 | tf_op jit(solution)/shard_map/ppermute | solution.py:137
  23.6 3.0 %apply_experts.6 = (bf16[128,512]{1,0:T(8,128)(2,1)S(1)}, bf16[128,512]{1,0:T(8,128)(2,1)S(1)}) custom-call(bf16[528,128]{1,0:T(8,128)(2,1)S(1)} %collective-permute-done.5.refs_0_, bf16[528,128]{1,0:T(8,128)(2,1)S(1)} %collective-permute-done.12.refs_1_, bf16[528,128]{1,0:T(8,128)(2,1)S(1)} %collective-permute-done.14.refs_2_, ...), custom_call_target="tpu_custom_call" | custom-call | flops 134217728 | bytes 1024 | tf_op jit(solution)/shard_map/apply_experts/pallas_call | solution.py:112
  26.9 0.8 %collective-permute-done.19.refs_1_ = bf16[528,128]{1,0:T(8,128)(2,1)S(1)} collective-permute-done((bf16[528,128]{1,0:T(8,128)(2,1)S(1)}, bf16[528,128]{1,0:T(8,128)(2,1)S(1)}, u32[]{:S(2)}, u32[]{:S(2)}) %collective-permute-start.19) | collective-permute-done | bytes 135200 | tf_op jit(solution)/shard_map/ppermute | solution.py:137
  27.8 1.4 %collective-permute-start.10 = (bf16[128,512]{1,0:T(8,128)(2,1)S(1)}, bf16[128,512]{1,0:T(8,128)(2,1)S(1)}, u32[]{:S(2)}, u32[]{:S(2)}) collective-permute-start(bf16[128,512]{1,0:T(8,128)(2,1)S(1)} %pad_maximum_fusion), channel_id=1, source_target_pairs={{0,2},{1,3},{2,0},{3,1},{4,6},{5,7},{6,4},{7,5},{8,10},{9,11},{10,... | collective-permute-start | bytes 393224 | tf_op jit(solution)/shard_map/ppermute | solution.py:137
  29.3 0.8 %collective-permute-start.17 = (bf16[64,512]{1,0:T(8,128)(2,1)S(1)}, bf16[64,512]{1,0:T(8,128)(2,1)S(1)}, u32[]{:S(2)}, u32[]{:S(2)}) collective-permute-start(bf16[64,512]{1,0:T(8,128)(2,1)S(1)} %slice.71), channel_id=1, source_target_pairs={{0,2},{1,3},{2,0},{3,1},{4,6},{5,7},{6,4},{7,5},{8,10},{9,11},{10,... | collective-permute-start | bytes 196616 | tf_op jit(solution)/shard_map/ppermute | solution.py:137
  30.1 3.1 %apply_experts.7 = (bf16[128,512]{1,0:T(8,128)(2,1)S(1)}, bf16[128,512]{1,0:T(8,128)(2,1)S(1)}) custom-call(bf16[528,128]{1,0:T(8,128)(2,1)S(1)} %collective-permute-done.13.refs_0_, bf16[528,128]{1,0:T(8,128)(2,1)S(1)} %collective-permute-done.19.refs_1_, bf16[528,128]{1,0:T(8,128)(2,1)S(1)} %collective-permute-done.20.refs_2_, ...), custom_call_target="tpu_custom_call" | custom-call | flops 134217728 | bytes 1024 | tf_op jit(solution)/shard_map/apply_experts/pallas_call | solution.py:112
  33.2 1.0 %collective-permute-done.10 = bf16[128,512]{1,0:T(8,128)(2,1)S(1)} collective-permute-done((bf16[128,512]{1,0:T(8,128)(2,1)S(1)}, bf16[128,512]{1,0:T(8,128)(2,1)S(1)}, u32[]{:S(2)}, u32[]{:S(2)}) %collective-permute-start.10) | collective-permute-done | bytes 131104 | tf_op jit(solution)/shard_map/ppermute | solution.py:137
  34.3 1.3 %collective-permute-start.11 = (bf16[64,512]{1,0:T(8,128)(2,1)S(1)}, bf16[64,512]{1,0:T(8,128)(2,1)S(1)}, u32[]{:S(2)}, u32[]{:S(2)}) collective-permute-start(bf16[64,512]{1,0:T(8,128)(2,1)S(1)} %fusion.2), channel_id=1, source_target_pairs={{0,4},{1,5},{2,6},{3,7},{4,0},{5,1},{6,2},{7,3},{8,12},{9,13},{10,... | collective-permute-start | bytes 196616 | tf_op jit(solution)/shard_map/ppermute | solution.py:137
  35.6 1.5 %collective-permute-start.23 = (bf16[64,512]{1,0:T(8,128)(2,1)S(1)}, bf16[64,512]{1,0:T(8,128)(2,1)S(1)}, u32[]{:S(2)}, u32[]{:S(2)}) collective-permute-start(bf16[64,512]{1,0:T(8,128)(2,1)S(1)} %slice.70), channel_id=1, source_target_pairs={{0,2},{1,3},{2,0},{3,1},{4,6},{5,7},{6,4},{7,5},{8,10},{9,11},{10,... | collective-permute-start | bytes 196616 | tf_op jit(solution)/shard_map/ppermute | solution.py:137
  37.2 1.9 %collective-permute-start.18 = (bf16[64,512]{1,0:T(8,128)(2,1)S(1)}, bf16[64,512]{1,0:T(8,128)(2,1)S(1)}, u32[]{:S(2)}, u32[]{:S(2)}) collective-permute-start(bf16[64,512]{1,0:T(8,128)(2,1)S(1)} %fusion.1), channel_id=1, source_target_pairs={{0,8},{1,9},{2,10},{3,11},{4,12},{5,13},{6,14},{7,15},{8,0},{9,1},... | collective-permute-start | bytes 196616 | tf_op jit(solution)/shard_map/ppermute | solution.py:137
  39.1 0.9 %collective-permute-done.23 = bf16[64,512]{1,0:T(8,128)(2,1)S(1)} collective-permute-done((bf16[64,512]{1,0:T(8,128)(2,1)S(1)}, bf16[64,512]{1,0:T(8,128)(2,1)S(1)}, u32[]{:S(2)}, u32[]{:S(2)}) %collective-permute-start.23) | collective-permute-done | bytes 65568 | tf_op jit(solution)/shard_map/ppermute | solution.py:137
  40.0 3.5 %collective-permute-start.24 = (bf16[64,512]{1,0:T(8,128)(2,1)S(1)}, bf16[64,512]{1,0:T(8,128)(2,1)S(1)}, u32[]{:S(2)}, u32[]{:S(2)}) collective-permute-start(bf16[64,512]{1,0:T(8,128)(2,1)S(1)} %fusion), channel_id=1, source_target_pairs={{0,12},{1,13},{2,14},{3,15},{4,8},{5,9},{6,10},{7,11},{8,4},{9,5},... | collective-permute-start | bytes 196616 | tf_op jit(solution)/shard_map/ppermute | solution.py:137
  43.5 1.0 %collective-permute-done.18 = bf16[64,512]{1,0:T(8,128)(2,1)S(1)} collective-permute-done((bf16[64,512]{1,0:T(8,128)(2,1)S(1)}, bf16[64,512]{1,0:T(8,128)(2,1)S(1)}, u32[]{:S(2)}, u32[]{:S(2)}) %collective-permute-start.18) | collective-permute-done | bytes 65568 | tf_op jit(solution)/shard_map/ppermute | solution.py:137
  44.5 1.6 %collective-permute-done.24 = bf16[64,512]{1,0:T(8,128)(2,1)S(1)} collective-permute-done((bf16[64,512]{1,0:T(8,128)(2,1)S(1)}, bf16[64,512]{1,0:T(8,128)(2,1)S(1)}, u32[]{:S(2)}, u32[]{:S(2)}) %collective-permute-start.24) | collective-permute-done | bytes 65568 | tf_op jit(solution)/shard_map/ppermute | solution.py:137
  46.1 0.7 %fusion.6 = bf16[64,512]{1,0:T(8,128)(2,1)} fusion(f32[128,512]{1,0:T(8,128)S(1)} %convert_element_type.61, bf16[64,512]{1,0:T(8,128)(2,1)S(1)} %collective-permute-done.24, bf16[64,512]{1,0:T(8,128)(2,1)S(1)} %collective-permute-done.18, bf16[64,512]{1,0:T(8,128)(2,1)S(1)} %collective-permute-done.11, bf16[64,512]{1,0:T(8,128)(2,1)S(1)} %collective-permute-done.1, ...), kind=kLoop, calls=%fused_computation.15 | loop fusion | flops 360448 | bytes 524288 | tf_op jit(solution)/shard_map/convert_element_type | solution.py:180
  (49 shorter events, 3.3 us)
Async XLA Ops:
  1.2 7.2 %collective-permute-start.3 = (bf16[528,128]{1,0:T(8,128)(2,1)S(1)}, bf16[528,128]{1,0:T(8,128)(2,1)S(1)}, u32[]{:S(2)}, u32[]{:S(2)}) collective-permute-start(bf16[528,128]{1,0:T(8,128)(2,1)S(1)} %tag_tokens.1.refs_0_), channel_id=1, source_target_pairs={{0,4},{1,5},{2,6},{3,7},{4,0},{5,1},{6,2},{7,3},{8,12},{9,13},{10,... | collective-permute-start | bytes 405512 | tf_op jit(solution)/shard_map/ppermute | solution.py:137
  4.3 5.3 %collective-permute-start = (bf16[528,128]{1,0:T(8,128)(2,1)S(1)}, bf16[528,128]{1,0:T(8,128)(2,1)S(1)}, u32[]{:S(2)}, u32[]{:S(2)}) collective-permute-start(bf16[528,128]{1,0:T(8,128)(2,1)S(1)} %tag_tokens.1.refs_0_), channel_id=1, source_target_pairs={{0,1},{1,0},{2,3},{3,2},{4,5},{5,4},{6,7},{7,6},{8,9},{9,8},{10,11... | collective-permute-start | bytes 405512 | tf_op jit(solution)/shard_map/ppermute | solution.py:137
  4.3 6.9 %collective-permute-start.2 = (bf16[528,128]{1,0:T(8,128)(2,1)S(1)}, bf16[528,128]{1,0:T(8,128)(2,1)S(1)}, u32[]{:S(2)}, u32[]{:S(2)}) collective-permute-start(bf16[528,128]{1,0:T(8,128)(2,1)S(1)} %tag_tokens.1.refs_0_), channel_id=1, source_target_pairs={{0,2},{1,3},{2,0},{3,1},{4,6},{5,7},{6,4},{7,5},{8,10},{9,11},{10,... | collective-permute-start | bytes 405512 | tf_op jit(solution)/shard_map/ppermute | solution.py:137
  5.8 9.5 %collective-permute-start.5 = (bf16[528,128]{1,0:T(8,128)(2,1)S(1)}, bf16[528,128]{1,0:T(8,128)(2,1)S(1)}, u32[]{:S(2)}, u32[]{:S(2)}) collective-permute-start(bf16[528,128]{1,0:T(8,128)(2,1)S(1)} %tag_tokens.1.refs_0_), channel_id=1, source_target_pairs={{0,8},{1,9},{2,10},{3,11},{4,12},{5,13},{6,14},{7,15},{8,0},{9,1},... | collective-permute-start | bytes 405512 | tf_op jit(solution)/shard_map/ppermute | solution.py:137
  8.4 6.9 %collective-permute-start.4 = (bf16[528,128]{1,0:T(8,128)(2,1)S(1)}, bf16[528,128]{1,0:T(8,128)(2,1)S(1)}, u32[]{:S(2)}, u32[]{:S(2)}) collective-permute-start(bf16[528,128]{1,0:T(8,128)(2,1)S(1)} %collective-permute-done.3.refs_1_), channel_id=1, source_target_pairs={{0,2},{1,3},{2,0},{3,1},{4,6},{5,7},{6,4},{7,5},{8,10},{9,11},{10,... | collective-permute-start | bytes 405512 | tf_op jit(solution)/shard_map/ppermute | solution.py:137
  11.2 4.9 %collective-permute-start.6 = (bf16[528,128]{1,0:T(8,128)(2,1)S(1)}, bf16[528,128]{1,0:T(8,128)(2,1)S(1)}, u32[]{:S(2)}, u32[]{:S(2)}) collective-permute-start(bf16[528,128]{1,0:T(8,128)(2,1)S(1)} %collective-permute-done.2.refs_0_), channel_id=1, source_target_pairs={{0,1},{1,0},{2,3},{3,2},{4,5},{5,4},{6,7},{7,6},{8,9},{9,8},{10,11... | collective-permute-start | bytes 405512 | tf_op jit(solution)/shard_map/ppermute | solution.py:137
  11.3 4.8 %collective-permute-start.7 = (bf16[528,128]{1,0:T(8,128)(2,1)S(1)}, bf16[528,128]{1,0:T(8,128)(2,1)S(1)}, u32[]{:S(2)}, u32[]{:S(2)}) collective-permute-start(bf16[528,128]{1,0:T(8,128)(2,1)S(1)} %collective-permute-done.3.refs_1_), channel_id=1, source_target_pairs={{0,1},{1,0},{2,3},{3,2},{4,5},{5,4},{6,7},{7,6},{8,9},{9,8},{10,11... | collective-permute-start | bytes 405512 | tf_op jit(solution)/shard_map/ppermute | solution.py:137
  15.3 6.4 %collective-permute-start.12 = (bf16[528,128]{1,0:T(8,128)(2,1)S(1)}, bf16[528,128]{1,0:T(8,128)(2,1)S(1)}, u32[]{:S(2)}, u32[]{:S(2)}) collective-permute-start(bf16[528,128]{1,0:T(8,128)(2,1)S(1)} %collective-permute-done.5.refs_0_), channel_id=1, source_target_pairs={{0,2},{1,3},{2,0},{3,1},{4,6},{5,7},{6,4},{7,5},{8,10},{9,11},{10,... | collective-permute-start | bytes 405512 | tf_op jit(solution)/shard_map/ppermute | solution.py:137
  15.8 5.9 %collective-permute-start.13 = (bf16[528,128]{1,0:T(8,128)(2,1)S(1)}, bf16[528,128]{1,0:T(8,128)(2,1)S(1)}, u32[]{:S(2)}, u32[]{:S(2)}) collective-permute-start(bf16[528,128]{1,0:T(8,128)(2,1)S(1)} %collective-permute-done.5.refs_0_), channel_id=1, source_target_pairs={{0,4},{1,5},{2,6},{3,7},{4,0},{5,1},{6,2},{7,3},{8,12},{9,13},{10,... | collective-permute-start | bytes 405512 | tf_op jit(solution)/shard_map/ppermute | solution.py:137
  21.1 6.6 %collective-permute-start.9 = (bf16[192,512]{1,0:T(8,128)(2,1)S(1)}, bf16[192,512]{1,0:T(8,128)(2,1)S(1)}, u32[]{:S(2)}, u32[]{:S(2)}) collective-permute-start(bf16[192,512]{1,0:T(8,128)(2,1)S(1)} %get-tuple-element.22), channel_id=1, source_target_pairs={{0,1},{1,0},{2,3},{3,2},{4,5},{5,4},{6,7},{7,6},{8,9},{9,8},{10,11... | collective-permute-start | bytes 589832 | tf_op jit(solution)/shard_map/ppermute | solution.py:137
  21.4 1.9 %collective-permute-start.14 = (bf16[528,128]{1,0:T(8,128)(2,1)S(1)}, bf16[528,128]{1,0:T(8,128)(2,1)S(1)}, u32[]{:S(2)}, u32[]{:S(2)}) collective-permute-start(bf16[528,128]{1,0:T(8,128)(2,1)S(1)} %collective-permute-done.5.refs_0_), channel_id=1, source_target_pairs={{0,1},{1,0},{2,3},{3,2},{4,5},{5,4},{6,7},{7,6},{8,9},{9,8},{10,11... | collective-permute-start | bytes 405512 | tf_op jit(solution)/shard_map/ppermute | solution.py:137
  21.7 1.8 %collective-permute-start.15 = (bf16[528,128]{1,0:T(8,128)(2,1)S(1)}, bf16[528,128]{1,0:T(8,128)(2,1)S(1)}, u32[]{:S(2)}, u32[]{:S(2)}) collective-permute-start(bf16[528,128]{1,0:T(8,128)(2,1)S(1)} %collective-permute-done.12.refs_1_), channel_id=1, source_target_pairs={{0,1},{1,0},{2,3},{3,2},{4,5},{5,4},{6,7},{7,6},{8,9},{9,8},{10,11... | collective-permute-start | bytes 405512 | tf_op jit(solution)/shard_map/ppermute | solution.py:137
  21.9 5.9 %collective-permute-start.19 = (bf16[528,128]{1,0:T(8,128)(2,1)S(1)}, bf16[528,128]{1,0:T(8,128)(2,1)S(1)}, u32[]{:S(2)}, u32[]{:S(2)}) collective-permute-start(bf16[528,128]{1,0:T(8,128)(2,1)S(1)} %collective-permute-done.13.refs_0_), channel_id=1, source_target_pairs={{0,2},{1,3},{2,0},{3,1},{4,6},{5,7},{6,4},{7,5},{8,10},{9,11},{10,... | collective-permute-start | bytes 405512 | tf_op jit(solution)/shard_map/ppermute | solution.py:137
  23.0 20.4 %collective-permute-start.1 = (bf16[64,512]{1,0:T(8,128)(2,1)S(1)}, bf16[64,512]{1,0:T(8,128)(2,1)S(1)}, u32[]{:S(2)}, u32[]{:S(2)}) collective-permute-start(bf16[64,512]{1,0:T(8,128)(2,1)S(1)} %get-tuple-element.18), channel_id=1, source_target_pairs={{0,1},{1,0},{2,3},{3,2},{4,5},{5,4},{6,7},{7,6},{8,9},{9,8},{10,11... | collective-permute-start | bytes 196616 | tf_op jit(solution)/shard_map/ppermute | solution.py:137
  23.3 6.8 %collective-permute-start.20 = (bf16[528,128]{1,0:T(8,128)(2,1)S(1)}, bf16[528,128]{1,0:T(8,128)(2,1)S(1)}, u32[]{:S(2)}, u32[]{:S(2)}) collective-permute-start(bf16[528,128]{1,0:T(8,128)(2,1)S(1)} %collective-permute-done.13.refs_0_), channel_id=1, source_target_pairs={{0,1},{1,0},{2,3},{3,2},{4,5},{5,4},{6,7},{7,6},{8,9},{9,8},{10,11... | collective-permute-start | bytes 405512 | tf_op jit(solution)/shard_map/ppermute | solution.py:137
  26.6 2.6 %collective-permute-start.16 = (bf16[128,512]{1,0:T(8,128)(2,1)S(1)}, bf16[128,512]{1,0:T(8,128)(2,1)S(1)}, u32[]{:S(2)}, u32[]{:S(2)}) collective-permute-start(bf16[128,512]{1,0:T(8,128)(2,1)S(1)} %get-tuple-element.25), channel_id=1, source_target_pairs={{0,1},{1,0},{2,3},{3,2},{4,5},{5,4},{6,7},{7,6},{8,9},{9,8},{10,11... | collective-permute-start | bytes 393224 | tf_op jit(solution)/shard_map/ppermute | solution.py:137
  27.7 2.3 %collective-permute-start.21 = (bf16[528,128]{1,0:T(8,128)(2,1)S(1)}, bf16[528,128]{1,0:T(8,128)(2,1)S(1)}, u32[]{:S(2)}, u32[]{:S(2)}) collective-permute-start(bf16[528,128]{1,0:T(8,128)(2,1)S(1)} %collective-permute-done.19.refs_1_), channel_id=1, source_target_pairs={{0,1},{1,0},{2,3},{3,2},{4,5},{5,4},{6,7},{7,6},{8,9},{9,8},{10,11... | collective-permute-start | bytes 405512 | tf_op jit(solution)/shard_map/ppermute | solution.py:137
  27.8 6.4 %collective-permute-start.10 = (bf16[128,512]{1,0:T(8,128)(2,1)S(1)}, bf16[128,512]{1,0:T(8,128)(2,1)S(1)}, u32[]{:S(2)}, u32[]{:S(2)}) collective-permute-start(bf16[128,512]{1,0:T(8,128)(2,1)S(1)} %pad_maximum_fusion), channel_id=1, source_target_pairs={{0,2},{1,3},{2,0},{3,1},{4,6},{5,7},{6,4},{7,5},{8,10},{9,11},{10,... | collective-permute-start | bytes 393224 | tf_op jit(solution)/shard_map/ppermute | solution.py:137
  29.3 7.9 %collective-permute-start.17 = (bf16[64,512]{1,0:T(8,128)(2,1)S(1)}, bf16[64,512]{1,0:T(8,128)(2,1)S(1)}, u32[]{:S(2)}, u32[]{:S(2)}) collective-permute-start(bf16[64,512]{1,0:T(8,128)(2,1)S(1)} %slice.71), channel_id=1, source_target_pairs={{0,2},{1,3},{2,0},{3,1},{4,6},{5,7},{6,4},{7,5},{8,10},{9,11},{10,... | collective-permute-start | bytes 196616 | tf_op jit(solution)/shard_map/ppermute | solution.py:137
  33.1 2.5 %collective-permute-start.22 = (bf16[128,512]{1,0:T(8,128)(2,1)S(1)}, bf16[128,512]{1,0:T(8,128)(2,1)S(1)}, u32[]{:S(2)}, u32[]{:S(2)}) collective-permute-start(bf16[128,512]{1,0:T(8,128)(2,1)S(1)} %get-tuple-element.28), channel_id=1, source_target_pairs={{0,1},{1,0},{2,3},{3,2},{4,5},{5,4},{6,7},{7,6},{8,9},{9,8},{10,11... | collective-permute-start | bytes 393224 | tf_op jit(solution)/shard_map/ppermute | solution.py:137
  34.3 9.2 %collective-permute-start.11 = (bf16[64,512]{1,0:T(8,128)(2,1)S(1)}, bf16[64,512]{1,0:T(8,128)(2,1)S(1)}, u32[]{:S(2)}, u32[]{:S(2)}) collective-permute-start(bf16[64,512]{1,0:T(8,128)(2,1)S(1)} %fusion.2), channel_id=1, source_target_pairs={{0,4},{1,5},{2,6},{3,7},{4,0},{5,1},{6,2},{7,3},{8,12},{9,13},{10,... | collective-permute-start | bytes 196616 | tf_op jit(solution)/shard_map/ppermute | solution.py:137
  35.6 4.3 %collective-permute-start.23 = (bf16[64,512]{1,0:T(8,128)(2,1)S(1)}, bf16[64,512]{1,0:T(8,128)(2,1)S(1)}, u32[]{:S(2)}, u32[]{:S(2)}) collective-permute-start(bf16[64,512]{1,0:T(8,128)(2,1)S(1)} %slice.70), channel_id=1, source_target_pairs={{0,2},{1,3},{2,0},{3,1},{4,6},{5,7},{6,4},{7,5},{8,10},{9,11},{10,... | collective-permute-start | bytes 196616 | tf_op jit(solution)/shard_map/ppermute | solution.py:137
  37.2 7.3 %collective-permute-start.18 = (bf16[64,512]{1,0:T(8,128)(2,1)S(1)}, bf16[64,512]{1,0:T(8,128)(2,1)S(1)}, u32[]{:S(2)}, u32[]{:S(2)}) collective-permute-start(bf16[64,512]{1,0:T(8,128)(2,1)S(1)} %fusion.1), channel_id=1, source_target_pairs={{0,8},{1,9},{2,10},{3,11},{4,12},{5,13},{6,14},{7,15},{8,0},{9,1},... | collective-permute-start | bytes 196616 | tf_op jit(solution)/shard_map/ppermute | solution.py:137
  40.0 6.1 %collective-permute-start.24 = (bf16[64,512]{1,0:T(8,128)(2,1)S(1)}, bf16[64,512]{1,0:T(8,128)(2,1)S(1)}, u32[]{:S(2)}, u32[]{:S(2)}) collective-permute-start(bf16[64,512]{1,0:T(8,128)(2,1)S(1)} %fusion), channel_id=1, source_target_pairs={{0,12},{1,13},{2,14},{3,15},{4,8},{5,9},{6,10},{7,11},{8,4},{9,5},... | collective-permute-start | bytes 196616 | tf_op jit(solution)/shard_map/ppermute | solution.py:137
  (4 other events, 30.1 us)
